TPU v7x, 512 devices: a whole 4x8x8 slice. The times are simulated.
512 devices in a mesh: gx: 64 (over z, y), gy: 8 (over x, core).
Axes of the slice: x: 4, y: 8, z: 8, core: 2. Of those that a mesh axis runs over, the one named last changes fastest.
Arguments:
- forward_coeff: float32 [192, 65536], P(None, ('gx', 'gy')), may hold values from -6 to 6
- incident: float32 [192, 65536], P(None, ('gx', 'gy')), may hold values from -6 to 6
- cost_grad: float32 [192, 65536], P(None, ('gx', 'gy')), may hold values from -6 to 6
- tmat_real: float32 [4, 96, 96], replicated, may hold values from -0.21875 to 0.21875
- tmat_imag: float32 [4, 96, 96], replicated, may hold values from -0.21875 to 0.21875
- translation_real: float32 [10, 96, 96], replicated, may hold values from -0.125 to 0.125
- translation_imaginary: float32 [10, 96, 96], replicated, may hold values from -0.125 to 0.125
- neighbours: int32 [10, 65536], P(None, ('gx', 'gy')), may hold values from -1 to 65535, as said below
- particle_type: int32 [65536], P(('gx', 'gy')), may hold values from 0 to 3
Outputs:
- adjoint: float32 [192, 65536], P(None, ('gx', 'gy'))
- sensitivity: float32 [4, 192, 192], replicated
Inputs may be any that keep to these rules, and one draw needn't show every extreme that they name: `neighbours`: particles sit on a lattice cut into spatial tiles of 4 rows (wide direction) by 32 columns (short direction); tile t holds slots t * 128 to t * 128 + 127, tiles numbered along the short direction fastest, and slot p of a tile sits at row p // 32 and column p % 32 of its tile. An entry of -1 marks an empty slot. Any other entry names a particle whose lattice row and column differ from the particle's own by dr and dc with 0 < dr^2 + dc^2 <= 5; the entries of one particle's list name distinct particles.
All inputs are finite; a program needn't handle non-finite values.
Results may differ from a plain program's by a relative error of at most 0.0001.
Values sent between devices are 32-bit elements; how exact they have to be, the bound alone decides.
No kernel may reach another device: no remote copies, remote signals or barrier semaphores. Data moves between devices by JAX's collectives and lax.ppermute only.
A program may use at most 64 MiB of HBM per device.

v0:
```python
import jax
import jax.numpy as jnp
from jax import lax
from jax.sharding import PartitionSpec as P

KRYLOV = 2


HIGH = lax.Precision.HIGHEST


def from_behind(block, axis, distance):
    devices = range(lax.axis_size(axis))
    route = [(i - distance, i) for i in devices if i - distance in devices]
    return lax.ppermute(block, axis, route)


def extended_2(x, sides, width):
    for axis, dim in sides:
        size, length = (lax.axis_size(axis), x.shape[dim])
        up = [(i, (i + 1) % size) for i in range(size - 1)]
        down = [(j, i) for i, j in up]
        last = lax.slice_in_dim(x, length - width, length, axis=dim)
        first = lax.slice_in_dim(x, 0, width, axis=dim)
        before = lax.ppermute(last, axis, up)
        after = lax.ppermute(first, axis, down)
        x = jnp.concatenate([before, x, after], axis=dim)
    return x


def complex_blocks(real_part, imag_part):
    upper_rows = jnp.concatenate([real_part, -imag_part], axis=2)
    lower_rows = jnp.concatenate([imag_part, real_part], axis=2)
    return jnp.concatenate([upper_rows, lower_rows], axis=1)


def small_solve(normal, right, steps):
    factor = jnp.linalg.cholesky(normal)
    forward_vals = []
    for row_index in range(steps):
        partial_sum = right[row_index]
        for col_index in range(row_index):
            partial_sum = partial_sum - factor[row_index, col_index] * forward_vals[col_index]
        forward_vals.append(partial_sum / factor[row_index, row_index])
    backward_vals = [None] * steps
    for row_index in reversed(range(steps)):
        partial_sum = forward_vals[row_index]
        for col_index in range(row_index + 1, steps):
            partial_sum = partial_sum - factor[col_index, row_index] * backward_vals[col_index]
        backward_vals[row_index] = partial_sum / factor[row_index, row_index]
    return backward_vals


def fold_wide(partial_value, dim):
    centre = jnp.take(partial_value, 1, axis=dim)
    for offset, piece in (
        (1, jnp.take(partial_value, 2, axis=dim)),
        (-1, jnp.take(partial_value, 0, axis=dim)),
    ):
        centre = centre + from_behind(piece, "gx", offset)
    return centre


def fold_short(partial_value, dim):
    centre = jnp.take(partial_value, 1, axis=dim)
    for offset, piece in (
        (1, jnp.take(partial_value, 2, axis=dim)),
        (-1, jnp.take(partial_value, 0, axis=dim)),
    ):
        centre = centre + from_behind(piece, "gy", offset)
    return centre


def body(
    forward_coeff,
    incident,
    cost_grad,
    tmat_real,
    tmat_imag,
    translation_real,
    translation_imaginary,
    neighbours,
    particle_type,
):
    width = forward_coeff.shape[0]
    local_count = forward_coeff.shape[1]
    kinds = tmat_real.shape[0]
    slots = translation_real.shape[0]
    steps = KRYLOV
    tmats = complex_blocks(tmat_real, tmat_imag)
    trans = complex_blocks(translation_real, translation_imaginary)
    tmat_stack = jnp.swapaxes(tmats, 1, 2).reshape(kinds * width, width)
    trans_adj = jnp.swapaxes(trans, 1, 2)
    kind_ids = jnp.arange(kinds, dtype=jnp.int32)
    type_mask = (particle_type[None, :] == kind_ids[:, None]).astype(jnp.float32)
    short_count = lax.axis_size("gy")
    tile = neighbours // local_count
    offset_x = tile // short_count - lax.axis_index("gx")
    offset_y = tile % short_count - lax.axis_index("gy")
    inner = neighbours % local_count
    target = (offset_x + 1) * (3 * local_count) + (offset_y + 1) * local_count + inner
    target = jnp.where(neighbours >= 0, target, 9 * local_count)
    flat_target = target.reshape(-1)
    extended = extended_2(
        forward_coeff.reshape(width, 1, 1, local_count), (("gx", 1), ("gy", 2)), 1
    )
    extended = jnp.concatenate(
        [extended.reshape(width, 9 * local_count), jnp.zeros((width, 1), jnp.float32)], axis=1
    )
    gathered = extended[:, target]
    exciting = incident + jnp.einsum("sdc,csp->dp", trans, gathered, precision=HIGH)
    beta = jnp.sqrt(lax.psum(jnp.sum(cost_grad * cost_grad), ("gx", "gy")))
    basis = [cost_grad / beta]
    columns = []
    for column in range(steps):
        vector = basis[column]
        all_kinds = jnp.dot(tmat_stack, vector, precision=HIGH).reshape(kinds, width, local_count)
        scaled = jnp.sum(type_mask[:, None, :] * all_kinds, axis=0)
        translated = jnp.einsum("sdc,cp->dsp", trans_adj, scaled, precision=HIGH).reshape(
            width, slots * local_count
        )
        collected = (
            jnp.zeros((width, 9 * local_count + 1), jnp.float32).at[:, flat_target].add(translated)
        )
        partial_value = collected[:, : 9 * local_count].reshape(width, 3, 3, local_count)
        summed = fold_short(fold_wide(partial_value, 1), 1)
        image = vector - summed
        local_dots = jnp.stack([jnp.sum(vec_item * image) for vec_item in basis])
        projections = lax.psum(local_dots, ("gx", "gy"))
        for row_index in range(column + 1):
            image = image - projections[row_index] * basis[row_index]
        height = jnp.sqrt(lax.psum(jnp.sum(image * image), ("gx", "gy")))
        columns.append(
            jnp.concatenate(
                [projections, height[None], jnp.zeros((steps - column - 1,), jnp.float32)]
            )
        )
        basis.append(image / height)
    hessen = jnp.stack(columns, axis=1)
    normal = jnp.dot(hessen.T, hessen, precision=HIGH)
    weights = small_solve(normal, beta * hessen[0], steps)
    adjoint = weights[0] * basis[0]
    column = 1
    adjoint = adjoint + weights[column] * basis[column]
    masked = adjoint[None, :, :] * type_mask[:, None, :]
    local_terms = jnp.einsum("kcp,dp->kcd", masked, exciting, precision=HIGH)
    sensitivity = lax.psum(local_terms, ("gx", "gy"))
    return (adjoint, sensitivity)


def solution(mesh):
    placed = (
        P(None, ("gx", "gy")),
        P(None, ("gx", "gy")),
        P(None, ("gx", "gy")),
        P(),
        P(),
        P(),
        P(),
        P(None, ("gx", "gy")),
        P(("gx", "gy")),
    )
    return jax.shard_map(
        body, mesh=mesh, in_specs=placed, out_specs=(P(None, ("gx", "gy")), P()), check_vma=False
    )
```

profile of v0, /device:TPU:1, one launch (start us, length us, event | category | flops | bytes accessed | tf_op | source)
XLA Modules:
  0.0 891.4 jit_solution(2647792898957183860)
XLA Ops:
  7.2 1.6 multiply_reduce_fusion.5
  8.8 106.1 %psum.42 = f32[]{:T(128)} all-reduce(f32[]{:T(128)} %multiply_reduce_fusion.5), channel_id=1, replica_groups=mesh['gx'=64,'gy'=8] {'gx','gy'}, use_global_device_ids=true, to_apply=%region_1.2 | all-reduce | flops 1 | bytes 8 | tf_op jit(solution)/shard_map/psum | solution.py:112
  115.6 0.7 fusion.51
  116.2 0.9 neg.6
  117.2 1.3 copy.23
  118.6 0.2 copy.24
  118.9 1.8 fusion.10
  120.7 1.7 fusion.4
  122.5 0.4 copy.27
  122.9 0.3 copy-done.16
  123.3 8.3 scatter_custom_fusion
  131.8 0.2 copy.38
  131.9 2.8 collective-permute-start
  134.8 0.2 copy.39
  134.9 1.3 collective-permute-start.1
  136.2 0.2 copy.37
  136.4 4.0 collective-permute-done
  140.4 4.0 collective-permute-done.1
  144.5 4.3 collective-permute-start.2
  148.8 1.9 collective-permute-start.3
  150.8 4.0 collective-permute-done.3
  154.8 0.7 multiply_reduce_fusion.4
  155.5 96.5 %psum.43 = f32[1]{0:T(128)} all-reduce(f32[1]{0:T(128)} %bitcast.14), channel_id=1, replica_groups=mesh['gx'=64,'gy'=8] {'gx','gy'}, use_global_device_ids=true, to_apply=%region_5.12 | all-reduce | flops 1 | bytes 8 | tf_op jit(solution)/shard_map/psum | solution.py:129
  252.0 1.2 multiply_reduce_fusion.3
  253.2 96.0 %psum.44 = f32[]{:T(128)} all-reduce(f32[]{:T(128)} %multiply_reduce_fusion.3), channel_id=1, replica_groups=mesh['gx'=64,'gy'=8] {'gx','gy'}, use_global_device_ids=true, to_apply=%region_7.14 | all-reduce | flops 1 | bytes 8 | tf_op jit(solution)/shard_map/psum | solution.py:132
  349.8 0.6 broadcast_divide_fusion
  350.4 2.9 fusion.11
  353.3 1.7 fusion.7
  355.1 0.4 copy.31
  355.5 8.3 scatter_custom_fusion.1
  363.9 0.1 fusion.62
  364.0 0.2 copy.41
  364.2 2.6 collective-permute-start.4
  366.8 0.9 copy.42
  367.7 1.3 collective-permute-start.5
  369.0 4.0 collective-permute-start.8
  373.0 1.3 collective-permute-start.9
  374.3 0.4 collective-permute-done.8
  374.6 5.3 collective-permute-done.9
  380.0 4.1 collective-permute-start.10
  384.0 1.9 collective-permute-start.11
  386.0 0.2 copy.40
  386.1 1.0 fusion.20
  387.2 3.6 collective-permute-start.6
  390.8 2.1 collective-permute-start.7
  393.1 0.4 copy.36
  393.6 4.1 gather_fusion
  397.7 1.6 multiply_reduce_fusion.2
  399.3 1.4 pad_maximum_fusion.3
  400.7 5.7 fusion.13
  406.4 100.3 %psum.45 = f32[2]{0:T(128)S(1)} all-reduce(f32[2]{0:T(128)S(1)} %pad_maximum_fusion.3), channel_id=1, replica_groups=mesh['gx'=64,'gy'=8] {'gx','gy'}, use_global_device_ids=true, to_apply=%region_12.19 | all-reduce | flops 2 | bytes 16 | tf_op jit(solution)/shard_map/psum | solution.py:129
  506.7 0.6 fusion.66
  507.3 1.9 multiply_reduce_fusion
  509.2 0.7 maximum_bitcast_fusion.3
  509.9 95.3 %psum.46 = f32[]{:T(128)} all-reduce(f32[]{:T(128)} %multiply_reduce_fusion), channel_id=1, replica_groups=mesh['gx'=64,'gy'=8] {'gx','gy'}, use_global_device_ids=true, to_apply=%region_14.21 | all-reduce | flops 1 | bytes 8 | tf_op jit(solution)/shard_map/psum | solution.py:132
  605.9 0.1 fusion.67
  606.1 0.2 cholesky.18
  606.4 0.6 compare_reduce_fusion
  607.0 0.6 compare_select_fusion.3
  607.7 0.6 fusion.64
  608.3 0.6 fusion.65
  614.1 1.7 fusion.18
  615.8 266.7 %all-reduce.3.cloned.1.call-done = f32[4,192,192]{2,1,0:T(8,128)} async-done(((f32[4,192,192]{2,1,0:T(8,128)}), f32[4,192,192]{2,1,0:T(8,128)}) %all-reduce.3.cloned.1.call-update) | async-done | bytes 589840 | tf_op jit(solution)/shard_map/psum | solution.py:147
  882.4 2.1 copy.46
  (66 shorter events, 1.0 us)
Async XLA Ops:
  7.2 111.5 %copy-start.1 = (f32[10,96,96]{2,1,0:T(8,128)S(1)}, f32[10,96,96]{2,1,0:T(8,128)}, u32[]{:S(2)}) copy-start(f32[10,96,96]{2,1,0:T(8,128)} %param.26) | copy-start | bytes 1105924
  7.2 875.3 %all-reduce.3.cloned.1.call-start = ((), (), s32[]{:S(2)}) async-start(), calls=%async_computation | async-start | bytes 1572864 | tf_op jit(solution)/shard_map/psum | solution.py:147
  116.2 234.2 %copy-start.14 = (f32[4,128]{1,0:T(4,128)}, f32[4,128]{1,0:T(4,128)S(1)}, u32[]{:S(2)}) copy-start(f32[4,128]{1,0:T(4,128)S(1)} %fusion.51) | copy-start | bytes 6148
  117.2 1.7 copy-start.12
  117.2 1.7 copy-start
  117.2 1.7 copy-start.10
  117.2 1.7 copy-start.17
  118.6 2.1 copy-start.2
  118.9 3.6 copy-start.5
  122.5 0.7 copy-start.16
  131.9 8.5 collective-permute-start
  134.9 9.5 %collective-permute-start.1 = (f32[192,3,128]{2,0,1:T(8,128)S(1)}, f32[192,3,128]{2,0,1:T(8,128)S(1)}, u32[]{:S(2)}, u32[]{:S(2)}) collective-permute-start(f32[192,3,128]{2,0,1:T(8,128)S(1)} %bitcast.132), channel_id=1, source_target_pairs={{8,0},{16,8},{24,16},{32,24},{40,32},{48,40},{56,48},{64,56},{72,6... | collective-permute-start | bytes 884744 | tf_op jit(solution)/shard_map/ppermute | solution.py:15
  136.4 214.0 %copy-start.11 = (f32[4,96,96]{2,1,0:T(8,128)S(1)}, f32[4,96,96]{2,1,0:T(8,128)}, u32[]{:S(2)}) copy-start(f32[4,96,96]{2,1,0:T(8,128)} %param.25) | copy-start | bytes 442372
  136.4 214.0 %copy-start.13 = (f32[4,96,96]{2,1,0:T(8,128)S(1)}, f32[4,96,96]{2,1,0:T(8,128)}, u32[]{:S(2)}) copy-start(f32[4,96,96]{2,1,0:T(8,128)} %copy-done.12) | copy-start | bytes 442372
  144.5 208.8 %copy-start.3 = (f32[10,96,96]{1,2,0:T(8,128)S(1)}, f32[10,96,96]{1,2,0:T(8,128)}, u32[]{:S(2)}) copy-start(f32[10,96,96]{1,2,0:T(8,128)} %copy-done.2) | copy-start | bytes 1105924
  144.5 208.8 %copy-start.6 = (f32[10,96,96]{1,2,0:T(8,128)S(1)}, f32[10,96,96]{1,2,0:T(8,128)}, u32[]{:S(2)}) copy-start(f32[10,96,96]{1,2,0:T(8,128)} %copy-done.5) | copy-start | bytes 1105924
  144.5 6.3 collective-permute-start.2
  148.8 5.9 collective-permute-start.3
  363.9 5.1 copy-start.8
  364.2 22.0 %collective-permute-start.4 = (f32[192,3,128]{2,0,1:T(8,128)S(1)}, f32[192,3,128]{2,0,1:T(8,128)S(1)}, u32[]{:S(2)}, u32[]{:S(2)}) collective-permute-start(f32[192,3,128]{2,0,1:T(8,128)S(1)} %bitcast.130), channel_id=1, source_target_pairs={{0,8},{8,16},{16,24},{24,32},{32,40},{40,48},{48,56},{56,64},{64,7... | collective-permute-start | bytes 884744 | tf_op jit(solution)/shard_map/ppermute | solution.py:15
  367.7 18.5 %collective-permute-start.5 = (f32[192,3,128]{2,0,1:T(8,128)}, f32[192,3,128]{2,0,1:T(8,128)}, u32[]{:S(2)}, u32[]{:S(2)}) collective-permute-start(f32[192,3,128]{2,0,1:T(8,128)} %bitcast.26), channel_id=1, source_target_pairs={{8,0},{16,8},{24,16},{32,24},{40,32},{48,40},{56,48},{64,56},{72,6... | collective-permute-start | bytes 884744 | tf_op jit(solution)/shard_map/ppermute | solution.py:15
  369.0 5.7 collective-permute-start.8
  373.0 7.0 collective-permute-start.9
  380.0 13.0 %collective-permute-start.10 = (f32[192,3,1,128]{3,0,2,1:T(8,128)S(1)}, f32[192,3,1,128]{3,0,2,1:T(8,128)S(1)}, u32[]{:S(2)}, u32[]{:S(2)}) collective-permute-start(f32[192,3,1,128]{3,0,2,1:T(8,128)S(1)} %pad_maximum_fusion.1), channel_id=1, source_target_pairs={{0,1},{1,2},{2,3},{3,4},{4,5},{5,6},{6,7},{8,9},{9,10},{10,11},{11... | collective-permute-start | bytes 884744 | tf_op jit(solution)/shard_map/ppermute | solution.py:25
  384.0 9.0 %collective-permute-start.11 = (f32[192,3,1,128]{3,0,2,1:T(8,128)S(1)}, f32[192,3,1,128]{3,0,2,1:T(8,128)S(1)}, u32[]{:S(2)}, u32[]{:S(2)}) collective-permute-start(f32[192,3,1,128]{3,0,2,1:T(8,128)S(1)} %pad_maximum_fusion.1), channel_id=1, source_target_pairs={{1,0},{2,1},{3,2},{4,3},{5,4},{6,5},{7,6},{9,8},{10,9},{11,10},{12... | collective-permute-start | bytes 884744 | tf_op jit(solution)/shard_map/ppermute | solution.py:26
  387.2 10.5 %collective-permute-start.6 = (f32[192,128]{1,0:T(8,128)S(1)}, f32[192,128]{1,0:T(8,128)}, u32[]{:S(2)}, u32[]{:S(2)}) collective-permute-start(f32[192,128]{1,0:T(8,128)S(1)} %get-tuple-element.87), channel_id=1, source_target_pairs={{0,1},{1,2},{2,3},{3,4},{4,5},{5,6},{6,7},{8,9},{9,10},{10,11},{11... | collective-permute-start | bytes 294920 | tf_op jit(solution)/shard_map/ppermute | solution.py:15
  390.8 6.9 collective-permute-start.7
  393.5 7.2 copy-start.4
  393.5 7.2 copy-start.7
  393.5 7.2 copy-start.18
  400.7 213.4 %copy-start.15 = (f32[4,128]{1,0:T(4,128)S(1)}, f32[4,128]{1,0:T(4,128)}, u32[]{:S(2)}) copy-start(f32[4,128]{1,0:T(4,128)} %copy-done.14) | copy-start | bytes 6148
  614.1 270.5 %copy-start.9 = (f32[192,128]{1,0:T(8,128)}, f32[192,128]{1,0:T(8,128)S(1)}, u32[]{:S(2)}) copy-start(f32[192,128]{1,0:T(8,128)S(1)} %multiply_add_fusion) | copy-start | bytes 294916
Sparse Core Ops, SparseCore 0:
  615.9 266.5 all-reduce.2
where the time goes:
time: 893 us; the launch traced here: 891 us
  blocking collectives  494 us (55%)
  waiting for transfers between devices  284 us (32%)
  starting transfers between devices  31.4 us (4%)
  other arithmetic  30.8 us (3%)
  between operations  21.8 us (2%)
  matrix products  15.7 us (2%)
  local copies, waits for them, and re-layouts  13.2 us (1%)
    psum x1, waiting for transfers between devices, body(): sensitivity = lax.psum(local_terms, ('gx', 'gy'))  267 us
    psum x2, blocking collectives, body(): projections = lax.psum(local_dots, ('gx', 'gy'))  197 us
    psum x2, blocking collectives, body(): height = jnp.sqrt(lax.psum(jnp.sum(image * image), ('gx', 'gy')))  191 us
    psum x1, blocking collectives, body(): beta = jnp.sqrt(lax.psum(jnp.sum(cost_grad * cost_grad), ('gx', 'gy')))  106 us
    ppermute x8, starting transfers between devices, from_behind(): return lax.ppermute(block, axis, route)  20.1 us
  transfers between devices with their start and end apart: 13, of which 6 were waited for; matrix products, arithmetic and copies ran while one was open for 1% of the time, Pallas kernels for 0%

commit v1 on v0

v1 whole, which is shorter than its diff:
```python
import jax
import jax.numpy as jnp
from jax import lax
from jax.experimental import pallas as pl
from jax.experimental.pallas import tpu as pltpu
from jax.sharding import PartitionSpec as P

F32 = jnp.float32
BF16 = jnp.bfloat16
W = 192
HALF = 96
PT = 128
SLOTS = 10
KINDS = 4
META = 16
ROWS = W + META
CHUNK = 296
VMEM = 56 * 1024 * 1024


def params():
    return pltpu.CompilerParams(vmem_limit_bytes=VMEM)


def split(x):
    hi = x.astype(BF16)
    return hi, (x - hi.astype(F32)).astype(BF16)


def dot(a, b):
    return lax.dot_general(a, b, (((1,), (0,)), ((), ())), preferred_element_type=F32)


def dot_nt(a, b):
    return lax.dot_general(a, b, (((1,), (1,)), ((), ())), preferred_element_type=F32)


def lanes(rows):
    return lax.broadcasted_iota(jnp.int32, (rows, PT), 1)


def pack_wide_kernel(fc_ref, b_ref, nb_ref, pt_ref, up_ref, dn_ref):
    meta = jnp.concatenate(
        [
            (nb_ref[...] + 1).astype(F32),
            pt_ref[...].astype(F32),
            jnp.zeros((META - SLOTS - 1, PT), F32),
        ],
        axis=0,
    )
    top, low = fc_ref[0:HALF, :], fc_ref[HALF:W, :]
    first = lanes(HALF) < 64
    for ref in (up_ref, dn_ref):
        ref[0:W, :] = b_ref[...]
        ref[W:ROWS, :] = meta
    up_ref[ROWS : ROWS + HALF, :] = jnp.where(first, pltpu.roll(top, 64, 1), low)
    dn_ref[ROWS : ROWS + HALF, :] = jnp.where(first, top, pltpu.roll(low, 64, 1))


def unpack_fc(up, dn):
    first = lanes(HALF) < 64
    return jnp.concatenate(
        [
            jnp.where(first, dn, pltpu.roll(up, 64, 1)),
            jnp.where(first, pltpu.roll(dn, 64, 1), up),
        ],
        axis=0,
    )


def pack_short_kernel(fc_ref, own_ref, up_ref, dn_ref, lo_ref, hi_ref):
    first = lanes(META) < 64
    fc_ud = unpack_fc(up_ref[ROWS : ROWS + HALF, :], dn_ref[ROWS : ROWS + HALF, :])

    def part(rows, tiles):
        col = lanes(rows.stop - rows.start) % 32
        up, own, dn, edge, edge_ud = tiles

        def moved(x, shift):
            return pltpu.roll(x, shift, 1) if shift else x

        low = moved(up, 0)
        low = jnp.where(col < 4, low, moved(own, 4))
        low = jnp.where(col < 8, low, moved(dn, 8))
        low = jnp.where(col < 12, low, moved(edge, 12))
        lo_ref[rows, :] = jnp.where(col < 14, low, moved(edge_ud, 14))
        high = moved(edge, 114)
        high = jnp.where(col < 18, high, moved(edge_ud, 116))
        high = jnp.where(col < 20, high, moved(up, 120))
        high = jnp.where(col < 24, high, moved(own, 124))
        hi_ref[rows, :] = jnp.where(col < 28, high, dn)

    part(slice(0, W), (up_ref[0:W, :], own_ref[0:W, :], dn_ref[0:W, :], fc_ref[...], fc_ud))
    m = slice(W, ROWS)
    meta_ud = jnp.where(first, dn_ref[m, :], up_ref[m, :])
    part(m, (up_ref[m, :], own_ref[m, :], dn_ref[m, :], own_ref[m, :], meta_ud))


def target_ids(base, row_stride):
    spot = lax.broadcasted_iota(jnp.int32, (3 * PT, PT), 0)
    lane = spot % PT
    row, col = lane // 32, lane % 32
    shift = jnp.where(row < 2, row_stride, -row_stride)
    own = base + lane
    beside = base + row * 32
    lr = jnp.where(
        col < 14,
        beside + PT + col - 12,
        jnp.where(
            col < 16,
            beside + PT + shift + col - 14,
            jnp.where(col < 18, beside - PT + col + 14, beside - PT + shift + col + 12),
        ),
    )
    lr = jnp.where((col >= 12) & (col < 20), lr, -10)
    ids = jnp.where(spot < PT, own, jnp.where(spot < 2 * PT, own + shift, lr))
    return jnp.where(ids >= 0, ids + 1, -10).astype(F32)


def main_kernel(
    base_ref,
    own_ref,
    up_ref,
    dn_ref,
    lf_ref,
    rt_ref,
    fc_ref,
    inc_ref,
    tw_ref,
    lw_ref,
    fw_ref,
    chunk_ref,
    u1_ref,
    ghi_ref,
    glo_ref,
):
    m = slice(W, ROWS)
    ids = target_ids(base_ref[0], base_ref[1])
    own_ids = ids[0:PT, :]
    first = lanes(META) < 64
    col = lanes(META) % 32
    b = own_ref[0:W, :]
    m_own, m_up, m_dn = own_ref[m, :], up_ref[m, :], dn_ref[m, :]
    m_ud = jnp.where(first, m_dn, m_up)
    wide = lanes(W) % 32 >= 16
    m_lr = jnp.where(col >= 16, lf_ref[m, :], rt_ref[m, :])
    x_lr = jnp.where(wide, lf_ref[0:W, :], rt_ref[0:W, :])
    b_zone = (col < 12) | (col >= 20)
    row_id = lax.broadcasted_iota(jnp.int32, (META, PT), 0)
    m_b = jnp.where(b_zone | (row_id >= SLOTS), m_lr, 0.0)
    m_f = jnp.where(b_zone & (row_id < SLOTS), 0.0, m_lr)

    def product(w_ref, hi, lo):
        rows = dot(w_ref[...], hi)
        return rows[0:W] + rows[W : 2 * W] + dot(w_ref[0:W, :], lo)

    def scaled_by_type(blocks, metas):
        his, los = [], []
        for v, meta in zip(blocks, metas):
            hi, lo = split(v)
            kind = meta[SLOTS : SLOTS + 1, :]
            his.append([jnp.where(kind == float(k), hi, jnp.zeros_like(hi)) for k in range(KINDS)])
            los.append([jnp.where(kind == float(k), lo, jnp.zeros_like(lo)) for k in range(KINDS)])
        hi = jnp.concatenate(
            [jnp.concatenate([h[k] for h in his], axis=1) for k in range(KINDS)], axis=0
        )
        lo = jnp.concatenate(
            [jnp.concatenate([x[k] for x in los], axis=1) for k in range(KINDS)], axis=0
        )
        s_hi, s_lo = split(product(tw_ref, hi, lo))
        return jnp.concatenate([s_hi, s_lo], axis=0)

    def one_hot(at, meta, s):
        return jnp.where(at == meta[s : s + 1, :], 1.0, 0.0).astype(BF16)

    metas = (m_own, m_up, m_dn, m_b)
    stack = scaled_by_type((b, up_ref[0:W, :], dn_ref[0:W, :], x_lr), metas)
    for s in range(SLOTS):
        pick = jnp.concatenate([one_hot(ids, meta, s) for meta in metas], axis=1)
        g = dot_nt(stack, pick)
        hi, lo = split(g[0:W] + g[W : 2 * W])
        ghi_ref[s * W : (s + 1) * W, :] = hi
        glo_ref[s * W : (s + 1) * W, :] = lo
    u1_all = product(lw_ref, ghi_ref[...], glo_ref[...])
    u1 = u1_all[:, 0:PT]
    u1_ref[...] = u1

    metas = (m_own, m_ud, m_f)
    stack = scaled_by_type([u1_all[:, i * PT : (i + 1) * PT] for i in range(3)], metas)
    for s in range(0, SLOTS, 2):
        pick = jnp.concatenate(
            [
                jnp.concatenate([one_hot(own_ids, meta, t) for meta in metas], axis=1)
                for t in (s, s + 1)
            ],
            axis=0,
        )
        g = dot_nt(stack, pick)
        hi, lo = split(g[0:W] + g[W : 2 * W])
        for t in (0, 1):
            rows = slice((s + t) * W, (s + t + 1) * W)
            ghi_ref[rows, 0:PT] = hi[:, t * PT : (t + 1) * PT]
            glo_ref[rows, 0:PT] = lo[:, t * PT : (t + 1) * PT]
    u2 = product(lw_ref, ghi_ref[:, 0:PT], glo_ref[:, 0:PT])

    fc_ud = unpack_fc(up_ref[ROWS : ROWS + HALF, :], dn_ref[ROWS : ROWS + HALF, :])
    f_hi, f_lo = split(jnp.concatenate([fc_ref[...], fc_ud, x_lr], axis=1))
    stack = jnp.concatenate([f_hi, f_lo], axis=0)
    for s in range(0, SLOTS, 2):
        pick = jnp.concatenate([one_hot(ids, m_own, s), one_hot(ids, m_own, s + 1)], axis=1)
        g = dot(stack, pick).astype(BF16)
        for t in (0, 1):
            rows = slice((s + t) * W, (s + t + 1) * W)
            ghi_ref[rows, PT : 2 * PT] = g[0:W, t * PT : (t + 1) * PT]
            glo_ref[rows, PT : 2 * PT] = g[W : 2 * W, t * PT : (t + 1) * PT]
    exc = inc_ref[...] + product(fw_ref, ghi_ref[:, PT : 2 * PT], glo_ref[:, PT : 2 * PT])

    e_hi, e_lo = split(jnp.concatenate([exc, jnp.zeros((64, PT), F32)], axis=0))
    v_hi, v_lo = split(jnp.concatenate([b, u1], axis=0))
    kind = m_own[SLOTS : SLOTS + 1, :]
    for k in range(KINDS):
        here = kind == float(k)
        k_hi = jnp.where(here, v_hi, jnp.zeros_like(v_hi))
        k_lo = jnp.where(here, v_lo, jnp.zeros_like(v_lo))
        out = dot_nt(k_hi, e_hi) + dot_nt(k_lo, e_hi) + dot_nt(k_hi, e_lo)
        for which in range(2):
            for h in range(2):
                block = out[which * W + h * HALF : which * W + (h + 1) * HALF, :]
                at = which * 144
                chunk_ref[2 * k + h, at : at + 96, :] = block[:, 0:PT]
                chunk_ref[2 * k + h, at + 96 : at + 144, :] = block[0:48, PT:] + pltpu.roll(
                    block[48:96, PT:], 64, 1
                )

    lane = lanes(8)
    gram = jnp.zeros((8, PT), F32)
    for i, (p, q) in enumerate(((b, b), (b, u1), (u1, u1), (b, u2), (u1, u2), (u2, u2))):
        gram = jnp.where(lane == i, jnp.sum(p * q), gram)
    for g in range(8):
        chunk_ref[g, 288:296, :] = gram


def spread_kernel(in_ref, out_ref):
    total = in_ref[0]
    for i in range(1, 8):
        total = total + in_ref[i]
    out_ref[...] = jnp.zeros_like(out_ref)
    for which in range(2):
        for j in range(3):
            at = which * 144 + j * 48
            out_ref[pl.ds(3 * which + j, 48, 8), :] = total[at : at + 48, :]
    out_ref[pl.ds(6, 64, 8), :] = jnp.broadcast_to(total[288:289, :], (64, PT))


def combine_kernel(in_ref, b_ref, u1_ref, out_ref, adj_ref):
    total = jnp.sum(in_ref[...].reshape(64, 8, PT), axis=0)
    lane = lanes(1)

    def entry(i):
        return jnp.sum(jnp.where(lane == i, total[6:7, :], 0.0), axis=1, keepdims=True)

    g00, g01, g11, g02, g12, g22 = [entry(i) for i in range(6)]
    alpha = g01 / g00
    beta = jnp.sqrt(g00)
    p2 = g11 - alpha * g01
    pn = jnp.sqrt(p2)
    h00 = 1.0 - alpha
    h10 = pn / beta
    h01 = (g02 - alpha * g01) / (beta * pn)
    qv1 = (g12 - alpha * g11 - alpha * g02 + alpha * alpha * g01) / p2
    h11 = 1.0 - qv1
    n00 = h00 * h00 + h10 * h10
    n01 = h00 * h01 + h10 * h11
    n11 = 1.0 - 2.0 * qv1 + (g22 - 2.0 * alpha * g12 + alpha * alpha * g11) / p2
    r0 = beta * h00
    r1 = beta * h01
    f00 = jnp.sqrt(n00)
    f10 = n01 / f00
    f11 = jnp.sqrt(n11 - f10 * f10)
    y0 = r0 / f00
    y1 = (r1 - f10 * y0) / f11
    w1 = y1 / f11
    w0 = (y0 - f10 * w1) / f00
    c1 = -w1 / pn
    c0 = w0 / beta - c1 * alpha
    mixed = jnp.concatenate(
        [c0 * total[0:3, :] + c1 * total[3:6, :], jnp.zeros((5, PT), F32)], axis=0
    )
    for i in range(64):
        out_ref[8 * i : 8 * i + 8, :] = mixed
    adj_ref[...] = c0 * b_ref[...] + c1 * u1_ref[...]


def expand_kernel(in_ref, out_ref):
    a0 = in_ref[pl.ds(0, 48, 8), :]
    a1 = in_ref[pl.ds(1, 48, 8), :]
    edge = in_ref[pl.ds(2, 48, 8), :]
    turned = pltpu.roll(edge, 64, 1)
    for i in range(8):
        out_ref[i, 0:48, 0:PT] = a0
        out_ref[i, 48:96, 0:PT] = a1
        out_ref[i, 0:48, PT:W] = edge[:, 0:64]
        out_ref[i, 48:96, PT:W] = turned[:, 0:64]


def call(kernel, shapes, *args, smem=0, **kw):
    return pl.pallas_call(
        kernel,
        out_shape=[jax.ShapeDtypeStruct(s, F32) for s in shapes],
        in_specs=[pl.BlockSpec(memory_space=pltpu.SMEM)] * smem
        + [pl.BlockSpec(memory_space=pltpu.VMEM)] * (len(args) - smem),
        compiler_params=params(),
        **kw,
    )(*args)


def complex_blocks(real_part, imag_part):
    upper_rows = jnp.concatenate([real_part, -imag_part], axis=2)
    lower_rows = jnp.concatenate([imag_part, real_part], axis=2)
    return jnp.concatenate([upper_rows, lower_rows], axis=1)


def weight_pair(w):
    n = w.shape[0]
    side = jnp.swapaxes(w, 0, 1).reshape(W, n * W)
    hi = lax.reduce_precision(side, 8, 7)
    return jnp.concatenate([hi, side - hi], axis=0).astype(BF16)


def shifted(block, axis, step):
    n = lax.axis_size(axis)
    return lax.ppermute(block, axis, [(i, i + step) for i in range(n) if 0 <= i + step < n])


def body(
    forward_coeff,
    incident,
    cost_grad,
    tmat_real,
    tmat_imag,
    translation_real,
    translation_imaginary,
    neighbours,
    particle_type,
):
    n_short = lax.axis_size("gy")
    tile = lax.axis_index("gx") * n_short + lax.axis_index("gy")
    base = jnp.stack([tile * PT, jnp.int32(n_short * PT)]).astype(jnp.int32)

    to_up, to_dn = call(
        pack_wide_kernel,
        [(ROWS + HALF, PT)] * 2,
        forward_coeff,
        cost_grad,
        neighbours,
        particle_type.reshape(1, PT),
    )
    up = shifted(to_up, "gx", 1)
    dn = shifted(to_dn, "gx", -1)
    to_lo, to_hi = call(
        pack_short_kernel, [(ROWS, PT)] * 2, forward_coeff, to_up, up, dn
    )
    lf = shifted(to_hi, "gy", 1)
    rt = shifted(to_lo, "gy", -1)

    tmats = complex_blocks(tmat_real, tmat_imag)
    trans = complex_blocks(translation_real, translation_imaginary)
    tw = weight_pair(jnp.swapaxes(tmats, 1, 2))
    lw = weight_pair(jnp.swapaxes(trans, 1, 2))
    fw = weight_pair(trans)

    chunks, u1 = call(
        main_kernel,
        [(8, CHUNK, PT), (W, PT)],
        base,
        to_up,
        up,
        dn,
        lf,
        rt,
        forward_coeff,
        incident,
        tw,
        lw,
        fw,
        smem=1,
        scratch_shapes=[pltpu.VMEM((SLOTS * W, 3 * PT), BF16)] * 2,
    )
    got = lax.all_to_all(chunks, "gy", 0, 0)
    (pieces,) = call(spread_kernel, [(512, PT)], got)
    got = lax.all_to_all(pieces.reshape(64, 8, PT), "gx", 0, 0)
    mixed, adjoint = call(
        combine_kernel, [(512, PT), (W, PT)], got.reshape(512, PT), cost_grad, u1
    )
    got = lax.all_to_all(mixed.reshape(64, 8, PT), "gx", 0, 0)
    (copies,) = call(expand_kernel, [(8, HALF, W)], got.reshape(512, PT))
    sensitivity = lax.all_to_all(copies, "gy", 0, 0).reshape(KINDS, W, W)
    return (adjoint, sensitivity)


def solution(mesh):
    placed = (
        P(None, ("gx", "gy")),
        P(None, ("gx", "gy")),
        P(None, ("gx", "gy")),
        P(),
        P(),
        P(),
        P(),
        P(None, ("gx", "gy")),
        P(("gx", "gy")),
    )
    return jax.shard_map(
        body, mesh=mesh, in_specs=placed, out_specs=(P(None, ("gx", "gy")), P()), check_vma=False
    )
```

time: 893 us -> 148 us (0.17)
  blocking collectives: 494 us -> 89.8 us
  waiting for transfers between devices: 284 us -> 2.18 us
  Pallas kernels: 0 us -> 21.2 us
  between operations: 21.8 us -> 0.79 us
  other arithmetic: 30.8 us -> 10.4 us
  starting transfers between devices: 31.4 us -> 13.3 us
  matrix products: 15.7 us -> 0 us
    psum x5 -> x0, blocking collectives: 494 us -> none  [the longest x2 197 us: body(): projections = lax.psum(local_dots, ('gx', 'gy'))]
    psum x1 -> x0, waiting for transfers between devices: 267 us -> none  [body(): sensitivity = lax.psum(local_terms, ('gx', 'gy'))]
    all_to_all x0 -> x4, blocking collectives: none -> 89.8 us  [the longest x1 30.6 us: body(): got = lax.all_to_all(pieces.reshape(64, 8, PT), 'gx', 0, 0)]
    pallas_call x0 -> x6, Pallas kernels: none -> 21.2 us  [call(): pl.pallas_call(kernel, out_shape=[jax.ShapeDtypeStruct(s, F32) for s in s...]
    ppermute x12 -> x4, starting transfers between devices: 31.3 us -> 13.3 us  [shifted(): lax.ppermute(block, axis, [(i, i + step) for i in range(n) if 0 <= i + st...]
    scatter-add x2 -> x0, other arithmetic: 16.6 us -> none  [body(): jnp.zeros((width, 9 * local_count + 1), jnp.float32).at[:, flat_target]]
    dot_general x7 -> x0, matrix products: 15.7 us -> none  [the longest x1 5.7 us: body(): jnp.einsum('sdc,csp->dp', trans, gathered, precision=HIGH)]
    ppermute x12 -> x4, waiting for transfers between devices: 17.6 us -> 2.18 us  [shifted(): lax.ppermute(block, axis, [(i, i + step) for i in range(n) if 0 <= i + st...]
  transfers between devices with their start and end apart: 13 -> 4, of which waited for: 6 -> 1; matrix products, arithmetic and copies ran while one was open for 1% -> 12% of each run, Pallas kernels for 0% -> 0%
where the time goes in v1:
time: 148 us; the launch traced here: 147 us
  blocking collectives  89.8 us (61%)
  Pallas kernels  21.2 us (14%)
  starting transfers between devices  13.3 us (9%)
  other arithmetic  10.4 us (7%)
  local copies, waits for them, and re-layouts  9.07 us (6%)
  waiting for transfers between devices  2.18 us (1%)
    all_to_all x1, blocking collectives, body(): got = lax.all_to_all(pieces.reshape(64, 8, PT), 'gx', 0, 0)  30.6 us
    pallas_call x6, Pallas kernels, call(): pl.pallas_call(kernel, out_shape=[jax.ShapeDtypeStruct(s, F32) for s in s...  21.2 us
    all_to_all x1, blocking collectives, body(): got = lax.all_to_all(chunks, 'gy', 0, 0)  21.2 us
    all_to_all x1, blocking collectives, body(): sensitivity = lax.all_to_all(copies, 'gy', 0, 0).reshape(KINDS, W, W)  19.8 us
    all_to_all x1, blocking collectives, body(): got = lax.all_to_all(mixed.reshape(64, 8, PT), 'gx', 0, 0)  18.3 us
    ppermute x4, starting transfers between devices, shifted(): lax.ppermute(block, axis, [(i, i + step) for i in range(n) if 0 <= i + st...  13.3 us
    reshape x3, local copies, waits for them, and re-layouts, weight_pair(): side = jnp.swapaxes(w, 0, 1).reshape(W, n * W)  4.16 us
    concatenate x2, other arithmetic, weight_pair(): return jnp.concatenate([hi, side - hi], axis=0).astype(BF16)  3.81 us
  transfers between devices with their start and end apart: 4, of which 1 were waited for; matrix products, arithmetic and copies ran while one was open for 12% of the time, Pallas kernels for 0%

profile of v1, /device:TPU:1, one launch (start us, length us, event | category | flops | bytes accessed | tf_op | source)
XLA Modules:
  0.0 146.8 jit_solution(17725810588421903936)
XLA Ops:
  0.6 0.0 copy-start.4
  0.6 0.0 copy-start.6
  0.7 1.8 %shard_map.104 = (f32[304,128]{1,0:T(8,128)}, f32[304,128]{1,0:T(8,128)}) custom-call(f32[192,128]{1,0:T(8,128)} %fc_ref.5, f32[192,128]{1,0:T(8,128)} %b_ref.3, s32[10,128]{1,0:T(8,128)} %nb_ref.1, s32[1,128]{1,0:T(1,128)} %bitcast.24), custom_call_target="tpu_custom_call" | custom-call | tf_op jit(solution)/shard_map/pallas_call | solution.py:307
  2.5 4.7 %collective-permute-start = (f32[304,128]{1,0:T(8,128)}, f32[304,128]{1,0:T(8,128)}, u32[]{:S(2)}, u32[]{:S(2)}) collective-permute-start(f32[304,128]{1,0:T(8,128)} %get-tuple-element.10.own_ref), channel_id=1, source_target_pairs={{0,8},{8,16},{16,24},{24,32},{32,40},{40,48},{48,56},{56,64},{64,7... | collective-permute-start | bytes 466952 | tf_op jit(solution)/shard_map/ppermute | solution.py:332
  7.2 1.3 collective-permute-start.1
  8.5 1.1 neg.7
  9.5 0.0 copy-done.4
  9.5 0.0 copy-done.6
  9.6 1.9 %fusion.3 = (f32[192,10,192]{2,0,1:T(8,128)}, f32[10,192,192]{2,1,0:T(8,128)S(1)}) fusion(f32[10,96,96]{2,1,0:T(8,128)S(1)} %copy-done.6, f32[10,96,96]{2,1,0:T(8,128)S(1)} %copy-done.4, f32[10,96,96]{2,1,0:T(8,128)S(1)} %neg.7), kind=kLoop, calls=%fused_computation.15 | loop fusion | flops 1105920 | bytes 4055040 | tf_op jit(solution)/shard_map/transpose | solution.py:325
  11.5 3.0 %copy.17 = f32[192,10,192]{0,2,1:T(8,128)} copy(f32[192,10,192]{2,0,1:T(8,128)} %get-tuple-element.20) | data formatting | bytes 2949120 | tf_op jit(solution)/shard_map/transpose | solution.py:325
  14.4 2.0 %copy.18 = f32[192,1920]{1,0:T(8,128)S(1)} copy(f32[192,1920]{0,1:T(8,128)} %bitcast.17) | data formatting | bytes 2949120 | tf_op jit(solution)/shard_map/reshape | solution.py:325
  16.5 1.3 reduce-precision_convert_fusion
  17.8 1.1 copy.15
  18.9 0.0 copy-start.5
  18.9 0.0 copy-start.7
  18.9 1.3 reduce-precision_convert_fusion.1
  20.2 0.0 copy-done.5
  20.2 0.0 copy-done.7
  20.2 0.0 copy-start
  20.2 0.0 copy-start.1
  20.2 0.0 copy-start.2
  20.2 0.3 maximum_maximum_fusion.1
  20.5 1.1 copy.20
  21.6 0.0 copy-done
  21.6 0.0 copy-done.1
  21.6 0.4 copy-done.2
  22.0 0.0 copy-start.3
  22.0 3.0 %pad_maximum_fusion = (bf16[384,1920]{1,0:T(8,128)(2,1)}, bf16[384,1920]{1,0:T(8,128)(2,1)}) fusion(bf16[192,1920]{1,0:T(8,128)(2,1)} %get-tuple-element.23, bf16[192,1920]{1,0:T(8,128)(2,1)S(1)} %copy-done.2, bf16[192,1920]{1,0:T(8,128)(2,1)S(1)} %copy-done.1, bf16[192,1920]{1,0:T(8,128)(2,1)S(1)} %copy-done), kind=kLoop, calls=%fused_computation.7 | loop fusion | flops 5898240 | bytes 5898240 | tf_op jit(solution)/shard_map/concatenate | solution.py:327
  24.9 0.0 copy-done.3
  24.9 0.1 reduce-precision_convert_fusion.2
  25.0 0.9 pad_maximum_fusion.2.tw_ref
  25.9 0.0 collective-permute-done.up_ref
  25.9 0.0 collective-permute-done.1.dn_ref
  25.9 2.1 %shard_map.105 = (f32[208,128]{1,0:T(8,128)}, f32[208,128]{1,0:T(8,128)}) custom-call(f32[192,128]{1,0:T(8,128)} %fc_ref.5, f32[304,128]{1,0:T(8,128)} %get-tuple-element.10.own_ref, f32[304,128]{1,0:T(8,128)} %collective-permute-done.up_ref, f32[304,128]{1,0:T(8,128)} %collective-permute-done.1.dn_ref), custom_call_target="tpu_custom_call" | custom-call | tf_op jit(solution)/shard_map/pallas_call | solution.py:307
  28.0 3.9 %collective-permute-start.2 = (f32[208,128]{1,0:T(8,128)}, f32[208,128]{1,0:T(8,128)S(1)}, u32[]{:S(2)}, u32[]{:S(2)}) collective-permute-start(f32[208,128]{1,0:T(8,128)} %get-tuple-element.12), channel_id=1, source_target_pairs={{0,1},{1,2},{2,3},{3,4},{4,5},{5,6},{6,7},{8,9},{9,10},{10,11},{11... | collective-permute-start | bytes 319496 | tf_op jit(solution)/shard_map/ppermute | solution.py:332
  31.9 3.4 %collective-permute-start.3 = (f32[208,128]{1,0:T(8,128)}, f32[208,128]{1,0:T(8,128)S(1)}, u32[]{:S(2)}, u32[]{:S(2)}) collective-permute-start(f32[208,128]{1,0:T(8,128)} %get-tuple-element.13), channel_id=1, source_target_pairs={{1,0},{2,1},{3,2},{4,3},{5,4},{6,5},{7,6},{9,8},{10,9},{11,10},{12... | collective-permute-start | bytes 319496 | tf_op jit(solution)/shard_map/ppermute | solution.py:332
  35.3 0.7 pad_add_fusion.base_ref
  36.0 0.0 collective-permute-done.2.lf_ref
  36.0 0.0 copy-start.8
  36.0 2.2 %collective-permute-done.3.rt_ref = f32[208,128]{1,0:T(8,128)S(1)} collective-permute-done((f32[208,128]{1,0:T(8,128)}, f32[208,128]{1,0:T(8,128)S(1)}, u32[]{:S(2)}, u32[]{:S(2)}) %collective-permute-start.3) | collective-permute-done | bytes 106528 | tf_op jit(solution)/shard_map/ppermute | solution.py:332
  38.2 0.0 copy-start.9
  38.2 0.0 copy-done.8
  38.2 0.6 copy-done.9
  38.8 11.3 %shard_map.106 = (f32[8,296,128]{2,1,0:T(8,128)}, f32[192,128]{1,0:T(8,128)}) custom-call(s32[2]{0:T(128)} %pad_add_fusion.base_ref, f32[304,128]{1,0:T(8,128)} %get-tuple-element.10.own_ref, f32[304,128]{1,0:T(8,128)} %collective-permute-done.up_ref, f32[304,128]{1,0:T(8,128)} %collective-permute-done.1.dn_ref, f32[208,128]{1,0:T(8,128)} %copy-done.8, ...), custom_call_target="tpu_custom_call" | custom-call | tf_op jit(solution)/shard_map/pallas_call | solution.py:307
  50.2 21.2 %all_to_all.20.in_ref = f32[8,296,128]{2,1,0:T(8,128)} all-to-all(f32[8,296,128]{2,1,0:T(8,128)} %get-tuple-element.14), channel_id=1, replica_groups=mesh['gx'=64,'gy'=8] {'gy'}, dimensions={0} | all-to-all | bytes 2424832 | tf_op jit(solution)/shard_map/all_to_all | solution.py:389
  71.3 2.1 %shard_map.107 = f32[512,128]{1,0:T(8,128)} custom-call(f32[8,296,128]{2,1,0:T(8,128)} %all_to_all.20.in_ref), custom_call_target="tpu_custom_call" | custom-call | tf_op jit(solution)/shard_map/pallas_call | solution.py:307
  73.4 30.6 %all_to_all.21 = f32[64,8,128]{2,1,0:T(8,128)} all-to-all(f32[64,8,128]{2,1,0:T(8,128)} %bitcast.21), channel_id=1, replica_groups=mesh['gx'=64,'gy'=8] {'gx'}, dimensions={0} | all-to-all | bytes 524288 | tf_op jit(solution)/shard_map/all_to_all | solution.py:391
  104.0 2.0 %shard_map.108 = (f32[512,128]{1,0:T(8,128)}, f32[192,128]{1,0:T(8,128)}) custom-call(f32[512,128]{1,0:T(8,128)} %bitcast.20, f32[192,128]{1,0:T(8,128)} %b_ref.3, f32[192,128]{1,0:T(8,128)} %get-tuple-element.15.u1_ref), custom_call_target="tpu_custom_call" | custom-call | tf_op jit(solution)/shard_map/pallas_call | solution.py:307
  106.0 18.3 %all_to_all.22 = f32[64,8,128]{2,1,0:T(8,128)} all-to-all(f32[64,8,128]{2,1,0:T(8,128)} %bitcast.23), channel_id=1, replica_groups=mesh['gx'=64,'gy'=8] {'gx'}, dimensions={0} | all-to-all | bytes 524288 | tf_op jit(solution)/shard_map/all_to_all | solution.py:395
  124.3 1.9 %shard_map.109 = f32[8,96,192]{2,1,0:T(8,128)} custom-call(f32[512,128]{1,0:T(8,128)} %bitcast.22), custom_call_target="tpu_custom_call" | custom-call | tf_op jit(solution)/shard_map/pallas_call | solution.py:307
  126.2 19.8 %all_to_all.23 = f32[8,96,192]{2,1,0:T(8,128)S(1)} all-to-all(f32[8,96,192]{2,1,0:T(8,128)} %shard_map.109), channel_id=1, replica_groups=mesh['gx'=64,'gy'=8] {'gy'}, dimensions={0} | all-to-all | bytes 1179648 | tf_op jit(solution)/shard_map/all_to_all | solution.py:397
  145.9 0.9 copy.22
  (1 shorter events, 0.0 us)
Async XLA Ops:
  0.6 8.9 %copy-start.4 = (f32[10,96,96]{2,1,0:T(8,128)S(1)}, f32[10,96,96]{2,1,0:T(8,128)}, u32[]{:S(2)}) copy-start(f32[10,96,96]{2,1,0:T(8,128)} %param.15) | copy-start | bytes 1105924
  0.6 8.9 %copy-start.6 = (f32[10,96,96]{2,1,0:T(8,128)S(1)}, f32[10,96,96]{2,1,0:T(8,128)}, u32[]{:S(2)}) copy-start(f32[10,96,96]{2,1,0:T(8,128)} %param.14) | copy-start | bytes 1105924
  2.5 23.4 %collective-permute-start = (f32[304,128]{1,0:T(8,128)}, f32[304,128]{1,0:T(8,128)}, u32[]{:S(2)}, u32[]{:S(2)}) collective-permute-start(f32[304,128]{1,0:T(8,128)} %get-tuple-element.10.own_ref), channel_id=1, source_target_pairs={{0,8},{8,16},{16,24},{24,32},{32,40},{40,48},{48,56},{56,64},{64,7... | collective-permute-start | bytes 466952 | tf_op jit(solution)/shard_map/ppermute | solution.py:332
  7.2 18.7 %collective-permute-start.1 = (f32[304,128]{1,0:T(8,128)}, f32[304,128]{1,0:T(8,128)}, u32[]{:S(2)}, u32[]{:S(2)}) collective-permute-start(f32[304,128]{1,0:T(8,128)} %get-tuple-element.11), channel_id=1, source_target_pairs={{8,0},{16,8},{24,16},{32,24},{40,32},{48,40},{56,48},{64,56},{72,6... | collective-permute-start | bytes 466952 | tf_op jit(solution)/shard_map/ppermute | solution.py:332
  18.9 1.3 copy-start.5
  18.9 1.3 copy-start.7
  20.2 1.4 copy-start
  20.2 1.4 copy-start.1
  20.2 1.8 %copy-start.2 = (bf16[192,1920]{1,0:T(8,128)(2,1)S(1)}, bf16[192,1920]{1,0:T(8,128)(2,1)}, u32[]{:S(2)}) copy-start(bf16[192,1920]{1,0:T(8,128)(2,1)} %get-tuple-element.22) | copy-start | bytes 2211844
  22.0 3.0 %copy-start.3 = (f32[192,768]{1,0:T(8,128)S(1)}, f32[192,768]{1,0:T(8,128)}, u32[]{:S(2)}) copy-start(f32[192,768]{1,0:T(8,128)} %copy.20) | copy-start | bytes 1769476
  28.0 8.0 %collective-permute-start.2 = (f32[208,128]{1,0:T(8,128)}, f32[208,128]{1,0:T(8,128)S(1)}, u32[]{:S(2)}, u32[]{:S(2)}) collective-permute-start(f32[208,128]{1,0:T(8,128)} %get-tuple-element.12), channel_id=1, source_target_pairs={{0,1},{1,2},{2,3},{3,4},{4,5},{5,6},{6,7},{8,9},{9,10},{10,11},{11... | collective-permute-start | bytes 319496 | tf_op jit(solution)/shard_map/ppermute | solution.py:332
  31.9 6.2 %collective-permute-start.3 = (f32[208,128]{1,0:T(8,128)}, f32[208,128]{1,0:T(8,128)S(1)}, u32[]{:S(2)}, u32[]{:S(2)}) collective-permute-start(f32[208,128]{1,0:T(8,128)} %get-tuple-element.13), channel_id=1, source_target_pairs={{1,0},{2,1},{3,2},{4,3},{5,4},{6,5},{7,6},{9,8},{10,9},{11,10},{12... | collective-permute-start | bytes 319496 | tf_op jit(solution)/shard_map/ppermute | solution.py:332
  36.0 2.2 %copy-start.8 = (f32[208,128]{1,0:T(8,128)}, f32[208,128]{1,0:T(8,128)S(1)}, u32[]{:S(2)}) copy-start(f32[208,128]{1,0:T(8,128)S(1)} %collective-permute-done.2.lf_ref) | copy-start | bytes 319492
  38.2 0.6 copy-start.9

commit v2 on v1

--- a/solution.py
+++ b/solution.py
@@ -15,11 +15,8 @@
 META = 16
 ROWS = W + META
 CHUNK = 296
-VMEM = 56 * 1024 * 1024
-
-
-def params():
-    return pltpu.CompilerParams(vmem_limit_bytes=VMEM)
+PART = 1024
+MIB = 1024 * 1024
 
 
 def split(x):
@@ -94,6 +91,34 @@
     m = slice(W, ROWS)
     meta_ud = jnp.where(first, dn_ref[m, :], up_ref[m, :])
     part(m, (up_ref[m, :], own_ref[m, :], dn_ref[m, :], own_ref[m, :], meta_ud))
+
+
+def weight_kernel(tr_ref, ti_ref, lr_ref, li_ref, tw_ref, lw_ref, fw_ref):
+    def turned(ref):
+        n = ref.shape[0]
+        fill = -n * HALF % PT
+        side = jnp.concatenate([ref[...].reshape(n * HALF, HALF), jnp.zeros((n * HALF, 32), F32)], axis=1)
+        if fill:
+            side = jnp.concatenate([side, jnp.zeros((fill, PT), F32)], axis=0)
+        return split(jnp.transpose(side)[0:HALF, :])
+
+    def beside(ref):
+        n = ref.shape[0]
+        return split(
+            jnp.concatenate([ref[s] for s in range(n)] + [jnp.zeros((HALF, -n * HALF % PT), F32)], axis=1)
+        )
+
+    def store(ref, real, imag, sign):
+        width = real[0].shape[1]
+        for at, re, im in zip((0, W), real, imag):
+            ref[at : at + HALF, 0:width] = re
+            ref[at : at + HALF, width:] = im if sign > 0 else -im
+            ref[at + HALF : at + W, 0:width] = -im if sign > 0 else im
+            ref[at + HALF : at + W, width:] = re
+
+    store(tw_ref, turned(tr_ref), turned(ti_ref), 1)
+    store(lw_ref, turned(lr_ref), turned(li_ref), 1)
+    store(fw_ref, beside(lr_ref), beside(li_ref), -1)
 
 
 def target_ids(base, row_stride):
@@ -161,17 +186,20 @@
             kind = meta[SLOTS : SLOTS + 1, :]
             his.append([jnp.where(kind == float(k), hi, jnp.zeros_like(hi)) for k in range(KINDS)])
             los.append([jnp.where(kind == float(k), lo, jnp.zeros_like(lo)) for k in range(KINDS)])
-        hi = jnp.concatenate(
-            [jnp.concatenate([h[k] for h in his], axis=1) for k in range(KINDS)], axis=0
-        )
-        lo = jnp.concatenate(
-            [jnp.concatenate([x[k] for x in los], axis=1) for k in range(KINDS)], axis=0
-        )
+        def by_part(pieces):
+            whole = [jnp.concatenate([p[k] for p in pieces], axis=1) for k in range(KINDS)]
+            return jnp.concatenate([w[0:HALF] for w in whole] + [w[HALF:W] for w in whole], axis=0)
+
+        hi, lo = by_part(his), by_part(los)
         s_hi, s_lo = split(product(tw_ref, hi, lo))
         return jnp.concatenate([s_hi, s_lo], axis=0)
 
     def one_hot(at, meta, s):
         return jnp.where(at == meta[s : s + 1, :], 1.0, 0.0).astype(BF16)
+
+    for ref in (ghi_ref, glo_ref):
+        for at in (SLOTS * HALF, PART + SLOTS * HALF):
+            ref[at : at + PART - SLOTS * HALF, :] = jnp.zeros((PART - SLOTS * HALF, 3 * PT), BF16)
 
     metas = (m_own, m_up, m_dn, m_b)
     stack = scaled_by_type((b, up_ref[0:W, :], dn_ref[0:W, :], x_lr), metas)
@@ -179,8 +207,9 @@
         pick = jnp.concatenate([one_hot(ids, meta, s) for meta in metas], axis=1)
         g = dot_nt(stack, pick)
         hi, lo = split(g[0:W] + g[W : 2 * W])
-        ghi_ref[s * W : (s + 1) * W, :] = hi
-        glo_ref[s * W : (s + 1) * W, :] = lo
+        for ref, part in ((ghi_ref, hi), (glo_ref, lo)):
+            ref[s * HALF : (s + 1) * HALF, :] = part[0:HALF]
+            ref[PART + s * HALF : PART + (s + 1) * HALF, :] = part[HALF:W]
     u1_all = product(lw_ref, ghi_ref[...], glo_ref[...])
     u1 = u1_all[:, 0:PT]
     u1_ref[...] = u1
@@ -198,9 +227,10 @@
         g = dot_nt(stack, pick)
         hi, lo = split(g[0:W] + g[W : 2 * W])
         for t in (0, 1):
-            rows = slice((s + t) * W, (s + t + 1) * W)
-            ghi_ref[rows, 0:PT] = hi[:, t * PT : (t + 1) * PT]
-            glo_ref[rows, 0:PT] = lo[:, t * PT : (t + 1) * PT]
+            at = (s + t) * HALF
+            for ref, part in ((ghi_ref, hi), (glo_ref, lo)):
+                ref[at : at + HALF, 0:PT] = part[0:HALF, t * PT : (t + 1) * PT]
+                ref[PART + at : PART + at + HALF, 0:PT] = part[HALF:W, t * PT : (t + 1) * PT]
     u2 = product(lw_ref, ghi_ref[:, 0:PT], glo_ref[:, 0:PT])
 
     fc_ud = unpack_fc(up_ref[ROWS : ROWS + HALF, :], dn_ref[ROWS : ROWS + HALF, :])
@@ -210,9 +240,12 @@
         pick = jnp.concatenate([one_hot(ids, m_own, s), one_hot(ids, m_own, s + 1)], axis=1)
         g = dot(stack, pick).astype(BF16)
         for t in (0, 1):
-            rows = slice((s + t) * W, (s + t + 1) * W)
-            ghi_ref[rows, PT : 2 * PT] = g[0:W, t * PT : (t + 1) * PT]
-            glo_ref[rows, PT : 2 * PT] = g[W : 2 * W, t * PT : (t + 1) * PT]
+            at = (s + t) * HALF
+            for ref, part in ((ghi_ref, g[0:W]), (glo_ref, g[W : 2 * W])):
+                ref[at : at + HALF, PT : 2 * PT] = part[0:HALF, t * PT : (t + 1) * PT]
+                ref[PART + at : PART + at + HALF, PT : 2 * PT] = part[
+                    HALF:W, t * PT : (t + 1) * PT
+                ]
     exc = inc_ref[...] + product(fw_ref, ghi_ref[:, PT : 2 * PT], glo_ref[:, PT : 2 * PT])
 
     e_hi, e_lo = split(jnp.concatenate([exc, jnp.zeros((64, PT), F32)], axis=0))
@@ -283,48 +316,40 @@
     w0 = (y0 - f10 * w1) / f00
     c1 = -w1 / pn
     c0 = w0 / beta - c1 * alpha
-    mixed = jnp.concatenate(
-        [c0 * total[0:3, :] + c1 * total[3:6, :], jnp.zeros((5, PT), F32)], axis=0
-    )
-    for i in range(64):
+    mixed = c0 * total[0:3, :] + c1 * total[3:6, :]
+    mixed = jnp.concatenate([mixed, jnp.zeros((1, PT), F32)] * 2, axis=0)
+    for i in range(32):
         out_ref[8 * i : 8 * i + 8, :] = mixed
     adj_ref[...] = c0 * b_ref[...] + c1 * u1_ref[...]
 
 
+def copies_kernel(in_ref, out_ref):
+    for j in range(3):
+        rows = in_ref[pl.ds(j, 48, 4), :]
+        for i in range(8):
+            out_ref[i, 48 * j : 48 * (j + 1), :] = rows
+
+
 def expand_kernel(in_ref, out_ref):
-    a0 = in_ref[pl.ds(0, 48, 8), :]
-    a1 = in_ref[pl.ds(1, 48, 8), :]
-    edge = in_ref[pl.ds(2, 48, 8), :]
-    turned = pltpu.roll(edge, 64, 1)
-    for i in range(8):
-        out_ref[i, 0:48, 0:PT] = a0
-        out_ref[i, 48:96, 0:PT] = a1
-        out_ref[i, 0:48, PT:W] = edge[:, 0:64]
-        out_ref[i, 48:96, PT:W] = turned[:, 0:64]
-
-
-def call(kernel, shapes, *args, smem=0, **kw):
+    for k in range(KINDS):
+        for h in range(2):
+            block = in_ref[2 * k + h]
+            at = h * HALF
+            edge = block[96:144, :]
+            out_ref[k, at : at + HALF, 0:PT] = block[0:HALF, :]
+            out_ref[k, at : at + 48, PT:W] = edge[:, 0:64]
+            out_ref[k, at + 48 : at + HALF, PT:W] = pltpu.roll(edge, 64, 1)[:, 0:64]
+
+
+def call(kernel, shapes, *args, smem=0, mib=6, dtype=F32, **kw):
     return pl.pallas_call(
         kernel,
-        out_shape=[jax.ShapeDtypeStruct(s, F32) for s in shapes],
+        out_shape=[jax.ShapeDtypeStruct(s, dtype) for s in shapes],
         in_specs=[pl.BlockSpec(memory_space=pltpu.SMEM)] * smem
         + [pl.BlockSpec(memory_space=pltpu.VMEM)] * (len(args) - smem),
-        compiler_params=params(),
+        compiler_params=pltpu.CompilerParams(vmem_limit_bytes=mib * MIB),
         **kw,
     )(*args)
-
-
-def complex_blocks(real_part, imag_part):
-    upper_rows = jnp.concatenate([real_part, -imag_part], axis=2)
-    lower_rows = jnp.concatenate([imag_part, real_part], axis=2)
-    return jnp.concatenate([upper_rows, lower_rows], axis=1)
-
-
-def weight_pair(w):
-    n = w.shape[0]
-    side = jnp.swapaxes(w, 0, 1).reshape(W, n * W)
-    hi = lax.reduce_precision(side, 8, 7)
-    return jnp.concatenate([hi, side - hi], axis=0).astype(BF16)
 
 
 def shifted(block, axis, step):
@@ -363,11 +388,16 @@
     lf = shifted(to_hi, "gy", 1)
     rt = shifted(to_lo, "gy", -1)
 
-    tmats = complex_blocks(tmat_real, tmat_imag)
-    trans = complex_blocks(translation_real, translation_imaginary)
-    tw = weight_pair(jnp.swapaxes(tmats, 1, 2))
-    lw = weight_pair(jnp.swapaxes(trans, 1, 2))
-    fw = weight_pair(trans)
+    tw, lw, fw = call(
+        weight_kernel,
+        [(2 * W, KINDS * W), (2 * W, 2 * PART), (2 * W, 2 * PART)],
+        tmat_real,
+        tmat_imag,
+        translation_real,
+        translation_imaginary,
+        mib=16,
+        dtype=BF16,
+    )
 
     chunks, u1 = call(
         main_kernel,
@@ -384,17 +414,19 @@
         lw,
         fw,
         smem=1,
-        scratch_shapes=[pltpu.VMEM((SLOTS * W, 3 * PT), BF16)] * 2,
+        mib=24,
+        scratch_shapes=[pltpu.VMEM((2 * PART, 3 * PT), BF16)] * 2,
     )
     got = lax.all_to_all(chunks, "gy", 0, 0)
     (pieces,) = call(spread_kernel, [(512, PT)], got)
     got = lax.all_to_all(pieces.reshape(64, 8, PT), "gx", 0, 0)
     mixed, adjoint = call(
-        combine_kernel, [(512, PT), (W, PT)], got.reshape(512, PT), cost_grad, u1
-    )
-    got = lax.all_to_all(mixed.reshape(64, 8, PT), "gx", 0, 0)
-    (copies,) = call(expand_kernel, [(8, HALF, W)], got.reshape(512, PT))
-    sensitivity = lax.all_to_all(copies, "gy", 0, 0).reshape(KINDS, W, W)
+        combine_kernel, [(256, PT), (W, PT)], got.reshape(512, PT), cost_grad, u1
+    )
+    got = lax.all_to_all(mixed.reshape(64, 4, PT), "gx", 0, 0)
+    (copies,) = call(copies_kernel, [(8, 144, PT)], got.reshape(256, PT))
+    got = lax.all_to_all(copies, "gy", 0, 0)
+    (sensitivity,) = call(expand_kernel, [(KINDS, W, W)], got)
     return (adjoint, sensitivity)
 
 

time: 148 us -> 119 us (0.80)
  other arithmetic: 10.4 us -> 0.08 us
  Pallas kernels: 21.2 us -> 11.6 us
  blocking collectives: 89.8 us -> 82.1 us
  starting transfers between devices: 13.3 us -> 15.9 us
  local copies, waits for them, and re-layouts: 9.07 us -> 7.05 us
    pallas_call x6 -> x8, Pallas kernels: 21.2 us -> 11.6 us  [call(): pl.pallas_call(kernel, out_shape=[jax.ShapeDtypeStruct(s, dtype) for s in...]
    all_to_all x2, blocking collectives: 38 us -> 32.7 us  [the longest x1 17 us: body(): got = lax.all_to_all(mixed.reshape(64, 4, PT), 'gx', 0, 0)]
    unnamed x21 -> x22, local copies, waits for them, and re-layouts: 1.96 us -> 7.05 us
    reshape x3 -> x0, local copies, waits for them, and re-layouts: 4.16 us -> none  [weight_pair(): side = jnp.swapaxes(w, 0, 1).reshape(W, n * W)]
    concatenate x3 -> x0, other arithmetic: 4.09 us -> none  [the longest x2 3.81 us: weight_pair(): return jnp.concatenate([hi, side - hi], axis=0).astype(BF16)]
    transpose x1 -> x0, local copies, waits for them, and re-layouts: 2.96 us -> none  [weight_pair(): side = jnp.swapaxes(w, 0, 1).reshape(W, n * W)]
    another operation x3 -> x0, other arithmetic: 2.65 us -> none
    ppermute x4, starting transfers between devices: 13.3 us -> 15.9 us  [shifted(): lax.ppermute(block, axis, [(i, i + step) for i in range(n) if 0 <= i + st...]
  transfers between devices with their start and end apart: 4 -> 4, of which waited for: 1 -> 1; matrix products, arithmetic and copies ran while one was open for 12% -> 0% of each run, Pallas kernels for 0% -> 1%
where the time goes in v2:
time: 119 us; the launch traced here: 118 us
  blocking collectives  82.1 us (69%)
  starting transfers between devices  15.9 us (13%)
  Pallas kernels  11.6 us (10%)
  local copies, waits for them, and re-layouts  7.05 us (6%)
    all_to_all x1, blocking collectives, body(): got = lax.all_to_all(pieces.reshape(64, 8, PT), 'gx', 0, 0)  29.1 us
    all_to_all x1, blocking collectives, body(): got = lax.all_to_all(chunks, 'gy', 0, 0)  20.4 us
    all_to_all x1, blocking collectives, body(): got = lax.all_to_all(mixed.reshape(64, 4, PT), 'gx', 0, 0)  17 us
    ppermute x4, starting transfers between devices, shifted(): lax.ppermute(block, axis, [(i, i + step) for i in range(n) if 0 <= i + st...  15.9 us
    all_to_all x1, blocking collectives, body(): got = lax.all_to_all(copies, 'gy', 0, 0)  15.7 us
    pallas_call x8, Pallas kernels, call(): pl.pallas_call(kernel, out_shape=[jax.ShapeDtypeStruct(s, dtype) for s in...  11.6 us
    unnamed x22, local copies, waits for them, and re-layouts  7.05 us
  transfers between devices with their start and end apart: 4, of which 1 were waited for; matrix products, arithmetic and copies ran while one was open for 0% of the time, Pallas kernels for 1%

profile of v2, /device:TPU:1, one launch (start us, length us, event | category | flops | bytes accessed | tf_op | source)
XLA Modules:
  0.0 118.4 jit_solution(10263658351373177991)
XLA Ops:
  0.6 0.0 copy-start
  0.6 0.9 copy-done
  1.5 0.0 copy-start.4
  1.5 0.9 copy-done.4
  2.4 0.0 copy-start.9
  2.4 0.7 copy-done.9
  3.1 0.0 copy-start.10
  3.1 0.7 copy-done.10
  3.8 0.0 copy-start.1
  3.8 0.0 copy-start.8
  3.8 0.1 shard_map.104
  3.9 1.3 %collective-permute-start.1 = (f32[304,128]{1,0:T(8,128)S(1)}, f32[304,128]{1,0:T(8,128)S(1)}, u32[]{:S(2)}, u32[]{:S(2)}) collective-permute-start(f32[304,128]{1,0:T(8,128)S(1)} %get-tuple-element.14), channel_id=1, source_target_pairs={{8,0},{16,8},{24,16},{32,24},{40,32},{48,40},{56,48},{64,56},{72,6... | collective-permute-start | bytes 466952 | tf_op jit(solution)/shard_map/ppermute | solution.py:357
  5.2 4.7 %collective-permute-start = (f32[304,128]{1,0:T(8,128)S(1)}, f32[304,128]{1,0:T(8,128)S(1)}, u32[]{:S(2)}, u32[]{:S(2)}) collective-permute-start(f32[304,128]{1,0:T(8,128)S(1)} %get-tuple-element.13.own_ref), channel_id=1, source_target_pairs={{0,8},{8,16},{16,24},{24,32},{32,40},{40,48},{48,56},{56,64},{64,7... | collective-permute-start | bytes 466952 | tf_op jit(solution)/shard_map/ppermute | solution.py:357
  9.8 0.0 copy-start.2
  9.9 1.0 copy-done.2
  10.9 0.0 copy-start.3
  10.9 1.0 copy-done.3
  11.9 0.0 copy-start.6
  11.9 0.9 copy-done.6
  12.8 0.0 copy-start.7
  12.8 0.9 copy-done.7
  13.8 0.7 shard_map.106
  14.5 0.0 collective-permute-done.1.dn_ref
  14.5 0.0 collective-permute-done.up_ref
  14.5 0.0 copy-done.1
  14.5 0.3 shard_map.105
  14.9 4.4 %collective-permute-start.2 = (f32[208,128]{1,0:T(8,128)S(1)}, f32[208,128]{1,0:T(8,128)S(1)}, u32[]{:S(2)}, u32[]{:S(2)}) collective-permute-start(f32[208,128]{1,0:T(8,128)S(1)} %get-tuple-element.15), channel_id=1, source_target_pairs={{0,1},{1,2},{2,3},{3,4},{4,5},{5,6},{6,7},{8,9},{9,10},{10,11},{11... | collective-permute-start | bytes 319496 | tf_op jit(solution)/shard_map/ppermute | solution.py:357
  19.3 5.6 %collective-permute-start.3 = (f32[208,128]{1,0:T(8,128)S(1)}, f32[208,128]{1,0:T(8,128)S(1)}, u32[]{:S(2)}, u32[]{:S(2)}) collective-permute-start(f32[208,128]{1,0:T(8,128)S(1)} %get-tuple-element.16), channel_id=1, source_target_pairs={{1,0},{2,1},{3,2},{4,3},{5,4},{6,5},{7,6},{9,8},{10,9},{11,10},{12... | collective-permute-start | bytes 319496 | tf_op jit(solution)/shard_map/ppermute | solution.py:357
  24.9 0.1 pad_add_fusion.base_ref
  24.9 0.0 collective-permute-done.2.lf_ref
  24.9 0.9 collective-permute-done.3.rt_ref
  25.8 0.0 copy-done.8
  25.8 8.5 %shard_map.107 = (f32[8,296,128]{2,1,0:T(8,128)S(1)}, f32[192,128]{1,0:T(8,128)S(1)}) custom-call(s32[2]{0:T(128)S(1)} %pad_add_fusion.base_ref, f32[304,128]{1,0:T(8,128)S(1)} %get-tuple-element.13.own_ref, f32[304,128]{1,0:T(8,128)S(1)} %collective-permute-done.up_ref, f32[304,128]{1,0:T(8,128)S(1)} %collective-permute-done.1.dn_ref, ...), custom_call_target="tpu_custom_call" | custom-call | tf_op jit(solution)/shard_map/pallas_call | solution.py:345
  34.3 20.4 %all_to_all.20.in_ref = f32[8,296,128]{2,1,0:T(8,128)S(1)} all-to-all(f32[8,296,128]{2,1,0:T(8,128)S(1)} %get-tuple-element.20), channel_id=1, replica_groups=mesh['gx'=64,'gy'=8] {'gy'}, dimensions={0} | all-to-all | bytes 2424832 | tf_op jit(solution)/shard_map/all_to_all | solution.py:420
  54.7 0.0 copy-start.5
  54.7 0.1 shard_map.108
  54.8 29.1 %all_to_all.21 = f32[64,8,128]{2,1,0:T(8,128)S(1)} all-to-all(f32[64,8,128]{2,1,0:T(8,128)S(1)} %bitcast.7), channel_id=1, replica_groups=mesh['gx'=64,'gy'=8] {'gx'}, dimensions={0} | all-to-all | bytes 524288 | tf_op jit(solution)/shard_map/all_to_all | solution.py:422
  83.9 0.0 copy-done.5
  83.9 0.9 shard_map.109
  84.7 17.0 %all_to_all.22 = f32[64,4,128]{2,1,0:T(4,128)S(1)} all-to-all(f32[64,4,128]{2,1,0:T(4,128)S(1)} %bitcast.9), channel_id=1, replica_groups=mesh['gx'=64,'gy'=8] {'gx'}, dimensions={0} | all-to-all | bytes 262144 | tf_op jit(solution)/shard_map/all_to_all | solution.py:426
  101.7 15.7 %all_to_all.23.in_ref = f32[8,144,128]{2,1,0:T(8,128)S(1)} all-to-all(f32[8,144,128]{2,1,0:T(8,128)S(1)} %shard_map.110), channel_id=1, replica_groups=mesh['gx'=64,'gy'=8] {'gy'}, dimensions={0} | all-to-all | bytes 1179648 | tf_op jit(solution)/shard_map/all_to_all | solution.py:428
  117.4 1.0 shard_map.111
  (1 shorter events, 0.0 us)
Async XLA Ops:
  0.6 0.9 copy-start
  1.5 0.9 copy-start.4
  2.4 0.7 copy-start.9
  3.1 0.7 copy-start.10
  3.8 10.8 %copy-start.1 = (f32[192,128]{1,0:T(8,128)S(1)}, f32[192,128]{1,0:T(8,128)}, u32[]{:S(2)}) copy-start(f32[192,128]{1,0:T(8,128)} %fc_ref.5) | copy-start | bytes 294916
  3.8 22.0 %copy-start.8 = (f32[192,128]{1,0:T(8,128)S(1)}, f32[192,128]{1,0:T(8,128)}, u32[]{:S(2)}) copy-start(f32[192,128]{1,0:T(8,128)} %inc_ref.1) | copy-start | bytes 294916
  3.9 10.7 %collective-permute-start.1 = (f32[304,128]{1,0:T(8,128)S(1)}, f32[304,128]{1,0:T(8,128)S(1)}, u32[]{:S(2)}, u32[]{:S(2)}) collective-permute-start(f32[304,128]{1,0:T(8,128)S(1)} %get-tuple-element.14), channel_id=1, source_target_pairs={{8,0},{16,8},{24,16},{32,24},{40,32},{48,40},{56,48},{64,56},{72,6... | collective-permute-start | bytes 466952 | tf_op jit(solution)/shard_map/ppermute | solution.py:357
  5.2 9.4 %collective-permute-start = (f32[304,128]{1,0:T(8,128)S(1)}, f32[304,128]{1,0:T(8,128)S(1)}, u32[]{:S(2)}, u32[]{:S(2)}) collective-permute-start(f32[304,128]{1,0:T(8,128)S(1)} %get-tuple-element.13.own_ref), channel_id=1, source_target_pairs={{0,8},{8,16},{16,24},{24,32},{32,40},{40,48},{48,56},{56,64},{64,7... | collective-permute-start | bytes 466952 | tf_op jit(solution)/shard_map/ppermute | solution.py:357
  9.8 1.0 copy-start.2
  10.9 1.0 copy-start.3
  11.9 0.9 copy-start.6
  12.8 0.9 copy-start.7
  14.9 10.1 %collective-permute-start.2 = (f32[208,128]{1,0:T(8,128)S(1)}, f32[208,128]{1,0:T(8,128)S(1)}, u32[]{:S(2)}, u32[]{:S(2)}) collective-permute-start(f32[208,128]{1,0:T(8,128)S(1)} %get-tuple-element.15), channel_id=1, source_target_pairs={{0,1},{1,2},{2,3},{3,4},{4,5},{5,6},{6,7},{8,9},{9,10},{10,11},{11... | collective-permute-start | bytes 319496 | tf_op jit(solution)/shard_map/ppermute | solution.py:357
  19.3 6.5 %collective-permute-start.3 = (f32[208,128]{1,0:T(8,128)S(1)}, f32[208,128]{1,0:T(8,128)S(1)}, u32[]{:S(2)}, u32[]{:S(2)}) collective-permute-start(f32[208,128]{1,0:T(8,128)S(1)} %get-tuple-element.16), channel_id=1, source_target_pairs={{1,0},{2,1},{3,2},{4,3},{5,4},{6,5},{7,6},{9,8},{10,9},{11,10},{12... | collective-permute-start | bytes 319496 | tf_op jit(solution)/shard_map/ppermute | solution.py:357
  54.7 29.2 %copy-start.5 = (f32[192,128]{1,0:T(8,128)S(1)}, f32[192,128]{1,0:T(8,128)}, u32[]{:S(2)}) copy-start(f32[192,128]{1,0:T(8,128)} %b_ref.3) | copy-start | bytes 294916

commit v3 on v2

--- a/solution.py
+++ b/solution.py
@@ -36,7 +36,21 @@
     return lax.broadcasted_iota(jnp.int32, (rows, PT), 1)
 
 
-def pack_wide_kernel(fc_ref, b_ref, nb_ref, pt_ref, up_ref, dn_ref):
+def fetch(sources, targets, sems):
+    copies = [
+        pltpu.make_async_copy(src, dst, sems.at[i])
+        for i, (src, dst) in enumerate(zip(sources, targets))
+    ]
+    for copy in copies:
+        copy.start()
+    for copy in copies:
+        copy.wait()
+
+
+def pack_wide_kernel(*refs):
+    up_ref, dn_ref = refs[4:6]
+    fc_ref, b_ref, nb_ref, pt_ref = refs[6:10]
+    fetch(refs[0:4], refs[6:10], refs[10])
     meta = jnp.concatenate(
         [
             (nb_ref[...] + 1).astype(F32),
@@ -93,7 +107,11 @@
     part(m, (up_ref[m, :], own_ref[m, :], dn_ref[m, :], own_ref[m, :], meta_ud))
 
 
-def weight_kernel(tr_ref, ti_ref, lr_ref, li_ref, tw_ref, lw_ref, fw_ref):
+def weight_kernel(*refs):
+    tw_ref, lw_ref, fw_ref = refs[4:7]
+    tr_ref, ti_ref, lr_ref, li_ref = refs[7:11]
+    fetch(refs[0:4], refs[7:11], refs[11])
+
     def turned(ref):
         n = ref.shape[0]
         fill = -n * HALF % PT
@@ -154,8 +172,7 @@
     tw_ref,
     lw_ref,
     fw_ref,
-    chunk_ref,
-    u1_ref,
+    vec_ref,
     ghi_ref,
     glo_ref,
 ):
@@ -212,7 +229,8 @@
             ref[PART + s * HALF : PART + (s + 1) * HALF, :] = part[HALF:W]
     u1_all = product(lw_ref, ghi_ref[...], glo_ref[...])
     u1 = u1_all[:, 0:PT]
-    u1_ref[...] = u1
+    vec_ref[0:W, :] = b
+    vec_ref[W : 2 * W, :] = u1
 
     metas = (m_own, m_ud, m_f)
     stack = scaled_by_type([u1_all[:, i * PT : (i + 1) * PT] for i in range(3)], metas)
@@ -248,11 +266,25 @@
                 ]
     exc = inc_ref[...] + product(fw_ref, ghi_ref[:, PT : 2 * PT], glo_ref[:, PT : 2 * PT])
 
-    e_hi, e_lo = split(jnp.concatenate([exc, jnp.zeros((64, PT), F32)], axis=0))
-    v_hi, v_lo = split(jnp.concatenate([b, u1], axis=0))
-    kind = m_own[SLOTS : SLOTS + 1, :]
-    for k in range(KINDS):
-        here = kind == float(k)
+    vec_ref[2 * W : 3 * W, :] = exc
+
+    lane, row = lanes(8), lax.broadcasted_iota(jnp.int32, (8, PT), 0)
+    gram = jnp.zeros((8, PT), F32)
+    for i, (p, q) in enumerate(((b, b), (b, u1), (u1, u1), (b, u2), (u1, u2), (u2, u2))):
+        gram = jnp.where(lane == i, jnp.sum(p * q), gram)
+    vec_ref[3 * W :, :] = jnp.where(row == 0, gram, m_own[SLOTS : SLOTS + 1, :])
+
+
+def outer_kernel(base_ref, own_ref, other_ref, chunk_ref):
+    def both(rows):
+        return jnp.concatenate([own_ref[rows, :], other_ref[rows, :]], axis=1)
+
+    exc = both(slice(2 * W, 3 * W))
+    e_hi, e_lo = split(jnp.concatenate([exc, jnp.zeros((64, 2 * PT), F32)], axis=0))
+    v_hi, v_lo = split(both(slice(0, 2 * W)))
+    kind = both(slice(3 * W + 1, 3 * W + 2))
+    for k in range(2):
+        here = kind == (2 * base_ref[2] + k).astype(F32)
         k_hi = jnp.where(here, v_hi, jnp.zeros_like(v_hi))
         k_lo = jnp.where(here, v_lo, jnp.zeros_like(v_lo))
         out = dot_nt(k_hi, e_hi) + dot_nt(k_lo, e_hi) + dot_nt(k_hi, e_lo)
@@ -264,18 +296,14 @@
                 chunk_ref[2 * k + h, at + 96 : at + 144, :] = block[0:48, PT:] + pltpu.roll(
                     block[48:96, PT:], 64, 1
                 )
-
-    lane = lanes(8)
-    gram = jnp.zeros((8, PT), F32)
-    for i, (p, q) in enumerate(((b, b), (b, u1), (u1, u1), (b, u2), (u1, u2), (u2, u2))):
-        gram = jnp.where(lane == i, jnp.sum(p * q), gram)
-    for g in range(8):
+    gram = own_ref[3 * W :, :] + other_ref[3 * W :, :]
+    for g in range(4):
         chunk_ref[g, 288:296, :] = gram
 
 
 def spread_kernel(in_ref, out_ref):
     total = in_ref[0]
-    for i in range(1, 8):
+    for i in range(1, 4):
         total = total + in_ref[i]
     out_ref[...] = jnp.zeros_like(out_ref)
     for which in range(2):
@@ -285,7 +313,7 @@
     out_ref[pl.ds(6, 64, 8), :] = jnp.broadcast_to(total[288:289, :], (64, PT))
 
 
-def combine_kernel(in_ref, b_ref, u1_ref, out_ref, adj_ref):
+def combine_kernel(in_ref, vec_ref, out_ref, adj_ref):
     total = jnp.sum(in_ref[...].reshape(64, 8, PT), axis=0)
     lane = lanes(1)
 
@@ -320,33 +348,38 @@
     mixed = jnp.concatenate([mixed, jnp.zeros((1, PT), F32)] * 2, axis=0)
     for i in range(32):
         out_ref[8 * i : 8 * i + 8, :] = mixed
-    adj_ref[...] = c0 * b_ref[...] + c1 * u1_ref[...]
+    adj_ref[...] = c0 * vec_ref[0:W, :] + c1 * vec_ref[W : 2 * W, :]
 
 
 def copies_kernel(in_ref, out_ref):
     for j in range(3):
         rows = in_ref[pl.ds(j, 48, 4), :]
-        for i in range(8):
+        for i in range(4):
             out_ref[i, 48 * j : 48 * (j + 1), :] = rows
 
 
-def expand_kernel(in_ref, out_ref):
-    for k in range(KINDS):
-        for h in range(2):
-            block = in_ref[2 * k + h]
-            at = h * HALF
-            edge = block[96:144, :]
-            out_ref[k, at : at + HALF, 0:PT] = block[0:HALF, :]
-            out_ref[k, at : at + 48, PT:W] = edge[:, 0:64]
-            out_ref[k, at + 48 : at + HALF, PT:W] = pltpu.roll(edge, 64, 1)[:, 0:64]
-
-
-def call(kernel, shapes, *args, smem=0, mib=6, dtype=F32, **kw):
+def expand_kernel(base_ref, own_ref, other_ref, out_ref):
+    core = base_ref[2]
+    for ref, first in ((own_ref, 2 * core), (other_ref, 2 - 2 * core)):
+        for k in range(2):
+            for h in range(2):
+                block = ref[2 * k + h]
+                at = h * HALF
+                edge = block[96:144, :]
+                out_ref[first + k, at : at + HALF, 0:PT] = block[0:HALF, :]
+                out_ref[first + k, at : at + 48, PT:W] = edge[:, 0:64]
+                out_ref[first + k, at + 48 : at + HALF, PT:W] = pltpu.roll(edge, 64, 1)[:, 0:64]
+
+
+def call(kernel, shapes, *args, smem=0, mib=6, dtype=F32, fetched=False, **kw):
+    if fetched:
+        kw["scratch_shapes"] = [pltpu.VMEM(a.shape, a.dtype) for a in args]
+        kw["scratch_shapes"].append(pltpu.SemaphoreType.DMA((len(args),)))
     return pl.pallas_call(
         kernel,
         out_shape=[jax.ShapeDtypeStruct(s, dtype) for s in shapes],
         in_specs=[pl.BlockSpec(memory_space=pltpu.SMEM)] * smem
-        + [pl.BlockSpec(memory_space=pltpu.VMEM)] * (len(args) - smem),
+        + [pl.BlockSpec(memory_space=pltpu.HBM if fetched else pltpu.VMEM)] * (len(args) - smem),
         compiler_params=pltpu.CompilerParams(vmem_limit_bytes=mib * MIB),
         **kw,
     )(*args)
@@ -370,7 +403,8 @@
 ):
     n_short = lax.axis_size("gy")
     tile = lax.axis_index("gx") * n_short + lax.axis_index("gy")
-    base = jnp.stack([tile * PT, jnp.int32(n_short * PT)]).astype(jnp.int32)
+    core = lax.axis_index("gy") % 2
+    base = jnp.stack([tile * PT, jnp.int32(n_short * PT), core]).astype(jnp.int32)
 
     to_up, to_dn = call(
         pack_wide_kernel,
@@ -379,6 +413,8 @@
         cost_grad,
         neighbours,
         particle_type.reshape(1, PT),
+        mib=60,
+        fetched=True,
     )
     up = shifted(to_up, "gx", 1)
     dn = shifted(to_dn, "gx", -1)
@@ -397,11 +433,12 @@
         translation_imaginary,
         mib=16,
         dtype=BF16,
-    )
-
-    chunks, u1 = call(
+        fetched=True,
+    )
+
+    (vectors,) = call(
         main_kernel,
-        [(8, CHUNK, PT), (W, PT)],
+        [(3 * W + 8, PT)],
         base,
         to_up,
         up,
@@ -417,16 +454,19 @@
         mib=24,
         scratch_shapes=[pltpu.VMEM((2 * PART, 3 * PT), BF16)] * 2,
     )
-    got = lax.all_to_all(chunks, "gy", 0, 0)
+    pairs = [(i, i ^ 1) for i in range(n_short)]
+    lines = [list(range(c, n_short, 2)) for c in range(2)]
+    partner = lax.ppermute(vectors, "gy", pairs)
+    (chunks,) = call(outer_kernel, [(4, CHUNK, PT)], base, vectors, partner, smem=1)
+    got = lax.all_to_all(chunks, "gy", 0, 0, axis_index_groups=lines)
     (pieces,) = call(spread_kernel, [(512, PT)], got)
     got = lax.all_to_all(pieces.reshape(64, 8, PT), "gx", 0, 0)
-    mixed, adjoint = call(
-        combine_kernel, [(256, PT), (W, PT)], got.reshape(512, PT), cost_grad, u1
-    )
+    mixed, adjoint = call(combine_kernel, [(256, PT), (W, PT)], got.reshape(512, PT), vectors)
     got = lax.all_to_all(mixed.reshape(64, 4, PT), "gx", 0, 0)
-    (copies,) = call(copies_kernel, [(8, 144, PT)], got.reshape(256, PT))
-    got = lax.all_to_all(copies, "gy", 0, 0)
-    (sensitivity,) = call(expand_kernel, [(KINDS, W, W)], got)
+    (copies,) = call(copies_kernel, [(4, 144, PT)], got.reshape(256, PT))
+    half = lax.all_to_all(copies, "gy", 0, 0, axis_index_groups=lines)
+    other = lax.ppermute(half, "gy", pairs)
+    (sensitivity,) = call(expand_kernel, [(KINDS, W, W)], base, half, other, smem=1)
     return (adjoint, sensitivity)
 
 

time: 119 us -> 116 us (0.975)
  blocking collectives: 82.1 us -> 66 us
  starting transfers between devices: 15.9 us -> 25.1 us
  Pallas kernels: 11.6 us -> 15.3 us
  waiting for transfers between devices: 0.86 us -> 3.26 us
  local copies, waits for them, and re-layouts: 7.05 us -> 4.83 us
    all_to_all x2, blocking collectives: 36.1 us -> 20.8 us  [the longest x1 12.8 us: body(): got = lax.all_to_all(chunks, 'gy', 0, 0, axis_index_groups=lines)]
    ppermute x0 -> x2, starting transfers between devices: none -> 9 us  [the longest x1 6.73 us: body(): other = lax.ppermute(half, 'gy', pairs)]
    pallas_call x8 -> x9, Pallas kernels: 11.6 us -> 15.3 us  [call(): pl.pallas_call(kernel, out_shape=[jax.ShapeDtypeStruct(s, dtype) for s in...]
    ppermute x0 -> x2, waiting for transfers between devices: none -> 2.4 us  [the longest x1 1.21 us: body(): partner = lax.ppermute(vectors, 'gy', pairs)]
    unnamed x22 -> x16, local copies, waits for them, and re-layouts: 7.05 us -> 4.83 us
  transfers between devices with their start and end apart: 4 -> 6, of which waited for: 1 -> 3; matrix products, arithmetic and copies ran while one was open for 0% -> 0% of each run, Pallas kernels for 1% -> 2%
where the time goes in v3:
time: 116 us; the launch traced here: 115 us
  blocking collectives  66 us (57%)
  starting transfers between devices  25.1 us (22%)
  Pallas kernels  15.3 us (13%)
  local copies, waits for them, and re-layouts  4.83 us (4%)
  waiting for transfers between devices  3.26 us (3%)
    all_to_all x1, blocking collectives, body(): got = lax.all_to_all(pieces.reshape(64, 8, PT), 'gx', 0, 0)  28.6 us
    all_to_all x1, blocking collectives, body(): got = lax.all_to_all(mixed.reshape(64, 4, PT), 'gx', 0, 0)  16.5 us
    ppermute x4, starting transfers between devices, shifted(): lax.ppermute(block, axis, [(i, i + step) for i in range(n) if 0 <= i + st...  16.1 us
    pallas_call x9, Pallas kernels, call(): pl.pallas_call(kernel, out_shape=[jax.ShapeDtypeStruct(s, dtype) for s in...  15.3 us
    all_to_all x1, blocking collectives, body(): got = lax.all_to_all(chunks, 'gy', 0, 0, axis_index_groups=lines)  12.8 us
    all_to_all x1, blocking collectives, body(): half = lax.all_to_all(copies, 'gy', 0, 0, axis_index_groups=lines)  8.07 us
    ppermute x1, starting transfers between devices, body(): other = lax.ppermute(half, 'gy', pairs)  6.73 us
    unnamed x16, local copies, waits for them, and re-layouts  4.83 us
  transfers between devices with their start and end apart: 6, of which 3 were waited for; matrix products, arithmetic and copies ran while one was open for 0% of the time, Pallas kernels for 2%

profile of v3, /device:TPU:1, one launch (start us, length us, event | category | flops | bytes accessed | tf_op | source)
XLA Modules:
  0.0 115.3 jit_solution(9818748163430215224)
XLA Ops:
  0.6 0.0 copy-start
  0.6 0.0 copy-start.7
  0.7 1.8 %shard_map.104 = (f32[304,128]{1,0:T(8,128)}, f32[304,128]{1,0:T(8,128)}) custom-call(f32[192,128]{1,0:T(8,128)} %fc_ref.3, f32[192,128]{1,0:T(8,128)} %refs_1_.2, s32[10,128]{1,0:T(8,128)} %refs_2_.2, s32[1,128]{1,0:T(1,128)} %bitcast.11), custom_call_target="tpu_custom_call" | custom-call | tf_op jit(solution)/shard_map/pallas_call | solution.py:378
  2.5 0.0 copy-start.2
  2.5 1.4 %collective-permute-start.1 = (f32[304,128]{1,0:T(8,128)}, f32[304,128]{1,0:T(8,128)S(1)}, u32[]{:S(2)}, u32[]{:S(2)}) collective-permute-start(f32[304,128]{1,0:T(8,128)} %get-tuple-element.12), channel_id=1, source_target_pairs={{8,0},{16,8},{24,16},{32,24},{40,32},{48,40},{56,48},{64,56},{72,6... | collective-permute-start | bytes 466952 | tf_op jit(solution)/shard_map/ppermute | solution.py:390
  3.9 4.7 %collective-permute-start = (f32[304,128]{1,0:T(8,128)}, f32[304,128]{1,0:T(8,128)S(1)}, u32[]{:S(2)}, u32[]{:S(2)}) collective-permute-start(f32[304,128]{1,0:T(8,128)} %get-tuple-element.11.own_ref), channel_id=1, source_target_pairs={{0,8},{8,16},{16,24},{24,32},{32,40},{40,48},{48,56},{56,64},{64,7... | collective-permute-start | bytes 466952 | tf_op jit(solution)/shard_map/ppermute | solution.py:390
  8.6 0.0 copy-start.3
  8.6 1.0 copy-done.3
  9.6 0.0 copy-start.4
  9.6 1.0 copy-done.4
  10.7 0.0 copy-start.5
  10.7 0.9 copy-done.5
  11.6 0.0 copy-start.6
  11.6 0.9 copy-done.6
  12.5 1.9 %shard_map.106 = (bf16[384,768]{1,0:T(8,128)(2,1)S(1)}, bf16[384,2048]{1,0:T(8,128)(2,1)S(1)}, bf16[384,2048]{1,0:T(8,128)(2,1)S(1)}) custom-call(f32[4,96,96]{2,1,0:T(8,128)S(1)} %copy-done.5, f32[4,96,96]{2,1,0:T(8,128)S(1)} %copy-done.6, f32[10,96,96]{2,1,0:T(8,128)S(1)} %copy-done.3, f32[10,96,96]{2,1,0:T(8,128)S(1)} %copy-done.4), custom_call_target="tpu_custom_call" | custom-call | tf_op jit(solution)/shard_map/pallas_call | solution.py:378
  14.4 0.0 collective-permute-done.1.dn_ref
  14.4 0.0 collective-permute-done.up_ref
  14.4 0.0 copy-done
  14.4 0.0 copy-start.1
  14.5 0.9 copy-done.1
  15.4 0.3 shard_map.105
  15.7 4.4 %collective-permute-start.2 = (f32[208,128]{1,0:T(8,128)S(1)}, f32[208,128]{1,0:T(8,128)S(1)}, u32[]{:S(2)}, u32[]{:S(2)}) collective-permute-start(f32[208,128]{1,0:T(8,128)S(1)} %get-tuple-element.13), channel_id=1, source_target_pairs={{0,1},{1,2},{2,3},{3,4},{4,5},{5,6},{6,7},{8,9},{9,10},{10,11},{11... | collective-permute-start | bytes 319496 | tf_op jit(solution)/shard_map/ppermute | solution.py:390
  20.1 5.6 %collective-permute-start.3 = (f32[208,128]{1,0:T(8,128)S(1)}, f32[208,128]{1,0:T(8,128)S(1)}, u32[]{:S(2)}, u32[]{:S(2)}) collective-permute-start(f32[208,128]{1,0:T(8,128)S(1)} %get-tuple-element.14), channel_id=1, source_target_pairs={{1,0},{2,1},{3,2},{4,3},{5,4},{6,5},{7,6},{9,8},{10,9},{11,10},{12... | collective-permute-start | bytes 319496 | tf_op jit(solution)/shard_map/ppermute | solution.py:390
  25.7 0.1 pad_add_fusion.base_ref
  25.7 0.0 collective-permute-done.2.lf_ref
  25.7 0.9 collective-permute-done.3.rt_ref
  26.6 0.0 copy-done.7
  26.6 0.0 copy-done.2
  26.6 7.7 %shard_map.107.own_ref.vec_ref = f32[584,128]{1,0:T(8,128)S(1)} custom-call(s32[3]{0:T(128)S(1)} %pad_add_fusion.base_ref, f32[304,128]{1,0:T(8,128)S(1)} %copy-done.2, f32[304,128]{1,0:T(8,128)S(1)} %collective-permute-done.up_ref, f32[304,128]{1,0:T(8,128)S(1)} %collective-permute-done.1.dn_ref, f32[208,128]{1,0:T(8,128)S(1)} %collective-permute-done.2.lf_ref, ...), custom_call_target="tpu_custom_call" | custom-call | tf_op jit(solution)/shard_map/pallas_call | solution.py:378
  34.3 2.3 %collective-permute-start.4 = (f32[584,128]{1,0:T(8,128)S(1)}, f32[584,128]{1,0:T(8,128)S(1)}, u32[]{:S(2)}, u32[]{:S(2)}) collective-permute-start(f32[584,128]{1,0:T(8,128)S(1)} %shard_map.107.own_ref.vec_ref), channel_id=1, source_target_pairs={{0,1},{1,0},{2,3},{3,2},{4,5},{5,4},{6,7},{7,6},{8,9},{9,8},{10,11... | collective-permute-start | bytes 897032 | tf_op jit(solution)/shard_map/ppermute | solution.py:459
  36.6 1.2 %collective-permute-done.4.other_ref = f32[584,128]{1,0:T(8,128)S(1)} collective-permute-done((f32[584,128]{1,0:T(8,128)S(1)}, f32[584,128]{1,0:T(8,128)S(1)}, u32[]{:S(2)}, u32[]{:S(2)}) %collective-permute-start.4) | collective-permute-done | bytes 299040 | tf_op jit(solution)/shard_map/ppermute | solution.py:459
  37.8 1.1 shard_map.108
  38.9 12.8 %all_to_all.20.in_ref = f32[4,296,128]{2,1,0:T(8,128)S(1)} all-to-all(f32[4,296,128]{2,1,0:T(8,128)S(1)} %shard_map.108), channel_id=1, replica_groups={{0,2,4,6},{1,3,5,7},{8,10,12,14},{9,11,13,15},{16,18,20,22},{17,19,21,2..., dimensions={0} | all-to-all | bytes 1212416 | tf_op jit(solution)/shard_map/all_to_all | solution.py:461
  51.7 0.1 shard_map.109
  51.8 28.6 %all_to_all.21 = f32[64,8,128]{2,1,0:T(8,128)S(1)} all-to-all(f32[64,8,128]{2,1,0:T(8,128)S(1)} %bitcast.8), channel_id=1, replica_groups=mesh['gx'=64,'gy'=8] {'gx'}, dimensions={0} | all-to-all | bytes 524288 | tf_op jit(solution)/shard_map/all_to_all | solution.py:463
  80.4 0.9 shard_map.110
  81.3 16.5 %all_to_all.22 = f32[64,4,128]{2,1,0:T(4,128)S(1)} all-to-all(f32[64,4,128]{2,1,0:T(4,128)S(1)} %bitcast.10), channel_id=1, replica_groups=mesh['gx'=64,'gy'=8] {'gx'}, dimensions={0} | all-to-all | bytes 262144 | tf_op jit(solution)/shard_map/all_to_all | solution.py:465
  97.8 8.1 %all_to_all.23.own_ref = f32[4,144,128]{2,1,0:T(8,128)S(1)} all-to-all(f32[4,144,128]{2,1,0:T(8,128)S(1)} %shard_map.111), channel_id=1, replica_groups={{0,2,4,6},{1,3,5,7},{8,10,12,14},{9,11,13,15},{16,18,20,22},{17,19,21,2..., dimensions={0} | all-to-all | bytes 589824 | tf_op jit(solution)/shard_map/all_to_all | solution.py:467
  105.9 6.7 %collective-permute-start.5 = (f32[4,144,128]{2,1,0:T(8,128)S(1)}, f32[4,144,128]{2,1,0:T(8,128)S(1)}, u32[]{:S(2)}, u32[]{:S(2)}) collective-permute-start(f32[4,144,128]{2,1,0:T(8,128)S(1)} %all_to_all.23.own_ref), channel_id=1, source_target_pairs={{0,1},{1,0},{2,3},{3,2},{4,5},{5,4},{6,7},{7,6},{8,9},{9,8},{10,11... | collective-permute-start | bytes 884744 | tf_op jit(solution)/shard_map/ppermute | solution.py:468
  112.6 1.2 %collective-permute-done.5.other_ref = f32[4,144,128]{2,1,0:T(8,128)S(1)} collective-permute-done((f32[4,144,128]{2,1,0:T(8,128)S(1)}, f32[4,144,128]{2,1,0:T(8,128)S(1)}, u32[]{:S(2)}, u32[]{:S(2)}) %collective-permute-start.5) | collective-permute-done | bytes 294944 | tf_op jit(solution)/shard_map/ppermute | solution.py:468
  113.8 1.5 %shard_map.112 = f32[4,192,192]{2,1,0:T(8,128)} custom-call(s32[3]{0:T(128)S(1)} %pad_add_fusion.base_ref, f32[4,144,128]{2,1,0:T(8,128)S(1)} %all_to_all.23.own_ref, f32[4,144,128]{2,1,0:T(8,128)S(1)} %collective-permute-done.5.other_ref), custom_call_target="tpu_custom_call" | custom-call | tf_op jit(solution)/shard_map/pallas_call | solution.py:378
  (1 shorter events, 0.0 us)
Async XLA Ops:
  0.6 13.8 %copy-start = (f32[192,128]{1,0:T(8,128)S(1)}, f32[192,128]{1,0:T(8,128)}, u32[]{:S(2)}) copy-start(f32[192,128]{1,0:T(8,128)} %fc_ref.3) | copy-start | bytes 294916
  0.6 26.0 %copy-start.7 = (f32[192,128]{1,0:T(8,128)S(1)}, f32[192,128]{1,0:T(8,128)}, u32[]{:S(2)}) copy-start(f32[192,128]{1,0:T(8,128)} %inc_ref.1) | copy-start | bytes 294916
  2.5 24.1 %copy-start.2 = (f32[304,128]{1,0:T(8,128)S(1)}, f32[304,128]{1,0:T(8,128)}, u32[]{:S(2)}) copy-start(f32[304,128]{1,0:T(8,128)} %get-tuple-element.11.own_ref) | copy-start | bytes 466948
  2.5 11.9 %collective-permute-start.1 = (f32[304,128]{1,0:T(8,128)}, f32[304,128]{1,0:T(8,128)S(1)}, u32[]{:S(2)}, u32[]{:S(2)}) collective-permute-start(f32[304,128]{1,0:T(8,128)} %get-tuple-element.12), channel_id=1, source_target_pairs={{8,0},{16,8},{24,16},{32,24},{40,32},{48,40},{56,48},{64,56},{72,6... | collective-permute-start | bytes 466952 | tf_op jit(solution)/shard_map/ppermute | solution.py:390
  3.9 10.5 %collective-permute-start = (f32[304,128]{1,0:T(8,128)}, f32[304,128]{1,0:T(8,128)S(1)}, u32[]{:S(2)}, u32[]{:S(2)}) collective-permute-start(f32[304,128]{1,0:T(8,128)} %get-tuple-element.11.own_ref), channel_id=1, source_target_pairs={{0,8},{8,16},{16,24},{24,32},{32,40},{40,48},{48,56},{56,64},{64,7... | collective-permute-start | bytes 466952 | tf_op jit(solution)/shard_map/ppermute | solution.py:390
  8.6 1.0 copy-start.3
  9.6 1.0 copy-start.4
  10.7 0.9 copy-start.5
  11.6 0.9 copy-start.6
  14.4 0.9 copy-start.1
  15.7 10.1 %collective-permute-start.2 = (f32[208,128]{1,0:T(8,128)S(1)}, f32[208,128]{1,0:T(8,128)S(1)}, u32[]{:S(2)}, u32[]{:S(2)}) collective-permute-start(f32[208,128]{1,0:T(8,128)S(1)} %get-tuple-element.13), channel_id=1, source_target_pairs={{0,1},{1,2},{2,3},{3,4},{4,5},{5,6},{6,7},{8,9},{9,10},{10,11},{11... | collective-permute-start | bytes 319496 | tf_op jit(solution)/shard_map/ppermute | solution.py:390
  20.1 6.5 %collective-permute-start.3 = (f32[208,128]{1,0:T(8,128)S(1)}, f32[208,128]{1,0:T(8,128)S(1)}, u32[]{:S(2)}, u32[]{:S(2)}) collective-permute-start(f32[208,128]{1,0:T(8,128)S(1)} %get-tuple-element.14), channel_id=1, source_target_pairs={{1,0},{2,1},{3,2},{4,3},{5,4},{6,5},{7,6},{9,8},{10,9},{11,10},{12... | collective-permute-start | bytes 319496 | tf_op jit(solution)/shard_map/ppermute | solution.py:390
  34.3 3.5 %collective-permute-start.4 = (f32[584,128]{1,0:T(8,128)S(1)}, f32[584,128]{1,0:T(8,128)S(1)}, u32[]{:S(2)}, u32[]{:S(2)}) collective-permute-start(f32[584,128]{1,0:T(8,128)S(1)} %shard_map.107.own_ref.vec_ref), channel_id=1, source_target_pairs={{0,1},{1,0},{2,3},{3,2},{4,5},{5,4},{6,7},{7,6},{8,9},{9,8},{10,11... | collective-permute-start | bytes 897032 | tf_op jit(solution)/shard_map/ppermute | solution.py:459
  105.9 7.9 %collective-permute-start.5 = (f32[4,144,128]{2,1,0:T(8,128)S(1)}, f32[4,144,128]{2,1,0:T(8,128)S(1)}, u32[]{:S(2)}, u32[]{:S(2)}) collective-permute-start(f32[4,144,128]{2,1,0:T(8,128)S(1)} %all_to_all.23.own_ref), channel_id=1, source_target_pairs={{0,1},{1,0},{2,3},{3,2},{4,5},{5,4},{6,7},{7,6},{8,9},{9,8},{10,11... | collective-permute-start | bytes 884744 | tf_op jit(solution)/shard_map/ppermute | solution.py:468

commit v4 on v3

--- a/solution.py
+++ b/solution.py
@@ -47,11 +47,8 @@
         copy.wait()
 
 
-def pack_wide_kernel(*refs):
-    up_ref, dn_ref = refs[4:6]
-    fc_ref, b_ref, nb_ref, pt_ref = refs[6:10]
-    fetch(refs[0:4], refs[6:10], refs[10])
-    meta = jnp.concatenate(
+def meta_rows(nb_ref, pt_ref):
+    return jnp.concatenate(
         [
             (nb_ref[...] + 1).astype(F32),
             pt_ref[...].astype(F32),
@@ -59,6 +56,13 @@
         ],
         axis=0,
     )
+
+
+def pack_wide_kernel(*refs):
+    up_ref, dn_ref = refs[4:6]
+    fc_ref, b_ref, nb_ref, pt_ref = refs[6:10]
+    fetch(refs[0:4], refs[6:10], refs[10])
+    meta = meta_rows(nb_ref, pt_ref)
     top, low = fc_ref[0:HALF, :], fc_ref[HALF:W, :]
     first = lanes(HALF) < 64
     for ref in (up_ref, dn_ref):
@@ -79,8 +83,9 @@
     )
 
 
-def pack_short_kernel(fc_ref, own_ref, up_ref, dn_ref, lo_ref, hi_ref):
+def pack_short_kernel(fc_ref, b_ref, nb_ref, pt_ref, up_ref, dn_ref, lo_ref, hi_ref):
     first = lanes(META) < 64
+    meta = meta_rows(nb_ref, pt_ref)
     fc_ud = unpack_fc(up_ref[ROWS : ROWS + HALF, :], dn_ref[ROWS : ROWS + HALF, :])
 
     def part(rows, tiles):
@@ -101,17 +106,13 @@
         high = jnp.where(col < 24, high, moved(own, 124))
         hi_ref[rows, :] = jnp.where(col < 28, high, dn)
 
-    part(slice(0, W), (up_ref[0:W, :], own_ref[0:W, :], dn_ref[0:W, :], fc_ref[...], fc_ud))
+    part(slice(0, W), (up_ref[0:W, :], b_ref[...], dn_ref[0:W, :], fc_ref[...], fc_ud))
     m = slice(W, ROWS)
     meta_ud = jnp.where(first, dn_ref[m, :], up_ref[m, :])
-    part(m, (up_ref[m, :], own_ref[m, :], dn_ref[m, :], own_ref[m, :], meta_ud))
-
-
-def weight_kernel(*refs):
-    tw_ref, lw_ref, fw_ref = refs[4:7]
-    tr_ref, ti_ref, lr_ref, li_ref = refs[7:11]
-    fetch(refs[0:4], refs[7:11], refs[11])
-
+    part(m, (up_ref[m, :], meta, dn_ref[m, :], meta, meta_ud))
+
+
+def weight_kernel(tr_ref, ti_ref, lr_ref, li_ref, tw_ref, lw_ref, fw_ref):
     def turned(ref):
         n = ref.shape[0]
         fill = -n * HALF % PT
@@ -162,7 +163,9 @@
 
 def main_kernel(
     base_ref,
-    own_ref,
+    b_ref,
+    nb_ref,
+    pt_ref,
     up_ref,
     dn_ref,
     lf_ref,
@@ -181,8 +184,8 @@
     own_ids = ids[0:PT, :]
     first = lanes(META) < 64
     col = lanes(META) % 32
-    b = own_ref[0:W, :]
-    m_own, m_up, m_dn = own_ref[m, :], up_ref[m, :], dn_ref[m, :]
+    b = b_ref[...]
+    m_own, m_up, m_dn = meta_rows(nb_ref, pt_ref), up_ref[m, :], dn_ref[m, :]
     m_ud = jnp.where(first, m_dn, m_up)
     wide = lanes(W) % 32 >= 16
     m_lr = jnp.where(col >= 16, lf_ref[m, :], rt_ref[m, :])
@@ -406,20 +409,21 @@
     core = lax.axis_index("gy") % 2
     base = jnp.stack([tile * PT, jnp.int32(n_short * PT), core]).astype(jnp.int32)
 
+    kinds = particle_type.reshape(1, PT)
     to_up, to_dn = call(
         pack_wide_kernel,
         [(ROWS + HALF, PT)] * 2,
         forward_coeff,
         cost_grad,
         neighbours,
-        particle_type.reshape(1, PT),
+        kinds,
         mib=60,
         fetched=True,
     )
     up = shifted(to_up, "gx", 1)
     dn = shifted(to_dn, "gx", -1)
     to_lo, to_hi = call(
-        pack_short_kernel, [(ROWS, PT)] * 2, forward_coeff, to_up, up, dn
+        pack_short_kernel, [(ROWS, PT)] * 2, forward_coeff, cost_grad, neighbours, kinds, up, dn
     )
     lf = shifted(to_hi, "gy", 1)
     rt = shifted(to_lo, "gy", -1)
@@ -433,14 +437,15 @@
         translation_imaginary,
         mib=16,
         dtype=BF16,
-        fetched=True,
     )
 
     (vectors,) = call(
         main_kernel,
         [(3 * W + 8, PT)],
         base,
-        to_up,
+        cost_grad,
+        neighbours,
+        kinds,
         up,
         dn,
         lf,

time: 116 us -> 115 us (level)
  starting transfers between devices: 25.1 us -> 22.5 us
  waiting for transfers between devices: 3.26 us -> 5.74 us
  blocking collectives: 66 us -> 67.2 us
    ppermute x4, starting transfers between devices: 16.1 us -> 13.8 us  [shifted(): lax.ppermute(block, axis, [(i, i + step) for i in range(n) if 0 <= i + st...]
    ppermute x4, waiting for transfers between devices: 0.86 us -> 3 us  [shifted(): lax.ppermute(block, axis, [(i, i + step) for i in range(n) if 0 <= i + st...]
    unnamed x16 -> x18, local copies, waits for them, and re-layouts: 4.83 us -> 3.93 us
  transfers between devices with their start and end apart: 6 -> 6, of which waited for: 3 -> 4; matrix products, arithmetic and copies ran while one was open for 0% -> 0% of each run, Pallas kernels for 2% -> 1%
where the time goes in v4:
time: 115 us; the launch traced here: 114 us
  blocking collectives  67.2 us (58%)
  starting transfers between devices  22.5 us (20%)
  Pallas kernels  14.2 us (12%)
  waiting for transfers between devices  5.74 us (5%)
  local copies, waits for them, and re-layouts  3.93 us (3%)
    all_to_all x1, blocking collectives, body(): got = lax.all_to_all(pieces.reshape(64, 8, PT), 'gx', 0, 0)  29.4 us
    all_to_all x1, blocking collectives, body(): got = lax.all_to_all(mixed.reshape(64, 4, PT), 'gx', 0, 0)  16.5 us
    pallas_call x9, Pallas kernels, call(): pl.pallas_call(kernel, out_shape=[jax.ShapeDtypeStruct(s, dtype) for s in...  14.2 us
    ppermute x4, starting transfers between devices, shifted(): lax.ppermute(block, axis, [(i, i + step) for i in range(n) if 0 <= i + st...  13.8 us
    all_to_all x1, blocking collectives, body(): got = lax.all_to_all(chunks, 'gy', 0, 0, axis_index_groups=lines)  13.3 us
    all_to_all x1, blocking collectives, body(): half = lax.all_to_all(copies, 'gy', 0, 0, axis_index_groups=lines)  8.07 us
    ppermute x1, starting transfers between devices, body(): other = lax.ppermute(half, 'gy', pairs)  6.73 us
    unnamed x18, local copies, waits for them, and re-layouts  3.93 us
  transfers between devices with their start and end apart: 6, of which 4 were waited for; matrix products, arithmetic and copies ran while one was open for 0% of the time, Pallas kernels for 1%

profile of v4, /device:TPU:1, one launch (start us, length us, event | category | flops | bytes accessed | tf_op | source)
XLA Modules:
  0.0 114.4 jit_solution(3601189847144602212)
XLA Ops:
  0.6 0.0 copy-start.7
  0.6 0.0 copy-start
  0.7 0.0 copy-start.1
  0.7 0.0 copy-start.8
  0.7 1.8 %shard_map.104 = (f32[304,128]{1,0:T(8,128)}, f32[304,128]{1,0:T(8,128)}) custom-call(f32[192,128]{1,0:T(8,128)} %fc_ref.3, f32[192,128]{1,0:T(8,128)} %b_ref.3, s32[10,128]{1,0:T(8,128)} %nb_ref.3, s32[1,128]{1,0:T(1,128)} %bitcast.11), custom_call_target="tpu_custom_call" | custom-call | tf_op jit(solution)/shard_map/pallas_call | solution.py:381
  2.5 4.0 %collective-permute-start = (f32[304,128]{1,0:T(8,128)}, f32[304,128]{1,0:T(8,128)S(1)}, u32[]{:S(2)}, u32[]{:S(2)}) collective-permute-start(f32[304,128]{1,0:T(8,128)} %get-tuple-element.11), channel_id=1, source_target_pairs={{0,8},{8,16},{16,24},{24,32},{32,40},{40,48},{48,56},{56,64},{64,7... | collective-permute-start | bytes 466952 | tf_op jit(solution)/shard_map/ppermute | solution.py:393
  6.6 1.3 %collective-permute-start.1 = (f32[304,128]{1,0:T(8,128)}, f32[304,128]{1,0:T(8,128)S(1)}, u32[]{:S(2)}, u32[]{:S(2)}) collective-permute-start(f32[304,128]{1,0:T(8,128)} %get-tuple-element.12), channel_id=1, source_target_pairs={{8,0},{16,8},{24,16},{32,24},{40,32},{48,40},{56,48},{64,56},{72,6... | collective-permute-start | bytes 466952 | tf_op jit(solution)/shard_map/ppermute | solution.py:393
  7.9 0.0 copy-start.2
  7.9 1.0 copy-done.2
  8.9 0.0 copy-start.3
  8.9 1.0 copy-done.3
  9.9 0.0 copy-start.4
  9.9 0.9 copy-done.4
  10.9 0.0 copy-start.5
  10.9 0.9 copy-done.5
  11.8 0.0 copy-start.6
  11.8 0.7 shard_map.106
  12.5 0.0 collective-permute-done.up_ref
  12.5 0.2 collective-permute-done.1.dn_ref
  12.7 0.0 copy-done.7
  12.7 0.0 copy-done
  12.7 0.0 copy-done.1
  12.7 0.0 copy-done.8
  12.8 0.3 shard_map.105
  13.1 5.4 %collective-permute-start.2 = (f32[208,128]{1,0:T(8,128)S(1)}, f32[208,128]{1,0:T(8,128)S(1)}, u32[]{:S(2)}, u32[]{:S(2)}) collective-permute-start(f32[208,128]{1,0:T(8,128)S(1)} %get-tuple-element.13), channel_id=1, source_target_pairs={{0,1},{1,2},{2,3},{3,4},{4,5},{5,6},{6,7},{8,9},{9,10},{10,11},{11... | collective-permute-start | bytes 319496 | tf_op jit(solution)/shard_map/ppermute | solution.py:393
  18.4 3.1 %collective-permute-start.3 = (f32[208,128]{1,0:T(8,128)S(1)}, f32[208,128]{1,0:T(8,128)S(1)}, u32[]{:S(2)}, u32[]{:S(2)}) collective-permute-start(f32[208,128]{1,0:T(8,128)S(1)} %get-tuple-element.14), channel_id=1, source_target_pairs={{1,0},{2,1},{3,2},{4,3},{5,4},{6,5},{7,6},{9,8},{10,9},{11,10},{12... | collective-permute-start | bytes 319496 | tf_op jit(solution)/shard_map/ppermute | solution.py:393
  21.6 0.1 pad_add_fusion.base_ref
  21.7 0.0 collective-permute-done.2.lf_ref
  21.7 2.8 %collective-permute-done.3.rt_ref = f32[208,128]{1,0:T(8,128)S(1)} collective-permute-done((f32[208,128]{1,0:T(8,128)S(1)}, f32[208,128]{1,0:T(8,128)S(1)}, u32[]{:S(2)}, u32[]{:S(2)}) %collective-permute-start.3) | collective-permute-done | bytes 106528 | tf_op jit(solution)/shard_map/ppermute | solution.py:393
  24.5 0.0 copy-done.6
  24.5 7.7 %shard_map.107.own_ref.vec_ref = f32[584,128]{1,0:T(8,128)S(1)} custom-call(s32[3]{0:T(128)S(1)} %pad_add_fusion.base_ref, f32[192,128]{1,0:T(8,128)S(1)} %copy-done, s32[10,128]{1,0:T(8,128)S(1)} %copy-done.7, s32[1,128]{1,0:T(1,128)S(1)} %bitcast.13, f32[304,128]{1,0:T(8,128)S(1)} %collective-permute-done.up_ref, ...), custom_call_target="tpu_custom_call" | custom-call | tf_op jit(solution)/shard_map/pallas_call | solution.py:381
  32.2 1.9 %collective-permute-start.4 = (f32[584,128]{1,0:T(8,128)S(1)}, f32[584,128]{1,0:T(8,128)S(1)}, u32[]{:S(2)}, u32[]{:S(2)}) collective-permute-start(f32[584,128]{1,0:T(8,128)S(1)} %shard_map.107.own_ref.vec_ref), channel_id=1, source_target_pairs={{0,1},{1,0},{2,3},{3,2},{4,5},{5,4},{6,7},{7,6},{8,9},{9,8},{10,11... | collective-permute-start | bytes 897032 | tf_op jit(solution)/shard_map/ppermute | solution.py:464
  34.1 1.6 %collective-permute-done.4.other_ref = f32[584,128]{1,0:T(8,128)S(1)} collective-permute-done((f32[584,128]{1,0:T(8,128)S(1)}, f32[584,128]{1,0:T(8,128)S(1)}, u32[]{:S(2)}, u32[]{:S(2)}) %collective-permute-start.4) | collective-permute-done | bytes 299040 | tf_op jit(solution)/shard_map/ppermute | solution.py:464
  35.7 1.1 shard_map.108
  36.8 13.3 %all_to_all.20.in_ref = f32[4,296,128]{2,1,0:T(8,128)S(1)} all-to-all(f32[4,296,128]{2,1,0:T(8,128)S(1)} %shard_map.108), channel_id=1, replica_groups={{0,2,4,6},{1,3,5,7},{8,10,12,14},{9,11,13,15},{16,18,20,22},{17,19,21,2..., dimensions={0} | all-to-all | bytes 1212416 | tf_op jit(solution)/shard_map/all_to_all | solution.py:466
  50.1 0.1 shard_map.109
  50.1 29.4 %all_to_all.21 = f32[64,8,128]{2,1,0:T(8,128)S(1)} all-to-all(f32[64,8,128]{2,1,0:T(8,128)S(1)} %bitcast.8), channel_id=1, replica_groups=mesh['gx'=64,'gy'=8] {'gx'}, dimensions={0} | all-to-all | bytes 524288 | tf_op jit(solution)/shard_map/all_to_all | solution.py:468
  79.5 0.9 shard_map.110
  80.3 16.5 %all_to_all.22 = f32[64,4,128]{2,1,0:T(4,128)S(1)} all-to-all(f32[64,4,128]{2,1,0:T(4,128)S(1)} %bitcast.10), channel_id=1, replica_groups=mesh['gx'=64,'gy'=8] {'gx'}, dimensions={0} | all-to-all | bytes 262144 | tf_op jit(solution)/shard_map/all_to_all | solution.py:470
  96.9 8.1 %all_to_all.23.own_ref = f32[4,144,128]{2,1,0:T(8,128)S(1)} all-to-all(f32[4,144,128]{2,1,0:T(8,128)S(1)} %shard_map.111), channel_id=1, replica_groups={{0,2,4,6},{1,3,5,7},{8,10,12,14},{9,11,13,15},{16,18,20,22},{17,19,21,2..., dimensions={0} | all-to-all | bytes 589824 | tf_op jit(solution)/shard_map/all_to_all | solution.py:472
  104.9 6.7 %collective-permute-start.5 = (f32[4,144,128]{2,1,0:T(8,128)S(1)}, f32[4,144,128]{2,1,0:T(8,128)S(1)}, u32[]{:S(2)}, u32[]{:S(2)}) collective-permute-start(f32[4,144,128]{2,1,0:T(8,128)S(1)} %all_to_all.23.own_ref), channel_id=1, source_target_pairs={{0,1},{1,0},{2,3},{3,2},{4,5},{5,4},{6,7},{7,6},{8,9},{9,8},{10,11... | collective-permute-start | bytes 884744 | tf_op jit(solution)/shard_map/ppermute | solution.py:473
  111.7 1.2 %collective-permute-done.5.other_ref = f32[4,144,128]{2,1,0:T(8,128)S(1)} collective-permute-done((f32[4,144,128]{2,1,0:T(8,128)S(1)}, f32[4,144,128]{2,1,0:T(8,128)S(1)}, u32[]{:S(2)}, u32[]{:S(2)}) %collective-permute-start.5) | collective-permute-done | bytes 294944 | tf_op jit(solution)/shard_map/ppermute | solution.py:473
  112.9 1.5 %shard_map.112 = f32[4,192,192]{2,1,0:T(8,128)} custom-call(s32[3]{0:T(128)S(1)} %pad_add_fusion.base_ref, f32[4,144,128]{2,1,0:T(8,128)S(1)} %all_to_all.23.own_ref, f32[4,144,128]{2,1,0:T(8,128)S(1)} %collective-permute-done.5.other_ref), custom_call_target="tpu_custom_call" | custom-call | tf_op jit(solution)/shard_map/pallas_call | solution.py:381
  (1 shorter events, 0.0 us)
Async XLA Ops:
  0.6 12.1 %copy-start.7 = (s32[10,128]{1,0:T(8,128)S(1)}, s32[10,128]{1,0:T(8,128)}, u32[]{:S(2)}) copy-start(s32[10,128]{1,0:T(8,128)} %nb_ref.3) | copy-start | bytes 15364
  0.6 12.1 %copy-start = (f32[192,128]{1,0:T(8,128)S(1)}, f32[192,128]{1,0:T(8,128)}, u32[]{:S(2)}) copy-start(f32[192,128]{1,0:T(8,128)} %b_ref.3) | copy-start | bytes 294916
  0.7 12.1 %copy-start.1 = (f32[192,128]{1,0:T(8,128)S(1)}, f32[192,128]{1,0:T(8,128)}, u32[]{:S(2)}) copy-start(f32[192,128]{1,0:T(8,128)} %fc_ref.3) | copy-start | bytes 294916
  0.7 12.1 %copy-start.8 = (s32[128]{0:T(128)S(1)}, s32[128]{0:T(128)}, u32[]{:S(2)}) copy-start(s32[128]{0:T(128)} %param.17) | copy-start | bytes 1540
  2.5 10.0 %collective-permute-start = (f32[304,128]{1,0:T(8,128)}, f32[304,128]{1,0:T(8,128)S(1)}, u32[]{:S(2)}, u32[]{:S(2)}) collective-permute-start(f32[304,128]{1,0:T(8,128)} %get-tuple-element.11), channel_id=1, source_target_pairs={{0,8},{8,16},{16,24},{24,32},{32,40},{40,48},{48,56},{56,64},{64,7... | collective-permute-start | bytes 466952 | tf_op jit(solution)/shard_map/ppermute | solution.py:393
  6.6 6.2 %collective-permute-start.1 = (f32[304,128]{1,0:T(8,128)}, f32[304,128]{1,0:T(8,128)S(1)}, u32[]{:S(2)}, u32[]{:S(2)}) collective-permute-start(f32[304,128]{1,0:T(8,128)} %get-tuple-element.12), channel_id=1, source_target_pairs={{8,0},{16,8},{24,16},{32,24},{40,32},{48,40},{56,48},{64,56},{72,6... | collective-permute-start | bytes 466952 | tf_op jit(solution)/shard_map/ppermute | solution.py:393
  7.9 1.0 copy-start.2
  8.9 1.0 copy-start.3
  9.9 0.9 copy-start.4
  10.9 0.9 copy-start.5
  11.8 12.7 %copy-start.6 = (f32[192,128]{1,0:T(8,128)S(1)}, f32[192,128]{1,0:T(8,128)}, u32[]{:S(2)}) copy-start(f32[192,128]{1,0:T(8,128)} %inc_ref.1) | copy-start | bytes 294916
  13.1 8.6 %collective-permute-start.2 = (f32[208,128]{1,0:T(8,128)S(1)}, f32[208,128]{1,0:T(8,128)S(1)}, u32[]{:S(2)}, u32[]{:S(2)}) collective-permute-start(f32[208,128]{1,0:T(8,128)S(1)} %get-tuple-element.13), channel_id=1, source_target_pairs={{0,1},{1,2},{2,3},{3,4},{4,5},{5,6},{6,7},{8,9},{9,10},{10,11},{11... | collective-permute-start | bytes 319496 | tf_op jit(solution)/shard_map/ppermute | solution.py:393
  18.4 6.0 %collective-permute-start.3 = (f32[208,128]{1,0:T(8,128)S(1)}, f32[208,128]{1,0:T(8,128)S(1)}, u32[]{:S(2)}, u32[]{:S(2)}) collective-permute-start(f32[208,128]{1,0:T(8,128)S(1)} %get-tuple-element.14), channel_id=1, source_target_pairs={{1,0},{2,1},{3,2},{4,3},{5,4},{6,5},{7,6},{9,8},{10,9},{11,10},{12... | collective-permute-start | bytes 319496 | tf_op jit(solution)/shard_map/ppermute | solution.py:393
  32.2 3.5 %collective-permute-start.4 = (f32[584,128]{1,0:T(8,128)S(1)}, f32[584,128]{1,0:T(8,128)S(1)}, u32[]{:S(2)}, u32[]{:S(2)}) collective-permute-start(f32[584,128]{1,0:T(8,128)S(1)} %shard_map.107.own_ref.vec_ref), channel_id=1, source_target_pairs={{0,1},{1,0},{2,3},{3,2},{4,5},{5,4},{6,7},{7,6},{8,9},{9,8},{10,11... | collective-permute-start | bytes 897032 | tf_op jit(solution)/shard_map/ppermute | solution.py:464
  104.9 7.9 %collective-permute-start.5 = (f32[4,144,128]{2,1,0:T(8,128)S(1)}, f32[4,144,128]{2,1,0:T(8,128)S(1)}, u32[]{:S(2)}, u32[]{:S(2)}) collective-permute-start(f32[4,144,128]{2,1,0:T(8,128)S(1)} %all_to_all.23.own_ref), channel_id=1, source_target_pairs={{0,1},{1,0},{2,3},{3,2},{4,5},{5,4},{6,7},{7,6},{8,9},{9,8},{10,11... | collective-permute-start | bytes 884744 | tf_op jit(solution)/shard_map/ppermute | solution.py:473

commit v5 on v4

--- a/solution.py
+++ b/solution.py
@@ -374,7 +374,7 @@
                 out_ref[first + k, at + 48 : at + HALF, PT:W] = pltpu.roll(edge, 64, 1)[:, 0:64]
 
 
-def call(kernel, shapes, *args, smem=0, mib=6, dtype=F32, fetched=False, **kw):
+def call(kernel, shapes, *args, smem=0, mib=6, dtype=F32, fetched=False, us=1, **kw):
     if fetched:
         kw["scratch_shapes"] = [pltpu.VMEM(a.shape, a.dtype) for a in args]
         kw["scratch_shapes"].append(pltpu.SemaphoreType.DMA((len(args),)))
@@ -383,6 +383,9 @@
         out_shape=[jax.ShapeDtypeStruct(s, dtype) for s in shapes],
         in_specs=[pl.BlockSpec(memory_space=pltpu.SMEM)] * smem
         + [pl.BlockSpec(memory_space=pltpu.HBM if fetched else pltpu.VMEM)] * (len(args) - smem),
+        cost_estimate=pl.CostEstimate(
+            flops=us * 10**9, bytes_accessed=us * 3 * 10**6, transcendentals=0
+        ),
         compiler_params=pltpu.CompilerParams(vmem_limit_bytes=mib * MIB),
         **kw,
     )(*args)
@@ -418,6 +421,7 @@
         neighbours,
         kinds,
         mib=60,
+        us=4,
         fetched=True,
     )
     up = shifted(to_up, "gx", 1)

time: 115 us -> 114 us (level)
  local copies, waits for them, and re-layouts: 3.93 us -> 0.05 us
  waiting for transfers between devices: 5.74 us -> 9.57 us
    unnamed x18, local copies, waits for them, and re-layouts: 3.93 us -> 0.05 us
    ppermute x4, waiting for transfers between devices: 3 us -> 6.83 us  [shifted(): lax.ppermute(block, axis, [(i, i + step) for i in range(n) if 0 <= i + st...]
  transfers between devices with their start and end apart: 6 -> 6, of which waited for: 4 -> 5; matrix products, arithmetic and copies ran while one was open for 0% -> 0% of each run, Pallas kernels for 1% -> 1%
where the time goes in v5:
time: 114 us
  blocking collectives  66.7 us (59%)
  starting transfers between devices  22.5 us (20%)
  Pallas kernels  14.2 us (12%)
  waiting for transfers between devices  9.57 us (8%)
    all_to_all x1, blocking collectives, body(): got = lax.all_to_all(pieces.reshape(64, 8, PT), 'gx', 0, 0)  28.8 us
    all_to_all x1, blocking collectives, body(): got = lax.all_to_all(mixed.reshape(64, 4, PT), 'gx', 0, 0)  16.5 us
    pallas_call x9, Pallas kernels, call(): pl.pallas_call(kernel, out_shape=[jax.ShapeDtypeStruct(s, dtype) for s in...  14.2 us
    ppermute x4, starting transfers between devices, shifted(): lax.ppermute(block, axis, [(i, i + step) for i in range(n) if 0 <= i + st...  13.8 us
    all_to_all x1, blocking collectives, body(): got = lax.all_to_all(chunks, 'gy', 0, 0, axis_index_groups=lines)  13.3 us
    all_to_all x1, blocking collectives, body(): half = lax.all_to_all(copies, 'gy', 0, 0, axis_index_groups=lines)  8.07 us
    ppermute x4, waiting for transfers between devices, shifted(): lax.ppermute(block, axis, [(i, i + step) for i in range(n) if 0 <= i + st...  6.83 us
    ppermute x1, starting transfers between devices, body(): other = lax.ppermute(half, 'gy', pairs)  6.73 us
  transfers between devices with their start and end apart: 6, of which 5 were waited for; matrix products, arithmetic and copies ran while one was open for 0% of the time, Pallas kernels for 1%

profile of v5, /device:TPU:1, one launch (start us, length us, event | category | flops | bytes accessed | tf_op | source)
XLA Modules:
  0.0 114.0 jit_solution(15951488974464240845)
XLA Ops:
  0.6 0.0 copy-start.5
  0.6 0.0 copy-start.6
  0.7 0.0 copy-start.7
  0.7 0.0 copy-start.8
  0.7 1.9 %shard_map.104 = (f32[304,128]{1,0:T(8,128)}, f32[304,128]{1,0:T(8,128)}) custom-call(f32[192,128]{1,0:T(8,128)} %fc_ref.3, f32[192,128]{1,0:T(8,128)} %b_ref.3, s32[10,128]{1,0:T(8,128)} %nb_ref.3, s32[1,128]{1,0:T(1,128)} %bitcast.11), custom_call_target="tpu_custom_call" | custom-call | flops 4000000000 | bytes 12000000 | tf_op jit(solution)/shard_map/pallas_call | solution.py:381
  2.6 4.0 %collective-permute-start = (f32[304,128]{1,0:T(8,128)}, f32[304,128]{1,0:T(8,128)S(1)}, u32[]{:S(2)}, u32[]{:S(2)}) collective-permute-start(f32[304,128]{1,0:T(8,128)} %get-tuple-element.11), channel_id=1, source_target_pairs={{0,8},{8,16},{16,24},{24,32},{32,40},{40,48},{48,56},{56,64},{64,7... | collective-permute-start | bytes 466952 | tf_op jit(solution)/shard_map/ppermute | solution.py:396
  6.6 1.3 %collective-permute-start.1 = (f32[304,128]{1,0:T(8,128)}, f32[304,128]{1,0:T(8,128)S(1)}, u32[]{:S(2)}, u32[]{:S(2)}) collective-permute-start(f32[304,128]{1,0:T(8,128)} %get-tuple-element.12), channel_id=1, source_target_pairs={{8,0},{16,8},{24,16},{32,24},{40,32},{48,40},{56,48},{64,56},{72,6... | collective-permute-start | bytes 466952 | tf_op jit(solution)/shard_map/ppermute | solution.py:396
  7.9 0.0 copy-done.5
  7.9 0.0 copy-done.6
  7.9 0.0 copy-done.7
  8.0 0.0 copy-done.8
  8.0 0.0 copy-start
  8.0 0.0 copy-start.1
  8.0 0.0 copy-start.3
  8.0 0.0 copy-start.4
  8.0 0.7 shard_map.106
  8.8 0.0 copy-start.2
  8.8 0.3 collective-permute-done.up_ref
  9.1 3.7 %collective-permute-done.1.dn_ref = f32[304,128]{1,0:T(8,128)S(1)} collective-permute-done((f32[304,128]{1,0:T(8,128)}, f32[304,128]{1,0:T(8,128)S(1)}, u32[]{:S(2)}, u32[]{:S(2)}) %collective-permute-start.1) | collective-permute-done | bytes 155680 | tf_op jit(solution)/shard_map/ppermute | solution.py:396
  12.8 0.0 copy-done
  12.8 0.0 copy-done.1
  12.8 0.0 copy-done.3
  12.8 0.0 copy-done.4
  12.8 0.3 shard_map.105
  13.1 5.4 %collective-permute-start.2 = (f32[208,128]{1,0:T(8,128)S(1)}, f32[208,128]{1,0:T(8,128)S(1)}, u32[]{:S(2)}, u32[]{:S(2)}) collective-permute-start(f32[208,128]{1,0:T(8,128)S(1)} %get-tuple-element.13), channel_id=1, source_target_pairs={{0,1},{1,2},{2,3},{3,4},{4,5},{5,6},{6,7},{8,9},{9,10},{10,11},{11... | collective-permute-start | bytes 319496 | tf_op jit(solution)/shard_map/ppermute | solution.py:396
  18.5 3.1 %collective-permute-start.3 = (f32[208,128]{1,0:T(8,128)S(1)}, f32[208,128]{1,0:T(8,128)S(1)}, u32[]{:S(2)}, u32[]{:S(2)}) collective-permute-start(f32[208,128]{1,0:T(8,128)S(1)} %get-tuple-element.14), channel_id=1, source_target_pairs={{1,0},{2,1},{3,2},{4,3},{5,4},{6,5},{7,6},{9,8},{10,9},{11,10},{12... | collective-permute-start | bytes 319496 | tf_op jit(solution)/shard_map/ppermute | solution.py:396
  21.6 0.1 pad_add_fusion.base_ref
  21.7 0.0 collective-permute-done.2.lf_ref
  21.7 2.8 %collective-permute-done.3.rt_ref = f32[208,128]{1,0:T(8,128)S(1)} collective-permute-done((f32[208,128]{1,0:T(8,128)S(1)}, f32[208,128]{1,0:T(8,128)S(1)}, u32[]{:S(2)}, u32[]{:S(2)}) %collective-permute-start.3) | collective-permute-done | bytes 106528 | tf_op jit(solution)/shard_map/ppermute | solution.py:396
  24.5 0.0 copy-done.2
  24.5 7.7 %shard_map.107.own_ref.vec_ref = f32[584,128]{1,0:T(8,128)S(1)} custom-call(s32[3]{0:T(128)S(1)} %pad_add_fusion.base_ref, f32[192,128]{1,0:T(8,128)S(1)} %copy-done, s32[10,128]{1,0:T(8,128)S(1)} %copy-done.3, s32[1,128]{1,0:T(1,128)S(1)} %bitcast.13, f32[304,128]{1,0:T(8,128)S(1)} %collective-permute-done.up_ref, ...), custom_call_target="tpu_custom_call" | custom-call | flops 1000000000 | bytes 3000000 | tf_op jit(solution)/shard_map/pallas_call | solution.py:381
  32.2 1.9 %collective-permute-start.4 = (f32[584,128]{1,0:T(8,128)S(1)}, f32[584,128]{1,0:T(8,128)S(1)}, u32[]{:S(2)}, u32[]{:S(2)}) collective-permute-start(f32[584,128]{1,0:T(8,128)S(1)} %shard_map.107.own_ref.vec_ref), channel_id=1, source_target_pairs={{0,1},{1,0},{2,3},{3,2},{4,5},{5,4},{6,7},{7,6},{8,9},{9,8},{10,11... | collective-permute-start | bytes 897032 | tf_op jit(solution)/shard_map/ppermute | solution.py:468
  34.2 1.6 %collective-permute-done.4.other_ref = f32[584,128]{1,0:T(8,128)S(1)} collective-permute-done((f32[584,128]{1,0:T(8,128)S(1)}, f32[584,128]{1,0:T(8,128)S(1)}, u32[]{:S(2)}, u32[]{:S(2)}) %collective-permute-start.4) | collective-permute-done | bytes 299040 | tf_op jit(solution)/shard_map/ppermute | solution.py:468
  35.7 1.1 shard_map.108
  36.8 13.3 %all_to_all.20.in_ref = f32[4,296,128]{2,1,0:T(8,128)S(1)} all-to-all(f32[4,296,128]{2,1,0:T(8,128)S(1)} %shard_map.108), channel_id=1, replica_groups={{0,2,4,6},{1,3,5,7},{8,10,12,14},{9,11,13,15},{16,18,20,22},{17,19,21,2..., dimensions={0} | all-to-all | bytes 1212416 | tf_op jit(solution)/shard_map/all_to_all | solution.py:470
  50.1 0.1 shard_map.109
  50.2 28.8 %all_to_all.21 = f32[64,8,128]{2,1,0:T(8,128)S(1)} all-to-all(f32[64,8,128]{2,1,0:T(8,128)S(1)} %bitcast.8), channel_id=1, replica_groups=mesh['gx'=64,'gy'=8] {'gx'}, dimensions={0} | all-to-all | bytes 524288 | tf_op jit(solution)/shard_map/all_to_all | solution.py:472
  79.0 0.9 shard_map.110
  79.9 16.5 %all_to_all.22 = f32[64,4,128]{2,1,0:T(4,128)S(1)} all-to-all(f32[64,4,128]{2,1,0:T(4,128)S(1)} %bitcast.9), channel_id=1, replica_groups=mesh['gx'=64,'gy'=8] {'gx'}, dimensions={0} | all-to-all | bytes 262144 | tf_op jit(solution)/shard_map/all_to_all | solution.py:474
  96.4 8.1 %all_to_all.23.own_ref = f32[4,144,128]{2,1,0:T(8,128)S(1)} all-to-all(f32[4,144,128]{2,1,0:T(8,128)S(1)} %shard_map.111), channel_id=1, replica_groups={{0,2,4,6},{1,3,5,7},{8,10,12,14},{9,11,13,15},{16,18,20,22},{17,19,21,2..., dimensions={0} | all-to-all | bytes 589824 | tf_op jit(solution)/shard_map/all_to_all | solution.py:476
  104.5 6.7 %collective-permute-start.5 = (f32[4,144,128]{2,1,0:T(8,128)S(1)}, f32[4,144,128]{2,1,0:T(8,128)S(1)}, u32[]{:S(2)}, u32[]{:S(2)}) collective-permute-start(f32[4,144,128]{2,1,0:T(8,128)S(1)} %all_to_all.23.own_ref), channel_id=1, source_target_pairs={{0,1},{1,0},{2,3},{3,2},{4,5},{5,4},{6,7},{7,6},{8,9},{9,8},{10,11... | collective-permute-start | bytes 884744 | tf_op jit(solution)/shard_map/ppermute | solution.py:477
  111.2 1.2 %collective-permute-done.5.other_ref = f32[4,144,128]{2,1,0:T(8,128)S(1)} collective-permute-done((f32[4,144,128]{2,1,0:T(8,128)S(1)}, f32[4,144,128]{2,1,0:T(8,128)S(1)}, u32[]{:S(2)}, u32[]{:S(2)}) %collective-permute-start.5) | collective-permute-done | bytes 294944 | tf_op jit(solution)/shard_map/ppermute | solution.py:477
  112.4 1.5 %shard_map.112 = f32[4,192,192]{2,1,0:T(8,128)} custom-call(s32[3]{0:T(128)S(1)} %pad_add_fusion.base_ref, f32[4,144,128]{2,1,0:T(8,128)S(1)} %all_to_all.23.own_ref, f32[4,144,128]{2,1,0:T(8,128)S(1)} %collective-permute-done.5.other_ref), custom_call_target="tpu_custom_call" | custom-call | flops 1000000000 | bytes 3000000 | tf_op jit(solution)/shard_map/pallas_call | solution.py:381
  (1 shorter events, 0.0 us)
Async XLA Ops:
  0.6 7.3 %copy-start.5 = (f32[10,96,96]{2,1,0:T(8,128)S(1)}, f32[10,96,96]{2,1,0:T(8,128)}, u32[]{:S(2)}) copy-start(f32[10,96,96]{2,1,0:T(8,128)} %lr_ref.1) | copy-start | bytes 1105924
  0.6 7.3 %copy-start.6 = (f32[10,96,96]{2,1,0:T(8,128)S(1)}, f32[10,96,96]{2,1,0:T(8,128)}, u32[]{:S(2)}) copy-start(f32[10,96,96]{2,1,0:T(8,128)} %li_ref.1) | copy-start | bytes 1105924
  0.7 7.3 %copy-start.7 = (f32[4,96,96]{2,1,0:T(8,128)S(1)}, f32[4,96,96]{2,1,0:T(8,128)}, u32[]{:S(2)}) copy-start(f32[4,96,96]{2,1,0:T(8,128)} %tr_ref.1) | copy-start | bytes 442372
  0.7 7.3 %copy-start.8 = (f32[4,96,96]{2,1,0:T(8,128)S(1)}, f32[4,96,96]{2,1,0:T(8,128)}, u32[]{:S(2)}) copy-start(f32[4,96,96]{2,1,0:T(8,128)} %ti_ref.1) | copy-start | bytes 442372
  2.6 6.5 %collective-permute-start = (f32[304,128]{1,0:T(8,128)}, f32[304,128]{1,0:T(8,128)S(1)}, u32[]{:S(2)}, u32[]{:S(2)}) collective-permute-start(f32[304,128]{1,0:T(8,128)} %get-tuple-element.11), channel_id=1, source_target_pairs={{0,8},{8,16},{16,24},{24,32},{32,40},{40,48},{48,56},{56,64},{64,7... | collective-permute-start | bytes 466952 | tf_op jit(solution)/shard_map/ppermute | solution.py:396
  6.6 6.2 %collective-permute-start.1 = (f32[304,128]{1,0:T(8,128)}, f32[304,128]{1,0:T(8,128)S(1)}, u32[]{:S(2)}, u32[]{:S(2)}) collective-permute-start(f32[304,128]{1,0:T(8,128)} %get-tuple-element.12), channel_id=1, source_target_pairs={{8,0},{16,8},{24,16},{32,24},{40,32},{48,40},{56,48},{64,56},{72,6... | collective-permute-start | bytes 466952 | tf_op jit(solution)/shard_map/ppermute | solution.py:396
  8.0 4.8 %copy-start = (f32[192,128]{1,0:T(8,128)S(1)}, f32[192,128]{1,0:T(8,128)}, u32[]{:S(2)}) copy-start(f32[192,128]{1,0:T(8,128)} %b_ref.3) | copy-start | bytes 294916
  8.0 4.8 %copy-start.1 = (f32[192,128]{1,0:T(8,128)S(1)}, f32[192,128]{1,0:T(8,128)}, u32[]{:S(2)}) copy-start(f32[192,128]{1,0:T(8,128)} %fc_ref.3) | copy-start | bytes 294916
  8.0 4.8 %copy-start.3 = (s32[10,128]{1,0:T(8,128)S(1)}, s32[10,128]{1,0:T(8,128)}, u32[]{:S(2)}) copy-start(s32[10,128]{1,0:T(8,128)} %nb_ref.3) | copy-start | bytes 15364
  8.0 4.8 %copy-start.4 = (s32[128]{0:T(128)S(1)}, s32[128]{0:T(128)}, u32[]{:S(2)}) copy-start(s32[128]{0:T(128)} %param.17) | copy-start | bytes 1540
  8.8 15.8 %copy-start.2 = (f32[192,128]{1,0:T(8,128)S(1)}, f32[192,128]{1,0:T(8,128)}, u32[]{:S(2)}) copy-start(f32[192,128]{1,0:T(8,128)} %inc_ref.1) | copy-start | bytes 294916
  13.1 8.6 %collective-permute-start.2 = (f32[208,128]{1,0:T(8,128)S(1)}, f32[208,128]{1,0:T(8,128)S(1)}, u32[]{:S(2)}, u32[]{:S(2)}) collective-permute-start(f32[208,128]{1,0:T(8,128)S(1)} %get-tuple-element.13), channel_id=1, source_target_pairs={{0,1},{1,2},{2,3},{3,4},{4,5},{5,6},{6,7},{8,9},{9,10},{10,11},{11... | collective-permute-start | bytes 319496 | tf_op jit(solution)/shard_map/ppermute | solution.py:396
  18.5 6.0 %collective-permute-start.3 = (f32[208,128]{1,0:T(8,128)S(1)}, f32[208,128]{1,0:T(8,128)S(1)}, u32[]{:S(2)}, u32[]{:S(2)}) collective-permute-start(f32[208,128]{1,0:T(8,128)S(1)} %get-tuple-element.14), channel_id=1, source_target_pairs={{1,0},{2,1},{3,2},{4,3},{5,4},{6,5},{7,6},{9,8},{10,9},{11,10},{12... | collective-permute-start | bytes 319496 | tf_op jit(solution)/shard_map/ppermute | solution.py:396
  32.2 3.5 %collective-permute-start.4 = (f32[584,128]{1,0:T(8,128)S(1)}, f32[584,128]{1,0:T(8,128)S(1)}, u32[]{:S(2)}, u32[]{:S(2)}) collective-permute-start(f32[584,128]{1,0:T(8,128)S(1)} %shard_map.107.own_ref.vec_ref), channel_id=1, source_target_pairs={{0,1},{1,0},{2,3},{3,2},{4,5},{5,4},{6,7},{7,6},{8,9},{9,8},{10,11... | collective-permute-start | bytes 897032 | tf_op jit(solution)/shard_map/ppermute | solution.py:468
  104.5 7.9 %collective-permute-start.5 = (f32[4,144,128]{2,1,0:T(8,128)S(1)}, f32[4,144,128]{2,1,0:T(8,128)S(1)}, u32[]{:S(2)}, u32[]{:S(2)}) collective-permute-start(f32[4,144,128]{2,1,0:T(8,128)S(1)} %all_to_all.23.own_ref), channel_id=1, source_target_pairs={{0,1},{1,0},{2,3},{3,2},{4,5},{5,4},{6,7},{7,6},{8,9},{9,8},{10,11... | collective-permute-start | bytes 884744 | tf_op jit(solution)/shard_map/ppermute | solution.py:477

commit v6 on v5

--- a/solution.py
+++ b/solution.py
@@ -1,3 +1,5 @@
+import functools
+
 import jax
 import jax.numpy as jnp
 from jax import lax
@@ -141,7 +143,7 @@
 
 
 def target_ids(base, row_stride):
-    spot = lax.broadcasted_iota(jnp.int32, (3 * PT, PT), 0)
+    spot = lax.broadcasted_iota(jnp.int32, (4 * PT, PT), 0)
     lane = spot % PT
     row, col = lane // 32, lane % 32
     shift = jnp.where(row < 2, row_stride, -row_stride)
@@ -157,12 +159,124 @@
         ),
     )
     lr = jnp.where((col >= 12) & (col < 20), lr, -10)
-    ids = jnp.where(spot < PT, own, jnp.where(spot < 2 * PT, own + shift, lr))
+    edge = jnp.where(
+        (col < 2) | (col >= 30),
+        own,
+        jnp.where(col < 4, own - 2 + shift, jnp.where(col >= 28, own + 2 + shift, lr)),
+    )
+    ids = jnp.where(
+        spot < PT,
+        own,
+        jnp.where(spot < 2 * PT, own + shift, jnp.where(spot < 3 * PT, lr, edge)),
+    )
     return jnp.where(ids >= 0, ids + 1, -10).astype(F32)
 
 
+def product(w_ref, hi, lo):
+    rows = dot(w_ref[...], hi)
+    return rows[0:W] + rows[W : 2 * W] + dot(w_ref[0:W, :], lo)
+
+
+def scaled_by_type(tw_ref, blocks, metas):
+    his, los = [], []
+    for v, meta in zip(blocks, metas):
+        hi, lo = split(v)
+        kind = meta[SLOTS : SLOTS + 1, :]
+        his.append([jnp.where(kind == float(k), hi, jnp.zeros_like(hi)) for k in range(KINDS)])
+        los.append([jnp.where(kind == float(k), lo, jnp.zeros_like(lo)) for k in range(KINDS)])
+
+    def by_part(pieces):
+        whole = [jnp.concatenate([p[k] for p in pieces], axis=1) for k in range(KINDS)]
+        return jnp.concatenate([w[0:HALF] for w in whole] + [w[HALF:W] for w in whole], axis=0)
+
+    s_hi, s_lo = split(product(tw_ref, by_part(his), by_part(los)))
+    return jnp.concatenate([s_hi, s_lo], axis=0)
+
+
+def one_hot(at, meta, s):
+    return jnp.where(at == meta[s : s + 1, :], 1.0, 0.0).astype(BF16)
+
+
+def place(refs, parts, s, lanes_at, lanes_from):
+    for ref, part in zip(refs, parts):
+        for half in range(2):
+            at = half * PART + s * HALF
+            ref[at : at + HALF, lanes_at] = part[half * HALF : (half + 1) * HALF, lanes_from]
+
+
+def clear_fill(refs):
+    for ref in refs:
+        for at in (SLOTS * HALF, PART + SLOTS * HALF):
+            rows = PART - SLOTS * HALF
+            ref[at : at + rows, :] = jnp.zeros((rows, ref.shape[1]), BF16)
+
+
+def scatter_pairs(refs, stack, ids, metas, lanes_at):
+    for s in range(0, SLOTS, 2):
+        pick = jnp.concatenate(
+            [
+                jnp.concatenate([one_hot(ids, meta, t) for meta in metas], axis=1)
+                for t in (s, s + 1)
+            ],
+            axis=0,
+        )
+        g = dot_nt(stack, pick)
+        parts = split(g[0:W] + g[W : 2 * W])
+        for t in (0, 1):
+            place(refs, parts, s + t, lanes_at, slice(t * PT, (t + 1) * PT))
+
+
+def gather_pairs(refs, blocks, ids, meta, lanes_at):
+    stack = jnp.concatenate(split(jnp.concatenate(blocks, axis=1)), axis=0)
+    for s in range(0, SLOTS, 2):
+        pick = jnp.concatenate([one_hot(ids, meta, s), one_hot(ids, meta, s + 1)], axis=1)
+        g = dot(stack, pick).astype(BF16)
+        for t in (0, 1):
+            place(
+                refs, (g[0:W], g[W : 2 * W]), s + t, lanes_at, slice(t * PT, (t + 1) * PT)
+            )
+
+
+def early_kernel(
+    stride,
+    tile_ref,
+    b_ref,
+    nb_ref,
+    pt_ref,
+    up_ref,
+    dn_ref,
+    fc_ref,
+    inc_ref,
+    tw_ref,
+    lw_ref,
+    fw_ref,
+    part_ref,
+    exc_ref,
+    ghi_ref,
+    glo_ref,
+):
+    m = slice(W, ROWS)
+    refs = (ghi_ref, glo_ref)
+    ids = target_ids(tile_ref[0] * PT, stride)
+    own = meta_rows(nb_ref, pt_ref)
+    metas = (own, up_ref[m, :], dn_ref[m, :])
+    clear_fill(refs)
+    stack = scaled_by_type(tw_ref, (b_ref[...], up_ref[0:W, :], dn_ref[0:W, :]), metas)
+    for s in range(SLOTS):
+        pick = jnp.concatenate([one_hot(ids[0 : 3 * PT, :], meta, s) for meta in metas], axis=1)
+        g = dot_nt(stack, pick)
+        place(refs, split(g[0:W] + g[W : 2 * W]), s, slice(0, 3 * PT), slice(0, 3 * PT))
+    part_ref[...] = product(lw_ref, ghi_ref[...], glo_ref[...])
+
+    fc_ud = unpack_fc(up_ref[ROWS : ROWS + HALF, :], dn_ref[ROWS : ROWS + HALF, :])
+    block = slice(0, PT)
+    gather_pairs(refs, (fc_ref[...], fc_ud), ids[0 : 2 * PT, :], own, block)
+    exc_ref[...] = inc_ref[...] + product(fw_ref, ghi_ref[:, block], glo_ref[:, block])
+
+
 def main_kernel(
-    base_ref,
+    stride,
+    tile_ref,
     b_ref,
     nb_ref,
     pt_ref,
@@ -170,8 +284,8 @@
     dn_ref,
     lf_ref,
     rt_ref,
-    fc_ref,
-    inc_ref,
+    part_ref,
+    exc_ref,
     tw_ref,
     lw_ref,
     fw_ref,
@@ -180,96 +294,41 @@
     glo_ref,
 ):
     m = slice(W, ROWS)
-    ids = target_ids(base_ref[0], base_ref[1])
-    own_ids = ids[0:PT, :]
-    first = lanes(META) < 64
+    refs = (ghi_ref, glo_ref)
+    ids = target_ids(tile_ref[0] * PT, stride)
     col = lanes(META) % 32
     b = b_ref[...]
-    m_own, m_up, m_dn = meta_rows(nb_ref, pt_ref), up_ref[m, :], dn_ref[m, :]
-    m_ud = jnp.where(first, m_dn, m_up)
-    wide = lanes(W) % 32 >= 16
+    m_own = meta_rows(nb_ref, pt_ref)
+    m_ud = jnp.where(lanes(META) < 64, dn_ref[m, :], up_ref[m, :])
     m_lr = jnp.where(col >= 16, lf_ref[m, :], rt_ref[m, :])
-    x_lr = jnp.where(wide, lf_ref[0:W, :], rt_ref[0:W, :])
+    wide = lanes(W) % 32
+    x_lr = jnp.where(wide >= 16, lf_ref[0:W, :], rt_ref[0:W, :])
     b_zone = (col < 12) | (col >= 20)
     row_id = lax.broadcasted_iota(jnp.int32, (META, PT), 0)
     m_b = jnp.where(b_zone | (row_id >= SLOTS), m_lr, 0.0)
     m_f = jnp.where(b_zone & (row_id < SLOTS), 0.0, m_lr)
-
-    def product(w_ref, hi, lo):
-        rows = dot(w_ref[...], hi)
-        return rows[0:W] + rows[W : 2 * W] + dot(w_ref[0:W, :], lo)
-
-    def scaled_by_type(blocks, metas):
-        his, los = [], []
-        for v, meta in zip(blocks, metas):
-            hi, lo = split(v)
-            kind = meta[SLOTS : SLOTS + 1, :]
-            his.append([jnp.where(kind == float(k), hi, jnp.zeros_like(hi)) for k in range(KINDS)])
-            los.append([jnp.where(kind == float(k), lo, jnp.zeros_like(lo)) for k in range(KINDS)])
-        def by_part(pieces):
-            whole = [jnp.concatenate([p[k] for p in pieces], axis=1) for k in range(KINDS)]
-            return jnp.concatenate([w[0:HALF] for w in whole] + [w[HALF:W] for w in whole], axis=0)
-
-        hi, lo = by_part(his), by_part(los)
-        s_hi, s_lo = split(product(tw_ref, hi, lo))
-        return jnp.concatenate([s_hi, s_lo], axis=0)
-
-    def one_hot(at, meta, s):
-        return jnp.where(at == meta[s : s + 1, :], 1.0, 0.0).astype(BF16)
-
-    for ref in (ghi_ref, glo_ref):
-        for at in (SLOTS * HALF, PART + SLOTS * HALF):
-            ref[at : at + PART - SLOTS * HALF, :] = jnp.zeros((PART - SLOTS * HALF, 3 * PT), BF16)
-
-    metas = (m_own, m_up, m_dn, m_b)
-    stack = scaled_by_type((b, up_ref[0:W, :], dn_ref[0:W, :], x_lr), metas)
-    for s in range(SLOTS):
-        pick = jnp.concatenate([one_hot(ids, meta, s) for meta in metas], axis=1)
-        g = dot_nt(stack, pick)
-        hi, lo = split(g[0:W] + g[W : 2 * W])
-        for ref, part in ((ghi_ref, hi), (glo_ref, lo)):
-            ref[s * HALF : (s + 1) * HALF, :] = part[0:HALF]
-            ref[PART + s * HALF : PART + (s + 1) * HALF, :] = part[HALF:W]
-    u1_all = product(lw_ref, ghi_ref[...], glo_ref[...])
-    u1 = u1_all[:, 0:PT]
+    clear_fill(refs)
+    first, second = slice(0, PT), slice(PT, 2 * PT)
+
+    stack = scaled_by_type(tw_ref, (x_lr,), (m_b,))
+    scatter_pairs(refs, stack, ids[3 * PT :, :], (m_b,), first)
+    edge = product(lw_ref, ghi_ref[:, first], glo_ref[:, first])
+    gather_pairs(refs, (x_lr,), ids[2 * PT : 3 * PT, :], m_own, second)
+    exc = exc_ref[...] + product(fw_ref, ghi_ref[:, second], glo_ref[:, second])
+    left, right = wide < 2, wide >= 30
+    u1 = part_ref[:, 0:PT] + jnp.where(left | right, edge, 0.0)
+    u1_ud = part_ref[:, PT : 2 * PT] + jnp.where(
+        left, pltpu.roll(edge, PT - 2, 1), jnp.where(right, pltpu.roll(edge, 2, 1), 0.0)
+    )
+    u1_lr = part_ref[:, 2 * PT :] + jnp.where((wide >= 12) & (wide < 20), edge, 0.0)
     vec_ref[0:W, :] = b
     vec_ref[W : 2 * W, :] = u1
+    vec_ref[2 * W : 3 * W, :] = exc
 
     metas = (m_own, m_ud, m_f)
-    stack = scaled_by_type([u1_all[:, i * PT : (i + 1) * PT] for i in range(3)], metas)
-    for s in range(0, SLOTS, 2):
-        pick = jnp.concatenate(
-            [
-                jnp.concatenate([one_hot(own_ids, meta, t) for meta in metas], axis=1)
-                for t in (s, s + 1)
-            ],
-            axis=0,
-        )
-        g = dot_nt(stack, pick)
-        hi, lo = split(g[0:W] + g[W : 2 * W])
-        for t in (0, 1):
-            at = (s + t) * HALF
-            for ref, part in ((ghi_ref, hi), (glo_ref, lo)):
-                ref[at : at + HALF, 0:PT] = part[0:HALF, t * PT : (t + 1) * PT]
-                ref[PART + at : PART + at + HALF, 0:PT] = part[HALF:W, t * PT : (t + 1) * PT]
-    u2 = product(lw_ref, ghi_ref[:, 0:PT], glo_ref[:, 0:PT])
-
-    fc_ud = unpack_fc(up_ref[ROWS : ROWS + HALF, :], dn_ref[ROWS : ROWS + HALF, :])
-    f_hi, f_lo = split(jnp.concatenate([fc_ref[...], fc_ud, x_lr], axis=1))
-    stack = jnp.concatenate([f_hi, f_lo], axis=0)
-    for s in range(0, SLOTS, 2):
-        pick = jnp.concatenate([one_hot(ids, m_own, s), one_hot(ids, m_own, s + 1)], axis=1)
-        g = dot(stack, pick).astype(BF16)
-        for t in (0, 1):
-            at = (s + t) * HALF
-            for ref, part in ((ghi_ref, g[0:W]), (glo_ref, g[W : 2 * W])):
-                ref[at : at + HALF, PT : 2 * PT] = part[0:HALF, t * PT : (t + 1) * PT]
-                ref[PART + at : PART + at + HALF, PT : 2 * PT] = part[
-                    HALF:W, t * PT : (t + 1) * PT
-                ]
-    exc = inc_ref[...] + product(fw_ref, ghi_ref[:, PT : 2 * PT], glo_ref[:, PT : 2 * PT])
-
-    vec_ref[2 * W : 3 * W, :] = exc
+    stack = scaled_by_type(tw_ref, (u1, u1_ud, u1_lr), metas)
+    scatter_pairs(refs, stack, ids[0:PT, :], metas, first)
+    u2 = product(lw_ref, ghi_ref[:, first], glo_ref[:, first])
 
     lane, row = lanes(8), lax.broadcasted_iota(jnp.int32, (8, PT), 0)
     gram = jnp.zeros((8, PT), F32)
@@ -278,7 +337,7 @@
     vec_ref[3 * W :, :] = jnp.where(row == 0, gram, m_own[SLOTS : SLOTS + 1, :])
 
 
-def outer_kernel(base_ref, own_ref, other_ref, chunk_ref):
+def outer_kernel(tile_ref, own_ref, other_ref, chunk_ref):
     def both(rows):
         return jnp.concatenate([own_ref[rows, :], other_ref[rows, :]], axis=1)
 
@@ -287,7 +346,7 @@
     v_hi, v_lo = split(both(slice(0, 2 * W)))
     kind = both(slice(3 * W + 1, 3 * W + 2))
     for k in range(2):
-        here = kind == (2 * base_ref[2] + k).astype(F32)
+        here = kind == (2 * lax.rem(tile_ref[0], 2) + k).astype(F32)
         k_hi = jnp.where(here, v_hi, jnp.zeros_like(v_hi))
         k_lo = jnp.where(here, v_lo, jnp.zeros_like(v_lo))
         out = dot_nt(k_hi, e_hi) + dot_nt(k_lo, e_hi) + dot_nt(k_hi, e_lo)
@@ -361,8 +420,8 @@
             out_ref[i, 48 * j : 48 * (j + 1), :] = rows
 
 
-def expand_kernel(base_ref, own_ref, other_ref, out_ref):
-    core = base_ref[2]
+def expand_kernel(tile_ref, own_ref, other_ref, out_ref):
+    core = lax.rem(tile_ref[0], 2)
     for ref, first in ((own_ref, 2 * core), (other_ref, 2 - 2 * core)):
         for k in range(2):
             for h in range(2):
@@ -409,9 +468,8 @@
 ):
     n_short = lax.axis_size("gy")
     tile = lax.axis_index("gx") * n_short + lax.axis_index("gy")
-    core = lax.axis_index("gy") % 2
-    base = jnp.stack([tile * PT, jnp.int32(n_short * PT), core]).astype(jnp.int32)
-
+    tile = tile.astype(jnp.int32).reshape(1)
+    stride = n_short * PT
     kinds = particle_type.reshape(1, PT)
     to_up, to_dn = call(
         pack_wide_kernel,
@@ -443,10 +501,31 @@
         dtype=BF16,
     )
 
+    scratch = pltpu.VMEM((2 * PART, 3 * PT), BF16)
+    part, exc = call(
+        functools.partial(early_kernel, stride),
+        [(W, 3 * PT), (W, PT)],
+        tile,
+        cost_grad,
+        neighbours,
+        kinds,
+        up,
+        dn,
+        forward_coeff,
+        incident,
+        tw,
+        lw,
+        fw,
+        smem=1,
+        mib=24,
+        us=4,
+        scratch_shapes=[scratch] * 2,
+    )
+    scratch = pltpu.VMEM((2 * PART, 2 * PT), BF16)
     (vectors,) = call(
-        main_kernel,
+        functools.partial(main_kernel, stride),
         [(3 * W + 8, PT)],
-        base,
+        tile,
         cost_grad,
         neighbours,
         kinds,
@@ -454,19 +533,20 @@
         dn,
         lf,
         rt,
-        forward_coeff,
-        incident,
+        part,
+        exc,
         tw,
         lw,
         fw,
         smem=1,
         mib=24,
-        scratch_shapes=[pltpu.VMEM((2 * PART, 3 * PT), BF16)] * 2,
+        us=4,
+        scratch_shapes=[scratch] * 2,
     )
     pairs = [(i, i ^ 1) for i in range(n_short)]
     lines = [list(range(c, n_short, 2)) for c in range(2)]
     partner = lax.ppermute(vectors, "gy", pairs)
-    (chunks,) = call(outer_kernel, [(4, CHUNK, PT)], base, vectors, partner, smem=1)
+    (chunks,) = call(outer_kernel, [(4, CHUNK, PT)], tile, vectors, partner, smem=1)
     got = lax.all_to_all(chunks, "gy", 0, 0, axis_index_groups=lines)
     (pieces,) = call(spread_kernel, [(512, PT)], got)
     got = lax.all_to_all(pieces.reshape(64, 8, PT), "gx", 0, 0)
@@ -475,7 +555,7 @@
     (copies,) = call(copies_kernel, [(4, 144, PT)], got.reshape(256, PT))
     half = lax.all_to_all(copies, "gy", 0, 0, axis_index_groups=lines)
     other = lax.ppermute(half, "gy", pairs)
-    (sensitivity,) = call(expand_kernel, [(KINDS, W, W)], base, half, other, smem=1)
+    (sensitivity,) = call(expand_kernel, [(KINDS, W, W)], tile, half, other, smem=1)
     return (adjoint, sensitivity)
 
 

time: 114 us -> 111 us (0.974)
  waiting for transfers between devices: 9.57 us -> 6.77 us
    ppermute x4, waiting for transfers between devices: 6.83 us -> 4.03 us  [shifted(): lax.ppermute(block, axis, [(i, i + step) for i in range(n) if 0 <= i + st...]
    pallas_call x9 -> x10, Pallas kernels: 14.2 us -> 14.6 us  [call(): pl.pallas_call(kernel, out_shape=[jax.ShapeDtypeStruct(s, dtype) for s in...]
  transfers between devices with their start and end apart: 6 -> 6, of which waited for: 5 -> 4; matrix products, arithmetic and copies ran while one was open for 0% -> 0% of each run, Pallas kernels for 1% -> 5%
where the time goes in v6:
time: 111 us
  blocking collectives  66 us (59%)
  starting transfers between devices  22.5 us (20%)
  Pallas kernels  14.6 us (13%)
  waiting for transfers between devices  6.77 us (6%)
    all_to_all x1, blocking collectives, body(): got = lax.all_to_all(pieces.reshape(64, 8, PT), 'gx', 0, 0)  28.8 us
    all_to_all x1, blocking collectives, body(): got = lax.all_to_all(mixed.reshape(64, 4, PT), 'gx', 0, 0)  16.5 us
    pallas_call x10, Pallas kernels, call(): pl.pallas_call(kernel, out_shape=[jax.ShapeDtypeStruct(s, dtype) for s in...  14.6 us
    ppermute x4, starting transfers between devices, shifted(): lax.ppermute(block, axis, [(i, i + step) for i in range(n) if 0 <= i + st...  13.8 us
    all_to_all x1, blocking collectives, body(): got = lax.all_to_all(chunks, 'gy', 0, 0, axis_index_groups=lines)  12.6 us
    all_to_all x1, blocking collectives, body(): half = lax.all_to_all(copies, 'gy', 0, 0, axis_index_groups=lines)  8.07 us
    ppermute x1, starting transfers between devices, body(): other = lax.ppermute(half, 'gy', pairs)  6.73 us
    ppermute x4, waiting for transfers between devices, shifted(): lax.ppermute(block, axis, [(i, i + step) for i in range(n) if 0 <= i + st...  4.03 us
  transfers between devices with their start and end apart: 6, of which 4 were waited for; matrix products, arithmetic and copies ran while one was open for 0% of the time, Pallas kernels for 5%

profile of v6, /device:TPU:1, one launch (start us, length us, event | category | flops | bytes accessed | tf_op | source)
XLA Modules:
  0.0 110.8 jit_solution(8473278016810967734)
XLA Ops:
  0.6 0.0 copy-start
  0.6 0.0 copy-start.1
  0.7 0.0 copy-start.2
  0.7 0.0 copy-start.3
  0.7 1.9 %shard_map.104 = (f32[304,128]{1,0:T(8,128)}, f32[304,128]{1,0:T(8,128)}) custom-call(f32[192,128]{1,0:T(8,128)} %fc_ref.3, f32[192,128]{1,0:T(8,128)} %b_ref.5, s32[10,128]{1,0:T(8,128)} %nb_ref.5, s32[1,128]{1,0:T(1,128)} %bitcast.10), custom_call_target="tpu_custom_call" | custom-call | flops 4000000000 | bytes 12000000 | tf_op jit(solution)/shard_map/pallas_call | solution.py:440
  2.5 4.0 %collective-permute-start = (f32[304,128]{1,0:T(8,128)}, f32[304,128]{1,0:T(8,128)S(1)}, u32[]{:S(2)}, u32[]{:S(2)}) collective-permute-start(f32[304,128]{1,0:T(8,128)} %get-tuple-element.13), channel_id=1, source_target_pairs={{0,8},{8,16},{16,24},{24,32},{32,40},{40,48},{48,56},{56,64},{64,7... | collective-permute-start | bytes 466952 | tf_op jit(solution)/shard_map/ppermute | solution.py:455
  6.6 1.3 %collective-permute-start.1 = (f32[304,128]{1,0:T(8,128)}, f32[304,128]{1,0:T(8,128)S(1)}, u32[]{:S(2)}, u32[]{:S(2)}) collective-permute-start(f32[304,128]{1,0:T(8,128)} %get-tuple-element.14), channel_id=1, source_target_pairs={{8,0},{16,8},{24,16},{32,24},{40,32},{48,40},{56,48},{64,56},{72,6... | collective-permute-start | bytes 466952 | tf_op jit(solution)/shard_map/ppermute | solution.py:455
  7.9 0.0 copy-done
  7.9 0.0 copy-done.1
  7.9 0.0 copy-done.2
  7.9 0.0 copy-done.3
  7.9 0.0 copy-start.4
  7.9 0.0 copy-start.6
  8.0 0.0 copy-start.7
  8.0 0.0 copy-start.8
  8.0 0.7 shard_map.106
  8.7 0.0 copy-start.5
  8.7 0.3 collective-permute-done.up_ref
  9.1 3.7 %collective-permute-done.1.dn_ref = f32[304,128]{1,0:T(8,128)S(1)} collective-permute-done((f32[304,128]{1,0:T(8,128)}, f32[304,128]{1,0:T(8,128)S(1)}, u32[]{:S(2)}, u32[]{:S(2)}) %collective-permute-start.1) | collective-permute-done | bytes 155680 | tf_op jit(solution)/shard_map/ppermute | solution.py:455
  12.8 0.0 copy-done.4
  12.8 0.0 copy-done.6
  12.8 0.0 copy-done.7
  12.8 0.0 copy-done.8
  12.8 0.3 shard_map.105
  13.1 5.4 %collective-permute-start.2 = (f32[208,128]{1,0:T(8,128)S(1)}, f32[208,128]{1,0:T(8,128)S(1)}, u32[]{:S(2)}, u32[]{:S(2)}) collective-permute-start(f32[208,128]{1,0:T(8,128)S(1)} %get-tuple-element.15), channel_id=1, source_target_pairs={{0,1},{1,2},{2,3},{3,4},{4,5},{5,6},{6,7},{8,9},{9,10},{10,11},{11... | collective-permute-start | bytes 319496 | tf_op jit(solution)/shard_map/ppermute | solution.py:455
  18.5 3.1 %collective-permute-start.3 = (f32[208,128]{1,0:T(8,128)S(1)}, f32[208,128]{1,0:T(8,128)S(1)}, u32[]{:S(2)}, u32[]{:S(2)}) collective-permute-start(f32[208,128]{1,0:T(8,128)S(1)} %get-tuple-element.16), channel_id=1, source_target_pairs={{1,0},{2,1},{3,2},{4,3},{5,4},{6,5},{7,6},{9,8},{10,9},{11,10},{12... | collective-permute-start | bytes 319496 | tf_op jit(solution)/shard_map/ppermute | solution.py:455
  21.6 0.0 copy-done.5
  21.6 4.8 %shard_map.107 = (f32[192,384]{1,0:T(8,128)S(1)}, f32[192,128]{1,0:T(8,128)S(1)}) custom-call(s32[1]{0:T(128)} %bitcast.tile_ref, f32[192,128]{1,0:T(8,128)S(1)} %copy-done.6, s32[10,128]{1,0:T(8,128)S(1)} %copy-done.7, s32[1,128]{1,0:T(1,128)S(1)} %bitcast.12, f32[304,128]{1,0:T(8,128)S(1)} %collective-permute-done.up_ref, ...), custom_call_target="tpu_custom_call" | custom-call | flops 4000000000 | bytes 12000000 | tf_op jit(solution)/shard_map/pallas_call | solution.py:440
  26.4 0.0 collective-permute-done.2.lf_ref
  26.4 0.0 collective-permute-done.3.rt_ref
  26.4 4.4 %shard_map.108.own_ref.vec_ref = f32[584,128]{1,0:T(8,128)S(1)} custom-call(s32[1]{0:T(128)} %bitcast.tile_ref, f32[192,128]{1,0:T(8,128)S(1)} %copy-done.6, s32[10,128]{1,0:T(8,128)S(1)} %copy-done.7, s32[1,128]{1,0:T(1,128)S(1)} %bitcast.13, f32[304,128]{1,0:T(8,128)S(1)} %collective-permute-done.up_ref, f32[304,128]{1,0:T(8,128)S(1)} %collective-permute-done.1.dn_ref, ...), custom_call_target="tpu_custom_call" | custom-call | flops 4000000000 | bytes 12000000 | tf_op jit(solution)/shard_map/pallas_call | solution.py:440
  30.8 1.9 %collective-permute-start.4 = (f32[584,128]{1,0:T(8,128)S(1)}, f32[584,128]{1,0:T(8,128)S(1)}, u32[]{:S(2)}, u32[]{:S(2)}) collective-permute-start(f32[584,128]{1,0:T(8,128)S(1)} %shard_map.108.own_ref.vec_ref), channel_id=1, source_target_pairs={{0,1},{1,0},{2,3},{3,2},{4,5},{5,4},{6,7},{7,6},{8,9},{9,8},{10,11... | collective-permute-start | bytes 897032 | tf_op jit(solution)/shard_map/ppermute | solution.py:548
  32.7 1.6 %collective-permute-done.4.other_ref = f32[584,128]{1,0:T(8,128)S(1)} collective-permute-done((f32[584,128]{1,0:T(8,128)S(1)}, f32[584,128]{1,0:T(8,128)S(1)}, u32[]{:S(2)}, u32[]{:S(2)}) %collective-permute-start.4) | collective-permute-done | bytes 299040 | tf_op jit(solution)/shard_map/ppermute | solution.py:548
  34.3 0.6 shard_map.109
  34.9 12.6 %all_to_all.20.in_ref = f32[4,296,128]{2,1,0:T(8,128)S(1)} all-to-all(f32[4,296,128]{2,1,0:T(8,128)S(1)} %shard_map.109), channel_id=1, replica_groups={{0,2,4,6},{1,3,5,7},{8,10,12,14},{9,11,13,15},{16,18,20,22},{17,19,21,2..., dimensions={0} | all-to-all | bytes 1212416 | tf_op jit(solution)/shard_map/all_to_all | solution.py:550
  47.5 0.1 shard_map.110
  47.5 28.8 %all_to_all.21 = f32[64,8,128]{2,1,0:T(8,128)S(1)} all-to-all(f32[64,8,128]{2,1,0:T(8,128)S(1)} %bitcast.7), channel_id=1, replica_groups=mesh['gx'=64,'gy'=8] {'gx'}, dimensions={0} | all-to-all | bytes 524288 | tf_op jit(solution)/shard_map/all_to_all | solution.py:552
  76.4 0.9 shard_map.111
  77.2 16.5 %all_to_all.22 = f32[64,4,128]{2,1,0:T(4,128)S(1)} all-to-all(f32[64,4,128]{2,1,0:T(4,128)S(1)} %bitcast.8), channel_id=1, replica_groups=mesh['gx'=64,'gy'=8] {'gx'}, dimensions={0} | all-to-all | bytes 262144 | tf_op jit(solution)/shard_map/all_to_all | solution.py:554
  93.8 8.1 %all_to_all.23.own_ref = f32[4,144,128]{2,1,0:T(8,128)S(1)} all-to-all(f32[4,144,128]{2,1,0:T(8,128)S(1)} %shard_map.112), channel_id=1, replica_groups={{0,2,4,6},{1,3,5,7},{8,10,12,14},{9,11,13,15},{16,18,20,22},{17,19,21,2..., dimensions={0} | all-to-all | bytes 589824 | tf_op jit(solution)/shard_map/all_to_all | solution.py:556
  101.9 6.7 %collective-permute-start.5 = (f32[4,144,128]{2,1,0:T(8,128)S(1)}, f32[4,144,128]{2,1,0:T(8,128)S(1)}, u32[]{:S(2)}, u32[]{:S(2)}) collective-permute-start(f32[4,144,128]{2,1,0:T(8,128)S(1)} %all_to_all.23.own_ref), channel_id=1, source_target_pairs={{0,1},{1,0},{2,3},{3,2},{4,5},{5,4},{6,7},{7,6},{8,9},{9,8},{10,11... | collective-permute-start | bytes 884744 | tf_op jit(solution)/shard_map/ppermute | solution.py:557
  108.6 1.2 %collective-permute-done.5.other_ref = f32[4,144,128]{2,1,0:T(8,128)S(1)} collective-permute-done((f32[4,144,128]{2,1,0:T(8,128)S(1)}, f32[4,144,128]{2,1,0:T(8,128)S(1)}, u32[]{:S(2)}, u32[]{:S(2)}) %collective-permute-start.5) | collective-permute-done | bytes 294944 | tf_op jit(solution)/shard_map/ppermute | solution.py:557
  109.8 1.0 shard_map.113
  (1 shorter events, 0.0 us)
Async XLA Ops:
  0.6 7.3 %copy-start = (f32[10,96,96]{2,1,0:T(8,128)S(1)}, f32[10,96,96]{2,1,0:T(8,128)}, u32[]{:S(2)}) copy-start(f32[10,96,96]{2,1,0:T(8,128)} %lr_ref.1) | copy-start | bytes 1105924
  0.6 7.3 %copy-start.1 = (f32[10,96,96]{2,1,0:T(8,128)S(1)}, f32[10,96,96]{2,1,0:T(8,128)}, u32[]{:S(2)}) copy-start(f32[10,96,96]{2,1,0:T(8,128)} %li_ref.1) | copy-start | bytes 1105924
  0.7 7.3 %copy-start.2 = (f32[4,96,96]{2,1,0:T(8,128)S(1)}, f32[4,96,96]{2,1,0:T(8,128)}, u32[]{:S(2)}) copy-start(f32[4,96,96]{2,1,0:T(8,128)} %tr_ref.1) | copy-start | bytes 442372
  0.7 7.3 %copy-start.3 = (f32[4,96,96]{2,1,0:T(8,128)S(1)}, f32[4,96,96]{2,1,0:T(8,128)}, u32[]{:S(2)}) copy-start(f32[4,96,96]{2,1,0:T(8,128)} %ti_ref.1) | copy-start | bytes 442372
  2.5 6.5 %collective-permute-start = (f32[304,128]{1,0:T(8,128)}, f32[304,128]{1,0:T(8,128)S(1)}, u32[]{:S(2)}, u32[]{:S(2)}) collective-permute-start(f32[304,128]{1,0:T(8,128)} %get-tuple-element.13), channel_id=1, source_target_pairs={{0,8},{8,16},{16,24},{24,32},{32,40},{40,48},{48,56},{56,64},{64,7... | collective-permute-start | bytes 466952 | tf_op jit(solution)/shard_map/ppermute | solution.py:455
  6.6 6.2 %collective-permute-start.1 = (f32[304,128]{1,0:T(8,128)}, f32[304,128]{1,0:T(8,128)S(1)}, u32[]{:S(2)}, u32[]{:S(2)}) collective-permute-start(f32[304,128]{1,0:T(8,128)} %get-tuple-element.14), channel_id=1, source_target_pairs={{8,0},{16,8},{24,16},{32,24},{40,32},{48,40},{56,48},{64,56},{72,6... | collective-permute-start | bytes 466952 | tf_op jit(solution)/shard_map/ppermute | solution.py:455
  7.9 4.8 %copy-start.4 = (f32[192,128]{1,0:T(8,128)S(1)}, f32[192,128]{1,0:T(8,128)}, u32[]{:S(2)}) copy-start(f32[192,128]{1,0:T(8,128)} %fc_ref.3) | copy-start | bytes 294916
  7.9 4.8 %copy-start.6 = (f32[192,128]{1,0:T(8,128)S(1)}, f32[192,128]{1,0:T(8,128)}, u32[]{:S(2)}) copy-start(f32[192,128]{1,0:T(8,128)} %b_ref.5) | copy-start | bytes 294916
  8.0 4.8 %copy-start.7 = (s32[10,128]{1,0:T(8,128)S(1)}, s32[10,128]{1,0:T(8,128)}, u32[]{:S(2)}) copy-start(s32[10,128]{1,0:T(8,128)} %nb_ref.5) | copy-start | bytes 15364
  8.0 4.8 %copy-start.8 = (s32[128]{0:T(128)S(1)}, s32[128]{0:T(128)}, u32[]{:S(2)}) copy-start(s32[128]{0:T(128)} %param.17) | copy-start | bytes 1540
  8.7 12.9 %copy-start.5 = (f32[192,128]{1,0:T(8,128)S(1)}, f32[192,128]{1,0:T(8,128)}, u32[]{:S(2)}) copy-start(f32[192,128]{1,0:T(8,128)} %inc_ref.1) | copy-start | bytes 294916
  13.1 13.3 %collective-permute-start.2 = (f32[208,128]{1,0:T(8,128)S(1)}, f32[208,128]{1,0:T(8,128)S(1)}, u32[]{:S(2)}, u32[]{:S(2)}) collective-permute-start(f32[208,128]{1,0:T(8,128)S(1)} %get-tuple-element.15), channel_id=1, source_target_pairs={{0,1},{1,2},{2,3},{3,4},{4,5},{5,6},{6,7},{8,9},{9,10},{10,11},{11... | collective-permute-start | bytes 319496 | tf_op jit(solution)/shard_map/ppermute | solution.py:455
  18.5 8.0 %collective-permute-start.3 = (f32[208,128]{1,0:T(8,128)S(1)}, f32[208,128]{1,0:T(8,128)S(1)}, u32[]{:S(2)}, u32[]{:S(2)}) collective-permute-start(f32[208,128]{1,0:T(8,128)S(1)} %get-tuple-element.16), channel_id=1, source_target_pairs={{1,0},{2,1},{3,2},{4,3},{5,4},{6,5},{7,6},{9,8},{10,9},{11,10},{12... | collective-permute-start | bytes 319496 | tf_op jit(solution)/shard_map/ppermute | solution.py:455
  30.8 3.5 %collective-permute-start.4 = (f32[584,128]{1,0:T(8,128)S(1)}, f32[584,128]{1,0:T(8,128)S(1)}, u32[]{:S(2)}, u32[]{:S(2)}) collective-permute-start(f32[584,128]{1,0:T(8,128)S(1)} %shard_map.108.own_ref.vec_ref), channel_id=1, source_target_pairs={{0,1},{1,0},{2,3},{3,2},{4,5},{5,4},{6,7},{7,6},{8,9},{9,8},{10,11... | collective-permute-start | bytes 897032 | tf_op jit(solution)/shard_map/ppermute | solution.py:548
  101.9 7.9 %collective-permute-start.5 = (f32[4,144,128]{2,1,0:T(8,128)S(1)}, f32[4,144,128]{2,1,0:T(8,128)S(1)}, u32[]{:S(2)}, u32[]{:S(2)}) collective-permute-start(f32[4,144,128]{2,1,0:T(8,128)S(1)} %all_to_all.23.own_ref), channel_id=1, source_target_pairs={{0,1},{1,0},{2,3},{3,2},{4,5},{5,4},{6,7},{7,6},{8,9},{9,8},{10,11... | collective-permute-start | bytes 884744 | tf_op jit(solution)/shard_map/ppermute | solution.py:557

commit v7 on v6

--- a/solution.py
+++ b/solution.py
@@ -60,18 +60,29 @@
     )
 
 
-def pack_wide_kernel(*refs):
-    up_ref, dn_ref = refs[4:6]
-    fc_ref, b_ref, nb_ref, pt_ref = refs[6:10]
-    fetch(refs[0:4], refs[6:10], refs[10])
+def even_row(short, tile_ref):
+    return lax.rem(lax.div(tile_ref[0], short), 2) == 0
+
+
+def even_col(tile_ref):
+    return lax.rem(tile_ref[0], 2) == 0
+
+
+def pack_wide_kernel(short, *refs):
+    even = even_row(short, refs[0])
+    one_ref, two_ref = refs[5:7]
+    fc_ref, b_ref, nb_ref, pt_ref = refs[7:11]
+    fetch(refs[1:5], refs[7:11], refs[11])
     meta = meta_rows(nb_ref, pt_ref)
     top, low = fc_ref[0:HALF, :], fc_ref[HALF:W, :]
     first = lanes(HALF) < 64
-    for ref in (up_ref, dn_ref):
+    for ref in (one_ref, two_ref):
         ref[0:W, :] = b_ref[...]
         ref[W:ROWS, :] = meta
-    up_ref[ROWS : ROWS + HALF, :] = jnp.where(first, pltpu.roll(top, 64, 1), low)
-    dn_ref[ROWS : ROWS + HALF, :] = jnp.where(first, top, pltpu.roll(low, 64, 1))
+    up = jnp.where(first, pltpu.roll(top, 64, 1), low)
+    dn = jnp.where(first, top, pltpu.roll(low, 64, 1))
+    one_ref[ROWS : ROWS + HALF, :] = jnp.where(even, up, dn)
+    two_ref[ROWS : ROWS + HALF, :] = jnp.where(even, dn, up)
 
 
 def unpack_fc(up, dn):
@@ -85,10 +96,26 @@
     )
 
 
-def pack_short_kernel(fc_ref, b_ref, nb_ref, pt_ref, up_ref, dn_ref, lo_ref, hi_ref):
+class Tiles:
+    def __init__(self, even, one_ref, two_ref):
+        self.even, self.one, self.two = even, one_ref, two_ref
+
+    def below(self, rows):
+        return jnp.where(self.even, self.two[rows, :], self.one[rows, :])
+
+    def above(self, rows):
+        return jnp.where(self.even, self.one[rows, :], self.two[rows, :])
+
+
+def pack_short_kernel(
+    short, tile_ref, fc_ref, b_ref, nb_ref, pt_ref, x1_ref, x2_ref, one_ref, two_ref
+):
+    wide = Tiles(even_row(short, tile_ref), x1_ref, x2_ref)
+    even = even_col(tile_ref)
+    half = slice(ROWS, ROWS + HALF)
     first = lanes(META) < 64
     meta = meta_rows(nb_ref, pt_ref)
-    fc_ud = unpack_fc(up_ref[ROWS : ROWS + HALF, :], dn_ref[ROWS : ROWS + HALF, :])
+    fc_ud = unpack_fc(wide.below(half), wide.above(half))
 
     def part(rows, tiles):
         col = lanes(rows.stop - rows.start) % 32
@@ -101,17 +128,19 @@
         low = jnp.where(col < 4, low, moved(own, 4))
         low = jnp.where(col < 8, low, moved(dn, 8))
         low = jnp.where(col < 12, low, moved(edge, 12))
-        lo_ref[rows, :] = jnp.where(col < 14, low, moved(edge_ud, 14))
+        low = jnp.where(col < 14, low, moved(edge_ud, 14))
         high = moved(edge, 114)
         high = jnp.where(col < 18, high, moved(edge_ud, 116))
         high = jnp.where(col < 20, high, moved(up, 120))
         high = jnp.where(col < 24, high, moved(own, 124))
-        hi_ref[rows, :] = jnp.where(col < 28, high, dn)
-
-    part(slice(0, W), (up_ref[0:W, :], b_ref[...], dn_ref[0:W, :], fc_ref[...], fc_ud))
-    m = slice(W, ROWS)
-    meta_ud = jnp.where(first, dn_ref[m, :], up_ref[m, :])
-    part(m, (up_ref[m, :], meta, dn_ref[m, :], meta, meta_ud))
+        high = jnp.where(col < 28, high, dn)
+        one_ref[rows, :] = jnp.where(even, high, low)
+        two_ref[rows, :] = jnp.where(even, low, high)
+
+    v, m = slice(0, W), slice(W, ROWS)
+    part(v, (wide.below(v), b_ref[...], wide.above(v), fc_ref[...], fc_ud))
+    meta_up, meta_dn = wide.below(m), wide.above(m)
+    part(m, (meta_up, meta, meta_dn, meta, jnp.where(first, meta_dn, meta_up)))
 
 
 def weight_kernel(tr_ref, ti_ref, lr_ref, li_ref, tw_ref, lw_ref, fw_ref):
@@ -215,7 +244,7 @@
     for s in range(0, SLOTS, 2):
         pick = jnp.concatenate(
             [
-                jnp.concatenate([one_hot(ids, meta, t) for meta in metas], axis=1)
+                jnp.concatenate([one_hot(at, meta, t) for at, meta in zip(ids, metas)], axis=1)
                 for t in (s, s + 1)
             ],
             axis=0,
@@ -238,54 +267,56 @@
 
 
 def early_kernel(
-    stride,
+    short,
     tile_ref,
     b_ref,
     nb_ref,
     pt_ref,
-    up_ref,
-    dn_ref,
+    x1_ref,
+    x2_ref,
     fc_ref,
-    inc_ref,
     tw_ref,
     lw_ref,
-    fw_ref,
     part_ref,
-    exc_ref,
+    stack_ref,
+    fhi_ref,
+    flo_ref,
     ghi_ref,
     glo_ref,
 ):
-    m = slice(W, ROWS)
-    refs = (ghi_ref, glo_ref)
-    ids = target_ids(tile_ref[0] * PT, stride)
+    wide = Tiles(even_row(short, tile_ref), x1_ref, x2_ref)
+    v, m, half = slice(0, W), slice(W, ROWS), slice(ROWS, ROWS + HALF)
+    refs, gathered = (ghi_ref, glo_ref), (fhi_ref, flo_ref)
+    ids = target_ids(tile_ref[0] * PT, short * PT)[0 : 2 * PT, :]
     own = meta_rows(nb_ref, pt_ref)
-    metas = (own, up_ref[m, :], dn_ref[m, :])
-    clear_fill(refs)
-    stack = scaled_by_type(tw_ref, (b_ref[...], up_ref[0:W, :], dn_ref[0:W, :]), metas)
+    metas = (own, wide.below(m), wide.above(m))
+    clear_fill(refs + gathered)
+    stack = scaled_by_type(tw_ref, (b_ref[...], wide.below(v), wide.above(v)), metas)
+    stack_ref[...] = stack
     for s in range(SLOTS):
-        pick = jnp.concatenate([one_hot(ids[0 : 3 * PT, :], meta, s) for meta in metas], axis=1)
+        pick = jnp.concatenate([one_hot(ids, meta, s) for meta in metas], axis=1)
         g = dot_nt(stack, pick)
-        place(refs, split(g[0:W] + g[W : 2 * W]), s, slice(0, 3 * PT), slice(0, 3 * PT))
+        place(refs, split(g[0:W] + g[W : 2 * W]), s, slice(0, 2 * PT), slice(0, 2 * PT))
     part_ref[...] = product(lw_ref, ghi_ref[...], glo_ref[...])
-
-    fc_ud = unpack_fc(up_ref[ROWS : ROWS + HALF, :], dn_ref[ROWS : ROWS + HALF, :])
-    block = slice(0, PT)
-    gather_pairs(refs, (fc_ref[...], fc_ud), ids[0 : 2 * PT, :], own, block)
-    exc_ref[...] = inc_ref[...] + product(fw_ref, ghi_ref[:, block], glo_ref[:, block])
+    fc_ud = unpack_fc(wide.below(half), wide.above(half))
+    gather_pairs(gathered, (fc_ref[...], fc_ud), ids, own, slice(0, PT))
 
 
 def main_kernel(
-    stride,
+    short,
     tile_ref,
     b_ref,
     nb_ref,
     pt_ref,
-    up_ref,
-    dn_ref,
-    lf_ref,
-    rt_ref,
+    inc_ref,
+    x1_ref,
+    x2_ref,
+    y1_ref,
+    y2_ref,
     part_ref,
-    exc_ref,
+    stack_ref,
+    fhi_ref,
+    flo_ref,
     tw_ref,
     lw_ref,
     fw_ref,
@@ -293,41 +324,50 @@
     ghi_ref,
     glo_ref,
 ):
-    m = slice(W, ROWS)
+    rows = Tiles(even_row(short, tile_ref), x1_ref, x2_ref)
+    cols = Tiles(even_col(tile_ref), y1_ref, y2_ref)
+    v, m = slice(0, W), slice(W, ROWS)
     refs = (ghi_ref, glo_ref)
-    ids = target_ids(tile_ref[0] * PT, stride)
+    ids = target_ids(tile_ref[0] * PT, short * PT)
     col = lanes(META) % 32
     b = b_ref[...]
     m_own = meta_rows(nb_ref, pt_ref)
-    m_ud = jnp.where(lanes(META) < 64, dn_ref[m, :], up_ref[m, :])
-    m_lr = jnp.where(col >= 16, lf_ref[m, :], rt_ref[m, :])
-    wide = lanes(W) % 32
-    x_lr = jnp.where(wide >= 16, lf_ref[0:W, :], rt_ref[0:W, :])
+    m_up, m_dn = rows.below(m), rows.above(m)
+    m_ud = jnp.where(lanes(META) < 64, m_dn, m_up)
+    m_lr = jnp.where(col >= 16, cols.below(m), cols.above(m))
+    spot = lanes(W) % 32
+    x_lr = jnp.where(spot >= 16, cols.below(v), cols.above(v))
     b_zone = (col < 12) | (col >= 20)
     row_id = lax.broadcasted_iota(jnp.int32, (META, PT), 0)
     m_b = jnp.where(b_zone | (row_id >= SLOTS), m_lr, 0.0)
     m_f = jnp.where(b_zone & (row_id < SLOTS), 0.0, m_lr)
     clear_fill(refs)
     first, second = slice(0, PT), slice(PT, 2 * PT)
-
-    stack = scaled_by_type(tw_ref, (x_lr,), (m_b,))
-    scatter_pairs(refs, stack, ids[3 * PT :, :], (m_b,), first)
+    own_ids, lr_ids, edge_ids = ids[0:PT, :], ids[2 * PT : 3 * PT, :], ids[3 * PT :, :]
+
+    stack = jnp.concatenate([stack_ref[...], scaled_by_type(tw_ref, (x_lr,), (m_b,))], axis=1)
+    scatter_pairs(
+        refs, stack, (lr_ids, lr_ids, lr_ids, edge_ids), (m_own, m_up, m_dn, m_b), first
+    )
     edge = product(lw_ref, ghi_ref[:, first], glo_ref[:, first])
-    gather_pairs(refs, (x_lr,), ids[2 * PT : 3 * PT, :], m_own, second)
-    exc = exc_ref[...] + product(fw_ref, ghi_ref[:, second], glo_ref[:, second])
-    left, right = wide < 2, wide >= 30
-    u1 = part_ref[:, 0:PT] + jnp.where(left | right, edge, 0.0)
-    u1_ud = part_ref[:, PT : 2 * PT] + jnp.where(
+    left, right = spot < 2, spot >= 30
+    u1 = part_ref[:, first] + jnp.where(left | right, edge, 0.0)
+    u1_ud = part_ref[:, second] + jnp.where(
         left, pltpu.roll(edge, PT - 2, 1), jnp.where(right, pltpu.roll(edge, 2, 1), 0.0)
     )
-    u1_lr = part_ref[:, 2 * PT :] + jnp.where((wide >= 12) & (wide < 20), edge, 0.0)
+    u1_lr = jnp.where((spot >= 12) & (spot < 20), edge, 0.0)
+
+    gather_pairs(refs, (x_lr,), lr_ids, m_own, second)
+    exc = inc_ref[...] + product(
+        fw_ref, ghi_ref[:, second] + fhi_ref[...], glo_ref[:, second] + flo_ref[...]
+    )
     vec_ref[0:W, :] = b
     vec_ref[W : 2 * W, :] = u1
     vec_ref[2 * W : 3 * W, :] = exc
 
     metas = (m_own, m_ud, m_f)
     stack = scaled_by_type(tw_ref, (u1, u1_ud, u1_lr), metas)
-    scatter_pairs(refs, stack, ids[0:PT, :], metas, first)
+    scatter_pairs(refs, stack, (own_ids,) * 3, metas, first)
     u2 = product(lw_ref, ghi_ref[:, first], glo_ref[:, first])
 
     lane, row = lanes(8), lax.broadcasted_iota(jnp.int32, (8, PT), 0)
@@ -435,11 +475,14 @@
 
 def call(kernel, shapes, *args, smem=0, mib=6, dtype=F32, fetched=False, us=1, **kw):
     if fetched:
-        kw["scratch_shapes"] = [pltpu.VMEM(a.shape, a.dtype) for a in args]
-        kw["scratch_shapes"].append(pltpu.SemaphoreType.DMA((len(args),)))
+        kw["scratch_shapes"] = [pltpu.VMEM(a.shape, a.dtype) for a in args[smem:]]
+        kw["scratch_shapes"].append(pltpu.SemaphoreType.DMA((len(args) - smem,)))
     return pl.pallas_call(
         kernel,
-        out_shape=[jax.ShapeDtypeStruct(s, dtype) for s in shapes],
+        out_shape=[
+            s if isinstance(s, jax.ShapeDtypeStruct) else jax.ShapeDtypeStruct(s, dtype)
+            for s in shapes
+        ],
         in_specs=[pl.BlockSpec(memory_space=pltpu.SMEM)] * smem
         + [pl.BlockSpec(memory_space=pltpu.HBM if fetched else pltpu.VMEM)] * (len(args) - smem),
         cost_estimate=pl.CostEstimate(
@@ -450,9 +493,11 @@
     )(*args)
 
 
-def shifted(block, axis, step):
+def swapped(one, two, axis):
     n = lax.axis_size(axis)
-    return lax.ppermute(block, axis, [(i, i + step) for i in range(n) if 0 <= i + step < n])
+    near = [(i, i ^ 1) for i in range(n)]
+    far = [(i, i - 1 if i % 2 == 0 else i + 1) for i in range(1, n - 1)]
+    return lax.ppermute(one, axis, near), lax.ppermute(two, axis, far)
 
 
 def body(
@@ -469,26 +514,34 @@
     n_short = lax.axis_size("gy")
     tile = lax.axis_index("gx") * n_short + lax.axis_index("gy")
     tile = tile.astype(jnp.int32).reshape(1)
-    stride = n_short * PT
     kinds = particle_type.reshape(1, PT)
-    to_up, to_dn = call(
-        pack_wide_kernel,
+    one, two = call(
+        functools.partial(pack_wide_kernel, n_short),
         [(ROWS + HALF, PT)] * 2,
+        tile,
         forward_coeff,
         cost_grad,
         neighbours,
         kinds,
+        smem=1,
         mib=60,
         us=4,
         fetched=True,
     )
-    up = shifted(to_up, "gx", 1)
-    dn = shifted(to_dn, "gx", -1)
-    to_lo, to_hi = call(
-        pack_short_kernel, [(ROWS, PT)] * 2, forward_coeff, cost_grad, neighbours, kinds, up, dn
-    )
-    lf = shifted(to_hi, "gy", 1)
-    rt = shifted(to_lo, "gy", -1)
+    x1, x2 = swapped(one, two, "gx")
+    one, two = call(
+        functools.partial(pack_short_kernel, n_short),
+        [(ROWS, PT)] * 2,
+        tile,
+        forward_coeff,
+        cost_grad,
+        neighbours,
+        kinds,
+        x1,
+        x2,
+        smem=1,
+    )
+    y1, y2 = swapped(one, two, "gy")
 
     tw, lw, fw = call(
         weight_kernel,
@@ -501,47 +554,45 @@
         dtype=BF16,
     )
 
-    scratch = pltpu.VMEM((2 * PART, 3 * PT), BF16)
-    part, exc = call(
-        functools.partial(early_kernel, stride),
-        [(W, 3 * PT), (W, PT)],
+    scratch = [pltpu.VMEM((2 * PART, 2 * PT), BF16)] * 2
+    early = call(
+        functools.partial(early_kernel, n_short),
+        [(W, 2 * PT), jax.ShapeDtypeStruct((2 * W, 3 * PT), BF16)]
+        + [jax.ShapeDtypeStruct((2 * PART, PT), BF16)] * 2,
         tile,
         cost_grad,
         neighbours,
         kinds,
-        up,
-        dn,
+        x1,
+        x2,
         forward_coeff,
+        tw,
+        lw,
+        smem=1,
+        mib=24,
+        us=4,
+        scratch_shapes=scratch,
+    )
+    (vectors,) = call(
+        functools.partial(main_kernel, n_short),
+        [(3 * W + 8, PT)],
+        tile,
+        cost_grad,
+        neighbours,
+        kinds,
         incident,
+        x1,
+        x2,
+        y1,
+        y2,
+        *early,
         tw,
         lw,
         fw,
         smem=1,
         mib=24,
         us=4,
-        scratch_shapes=[scratch] * 2,
-    )
-    scratch = pltpu.VMEM((2 * PART, 2 * PT), BF16)
-    (vectors,) = call(
-        functools.partial(main_kernel, stride),
-        [(3 * W + 8, PT)],
-        tile,
-        cost_grad,
-        neighbours,
-        kinds,
-        up,
-        dn,
-        lf,
-        rt,
-        part,
-        exc,
-        tw,
-        lw,
-        fw,
-        smem=1,
-        mib=24,
-        us=4,
-        scratch_shapes=[scratch] * 2,
+        scratch_shapes=scratch,
     )
     pairs = [(i, i ^ 1) for i in range(n_short)]
     lines = [list(range(c, n_short, 2)) for c in range(2)]

time: 111 us -> 110 us (level)
  starting transfers between devices: 22.5 us -> 24.7 us
  waiting for transfers between devices: 6.77 us -> 4.85 us
  Pallas kernels: 14.6 us -> 13.1 us
    ppermute x4, starting transfers between devices: 13.8 us -> 16 us  [swapped(): return (lax.ppermute(one, axis, near), lax.ppermute(two, axis, far))]
    ppermute x4, waiting for transfers between devices: 4.03 us -> 2.11 us  [swapped(): return (lax.ppermute(one, axis, near), lax.ppermute(two, axis, far))]
    pallas_call x10, Pallas kernels: 14.6 us -> 13.1 us  [call(): pl.pallas_call(kernel, out_shape=[s if isinstance(s, jax.ShapeDtypeStruct...]
  transfers between devices with their start and end apart: 6 -> 6, of which waited for: 4 -> 4; matrix products, arithmetic and copies ran while one was open for 0% -> 0% of each run, Pallas kernels for 5% -> 4%
where the time goes in v7:
time: 110 us; the launch traced here: 109 us
  blocking collectives  65.6 us (60%)
  starting transfers between devices  24.7 us (22%)
  Pallas kernels  13.1 us (12%)
  waiting for transfers between devices  4.85 us (4%)
    all_to_all x1, blocking collectives, body(): got = lax.all_to_all(pieces.reshape(64, 8, PT), 'gx', 0, 0)  28.3 us
    all_to_all x1, blocking collectives, body(): got = lax.all_to_all(mixed.reshape(64, 4, PT), 'gx', 0, 0)  16.5 us
    ppermute x4, starting transfers between devices, swapped(): return (lax.ppermute(one, axis, near), lax.ppermute(two, axis, far))  16 us
    pallas_call x10, Pallas kernels, call(): pl.pallas_call(kernel, out_shape=[s if isinstance(s, jax.ShapeDtypeStruct...  13.1 us
    all_to_all x1, blocking collectives, body(): got = lax.all_to_all(chunks, 'gy', 0, 0, axis_index_groups=lines)  12.7 us
    all_to_all x1, blocking collectives, body(): half = lax.all_to_all(copies, 'gy', 0, 0, axis_index_groups=lines)  8.07 us
    ppermute x1, starting transfers between devices, body(): other = lax.ppermute(half, 'gy', pairs)  6.73 us
  transfers between devices with their start and end apart: 6, of which 4 were waited for; matrix products, arithmetic and copies ran while one was open for 0% of the time, Pallas kernels for 4%

profile of v7, /device:TPU:1, one launch (start us, length us, event | category | flops | bytes accessed | tf_op | source)
XLA Modules:
  0.0 109.2 jit_solution(11448429871185540668)
XLA Ops:
  0.6 0.0 copy-start
  0.6 0.0 copy-start.1
  0.7 0.0 copy-start.2
  0.7 0.0 copy-start.3
  0.7 1.9 %shard_map.104 = (f32[304,128]{1,0:T(8,128)}, f32[304,128]{1,0:T(8,128)}) custom-call(s32[1]{0:T(128)} %bitcast.refs_0_.tile_ref, f32[192,128]{1,0:T(8,128)} %fc_ref.3, f32[192,128]{1,0:T(8,128)} %b_ref.5, s32[10,128]{1,0:T(8,128)} %nb_ref.5, s32[1,128]{1,0:T(1,128)} %bitcast.10), custom_call_target="tpu_custom_call" | custom-call | flops 4000000000 | bytes 12000000 | tf_op jit(solution)/shard_map/pallas_call | solution.py:480
  2.6 4.0 %collective-permute-start = (f32[304,128]{1,0:T(8,128)}, f32[304,128]{1,0:T(8,128)S(1)}, u32[]{:S(2)}, u32[]{:S(2)}) collective-permute-start(f32[304,128]{1,0:T(8,128)} %get-tuple-element.15), channel_id=1, source_target_pairs={{0,8},{8,0},{16,24},{24,16},{32,40},{40,32},{48,56},{56,48},{64,72... | collective-permute-start | bytes 466952 | tf_op jit(solution)/shard_map/ppermute | solution.py:500
  6.6 0.0 copy-start.4
  6.6 0.0 copy-start.5
  6.6 0.0 copy-start.7
  6.6 0.0 copy-start.8
  6.7 0.8 collective-permute-start.1
  7.5 0.0 copy-done
  7.5 0.0 copy-done.1
  7.5 0.0 copy-done.2
  7.5 0.0 copy-done.3
  7.5 0.7 shard_map.106
  8.3 1.2 %collective-permute-done.x1_ref = f32[304,128]{1,0:T(8,128)S(1)} collective-permute-done((f32[304,128]{1,0:T(8,128)}, f32[304,128]{1,0:T(8,128)S(1)}, u32[]{:S(2)}, u32[]{:S(2)}) %collective-permute-start) | collective-permute-done | bytes 155680 | tf_op jit(solution)/shard_map/ppermute | solution.py:500
  9.4 0.0 collective-permute-done.1.x2_ref
  9.4 0.0 copy-done.4
  9.4 0.0 copy-done.5
  9.4 0.0 copy-done.7
  9.4 0.0 copy-done.8
  9.5 0.3 shard_map.105
  9.8 9.3 %collective-permute-start.2 = (f32[208,128]{1,0:T(8,128)S(1)}, f32[208,128]{1,0:T(8,128)S(1)}, u32[]{:S(2)}, u32[]{:S(2)}) collective-permute-start(f32[208,128]{1,0:T(8,128)S(1)} %get-tuple-element.17), channel_id=1, source_target_pairs={{0,1},{1,0},{2,3},{3,2},{4,5},{5,4},{6,7},{7,6},{8,9},{9,8},{10,11... | collective-permute-start | bytes 319496 | tf_op jit(solution)/shard_map/ppermute | solution.py:500
  19.1 1.9 %collective-permute-start.3 = (f32[208,128]{1,0:T(8,128)S(1)}, f32[208,128]{1,0:T(8,128)S(1)}, u32[]{:S(2)}, u32[]{:S(2)}) collective-permute-start(f32[208,128]{1,0:T(8,128)S(1)} %get-tuple-element.18), channel_id=1, source_target_pairs={{1,2},{2,1},{3,4},{4,3},{5,6},{6,5},{9,10},{10,9},{11,12},{12,11},... | collective-permute-start | bytes 319496 | tf_op jit(solution)/shard_map/ppermute | solution.py:500
  21.0 0.0 copy-start.6
  21.0 3.1 %shard_map.107 = (f32[192,256]{1,0:T(8,128)S(1)}, bf16[384,384]{1,0:T(8,128)(2,1)S(1)}, bf16[2048,128]{1,0:T(8,128)(2,1)S(1)}, bf16[2048,128]{1,0:T(8,128)(2,1)S(1)}) custom-call(s32[1]{0:T(128)} %bitcast.refs_0_.tile_ref, f32[192,128]{1,0:T(8,128)S(1)} %copy-done.5, s32[10,128]{1,0:T(8,128)S(1)} %copy-done.7, s32[1,128]{1,0:T(1,128)S(1)} %bitcast.12, ...), custom_call_target="tpu_custom_call" | custom-call | flops 4000000000 | bytes 12000000 | tf_op jit(solution)/shard_map/pallas_call | solution.py:480
  24.1 0.0 collective-permute-done.2.y1_ref
  24.1 0.9 collective-permute-done.3.y2_ref
  25.1 0.0 copy-done.6
  25.1 4.5 %shard_map.108.own_ref.vec_ref = f32[584,128]{1,0:T(8,128)S(1)} custom-call(s32[1]{0:T(128)} %bitcast.refs_0_.tile_ref, f32[192,128]{1,0:T(8,128)S(1)} %copy-done.5, s32[10,128]{1,0:T(8,128)S(1)} %copy-done.7, s32[1,128]{1,0:T(1,128)S(1)} %bitcast.13, f32[192,128]{1,0:T(8,128)S(1)} %copy-done.6, f32[304,128]{1,0:T(8,128)S(1)} %collective-permute-done.x1_ref, ...), custom_call_target="tpu_custom_call" | custom-call | flops 4000000000 | bytes 12000000 | tf_op jit(solution)/shard_map/pallas_call | solution.py:480
  29.6 1.9 %collective-permute-start.4 = (f32[584,128]{1,0:T(8,128)S(1)}, f32[584,128]{1,0:T(8,128)S(1)}, u32[]{:S(2)}, u32[]{:S(2)}) collective-permute-start(f32[584,128]{1,0:T(8,128)S(1)} %shard_map.108.own_ref.vec_ref), channel_id=1, source_target_pairs={{0,1},{1,0},{2,3},{3,2},{4,5},{5,4},{6,7},{7,6},{8,9},{9,8},{10,11... | collective-permute-start | bytes 897032 | tf_op jit(solution)/shard_map/ppermute | solution.py:599
  31.5 1.6 %collective-permute-done.4.other_ref = f32[584,128]{1,0:T(8,128)S(1)} collective-permute-done((f32[584,128]{1,0:T(8,128)S(1)}, f32[584,128]{1,0:T(8,128)S(1)}, u32[]{:S(2)}, u32[]{:S(2)}) %collective-permute-start.4) | collective-permute-done | bytes 299040 | tf_op jit(solution)/shard_map/ppermute | solution.py:599
  33.1 0.6 shard_map.109
  33.7 12.7 %all_to_all.20.in_ref = f32[4,296,128]{2,1,0:T(8,128)S(1)} all-to-all(f32[4,296,128]{2,1,0:T(8,128)S(1)} %shard_map.109), channel_id=1, replica_groups={{0,2,4,6},{1,3,5,7},{8,10,12,14},{9,11,13,15},{16,18,20,22},{17,19,21,2..., dimensions={0} | all-to-all | bytes 1212416 | tf_op jit(solution)/shard_map/all_to_all | solution.py:601
  46.4 0.1 shard_map.110
  46.5 28.3 %all_to_all.21 = f32[64,8,128]{2,1,0:T(8,128)S(1)} all-to-all(f32[64,8,128]{2,1,0:T(8,128)S(1)} %bitcast.7), channel_id=1, replica_groups=mesh['gx'=64,'gy'=8] {'gx'}, dimensions={0} | all-to-all | bytes 524288 | tf_op jit(solution)/shard_map/all_to_all | solution.py:603
  74.8 0.9 shard_map.111
  75.7 16.5 %all_to_all.22 = f32[64,4,128]{2,1,0:T(4,128)S(1)} all-to-all(f32[64,4,128]{2,1,0:T(4,128)S(1)} %bitcast.8), channel_id=1, replica_groups=mesh['gx'=64,'gy'=8] {'gx'}, dimensions={0} | all-to-all | bytes 262144 | tf_op jit(solution)/shard_map/all_to_all | solution.py:605
  92.2 8.1 %all_to_all.23.own_ref = f32[4,144,128]{2,1,0:T(8,128)S(1)} all-to-all(f32[4,144,128]{2,1,0:T(8,128)S(1)} %shard_map.112), channel_id=1, replica_groups={{0,2,4,6},{1,3,5,7},{8,10,12,14},{9,11,13,15},{16,18,20,22},{17,19,21,2..., dimensions={0} | all-to-all | bytes 589824 | tf_op jit(solution)/shard_map/all_to_all | solution.py:607
  100.2 6.7 %collective-permute-start.5 = (f32[4,144,128]{2,1,0:T(8,128)S(1)}, f32[4,144,128]{2,1,0:T(8,128)S(1)}, u32[]{:S(2)}, u32[]{:S(2)}) collective-permute-start(f32[4,144,128]{2,1,0:T(8,128)S(1)} %all_to_all.23.own_ref), channel_id=1, source_target_pairs={{0,1},{1,0},{2,3},{3,2},{4,5},{5,4},{6,7},{7,6},{8,9},{9,8},{10,11... | collective-permute-start | bytes 884744 | tf_op jit(solution)/shard_map/ppermute | solution.py:608
  107.0 1.2 %collective-permute-done.5.other_ref = f32[4,144,128]{2,1,0:T(8,128)S(1)} collective-permute-done((f32[4,144,128]{2,1,0:T(8,128)S(1)}, f32[4,144,128]{2,1,0:T(8,128)S(1)}, u32[]{:S(2)}, u32[]{:S(2)}) %collective-permute-start.5) | collective-permute-done | bytes 294944 | tf_op jit(solution)/shard_map/ppermute | solution.py:608
  108.2 1.0 shard_map.113
  (1 shorter events, 0.0 us)
Async XLA Ops:
  0.6 6.8 %copy-start = (f32[10,96,96]{2,1,0:T(8,128)S(1)}, f32[10,96,96]{2,1,0:T(8,128)}, u32[]{:S(2)}) copy-start(f32[10,96,96]{2,1,0:T(8,128)} %lr_ref.1) | copy-start | bytes 1105924
  0.6 6.8 %copy-start.1 = (f32[10,96,96]{2,1,0:T(8,128)S(1)}, f32[10,96,96]{2,1,0:T(8,128)}, u32[]{:S(2)}) copy-start(f32[10,96,96]{2,1,0:T(8,128)} %li_ref.1) | copy-start | bytes 1105924
  0.7 6.8 %copy-start.2 = (f32[4,96,96]{2,1,0:T(8,128)S(1)}, f32[4,96,96]{2,1,0:T(8,128)}, u32[]{:S(2)}) copy-start(f32[4,96,96]{2,1,0:T(8,128)} %tr_ref.1) | copy-start | bytes 442372
  0.7 6.8 %copy-start.3 = (f32[4,96,96]{2,1,0:T(8,128)S(1)}, f32[4,96,96]{2,1,0:T(8,128)}, u32[]{:S(2)}) copy-start(f32[4,96,96]{2,1,0:T(8,128)} %ti_ref.1) | copy-start | bytes 442372
  2.6 6.9 %collective-permute-start = (f32[304,128]{1,0:T(8,128)}, f32[304,128]{1,0:T(8,128)S(1)}, u32[]{:S(2)}, u32[]{:S(2)}) collective-permute-start(f32[304,128]{1,0:T(8,128)} %get-tuple-element.15), channel_id=1, source_target_pairs={{0,8},{8,0},{16,24},{24,16},{32,40},{40,32},{48,56},{56,48},{64,72... | collective-permute-start | bytes 466952 | tf_op jit(solution)/shard_map/ppermute | solution.py:500
  6.6 2.8 %copy-start.4 = (f32[192,128]{1,0:T(8,128)S(1)}, f32[192,128]{1,0:T(8,128)}, u32[]{:S(2)}) copy-start(f32[192,128]{1,0:T(8,128)} %fc_ref.3) | copy-start | bytes 294916
  6.6 2.8 %copy-start.5 = (f32[192,128]{1,0:T(8,128)S(1)}, f32[192,128]{1,0:T(8,128)}, u32[]{:S(2)}) copy-start(f32[192,128]{1,0:T(8,128)} %b_ref.5) | copy-start | bytes 294916
  6.6 2.8 %copy-start.7 = (s32[10,128]{1,0:T(8,128)S(1)}, s32[10,128]{1,0:T(8,128)}, u32[]{:S(2)}) copy-start(s32[10,128]{1,0:T(8,128)} %nb_ref.5) | copy-start | bytes 15364
  6.6 2.8 %copy-start.8 = (s32[128]{0:T(128)S(1)}, s32[128]{0:T(128)}, u32[]{:S(2)}) copy-start(s32[128]{0:T(128)} %param.17) | copy-start | bytes 1540
  6.7 2.8 %collective-permute-start.1 = (f32[304,128]{1,0:T(8,128)}, f32[304,128]{1,0:T(8,128)S(1)}, u32[]{:S(2)}, u32[]{:S(2)}) collective-permute-start(f32[304,128]{1,0:T(8,128)} %get-tuple-element.16), channel_id=1, source_target_pairs={{8,16},{16,8},{24,32},{32,24},{40,48},{48,40},{56,64},{64,56},{72,... | collective-permute-start | bytes 466952 | tf_op jit(solution)/shard_map/ppermute | solution.py:500
  9.8 14.3 %collective-permute-start.2 = (f32[208,128]{1,0:T(8,128)S(1)}, f32[208,128]{1,0:T(8,128)S(1)}, u32[]{:S(2)}, u32[]{:S(2)}) collective-permute-start(f32[208,128]{1,0:T(8,128)S(1)} %get-tuple-element.17), channel_id=1, source_target_pairs={{0,1},{1,0},{2,3},{3,2},{4,5},{5,4},{6,7},{7,6},{8,9},{9,8},{10,11... | collective-permute-start | bytes 319496 | tf_op jit(solution)/shard_map/ppermute | solution.py:500
  19.1 6.0 %collective-permute-start.3 = (f32[208,128]{1,0:T(8,128)S(1)}, f32[208,128]{1,0:T(8,128)S(1)}, u32[]{:S(2)}, u32[]{:S(2)}) collective-permute-start(f32[208,128]{1,0:T(8,128)S(1)} %get-tuple-element.18), channel_id=1, source_target_pairs={{1,2},{2,1},{3,4},{4,3},{5,6},{6,5},{9,10},{10,9},{11,12},{12,11},... | collective-permute-start | bytes 319496 | tf_op jit(solution)/shard_map/ppermute | solution.py:500
  21.0 4.1 %copy-start.6 = (f32[192,128]{1,0:T(8,128)S(1)}, f32[192,128]{1,0:T(8,128)}, u32[]{:S(2)}) copy-start(f32[192,128]{1,0:T(8,128)} %inc_ref.1) | copy-start | bytes 294916
  29.6 3.5 %collective-permute-start.4 = (f32[584,128]{1,0:T(8,128)S(1)}, f32[584,128]{1,0:T(8,128)S(1)}, u32[]{:S(2)}, u32[]{:S(2)}) collective-permute-start(f32[584,128]{1,0:T(8,128)S(1)} %shard_map.108.own_ref.vec_ref), channel_id=1, source_target_pairs={{0,1},{1,0},{2,3},{3,2},{4,5},{5,4},{6,7},{7,6},{8,9},{9,8},{10,11... | collective-permute-start | bytes 897032 | tf_op jit(solution)/shard_map/ppermute | solution.py:599
  100.2 7.9 %collective-permute-start.5 = (f32[4,144,128]{2,1,0:T(8,128)S(1)}, f32[4,144,128]{2,1,0:T(8,128)S(1)}, u32[]{:S(2)}, u32[]{:S(2)}) collective-permute-start(f32[4,144,128]{2,1,0:T(8,128)S(1)} %all_to_all.23.own_ref), channel_id=1, source_target_pairs={{0,1},{1,0},{2,3},{3,2},{4,5},{5,4},{6,7},{7,6},{8,9},{9,8},{10,11... | collective-permute-start | bytes 884744 | tf_op jit(solution)/shard_map/ppermute | solution.py:608

commit v8 on v7

--- a/solution.py
+++ b/solution.py
@@ -38,17 +38,6 @@
     return lax.broadcasted_iota(jnp.int32, (rows, PT), 1)
 
 
-def fetch(sources, targets, sems):
-    copies = [
-        pltpu.make_async_copy(src, dst, sems.at[i])
-        for i, (src, dst) in enumerate(zip(sources, targets))
-    ]
-    for copy in copies:
-        copy.start()
-    for copy in copies:
-        copy.wait()
-
-
 def meta_rows(nb_ref, pt_ref):
     return jnp.concatenate(
         [
@@ -68,11 +57,8 @@
     return lax.rem(tile_ref[0], 2) == 0
 
 
-def pack_wide_kernel(short, *refs):
-    even = even_row(short, refs[0])
-    one_ref, two_ref = refs[5:7]
-    fc_ref, b_ref, nb_ref, pt_ref = refs[7:11]
-    fetch(refs[1:5], refs[7:11], refs[11])
+def pack_wide_kernel(short, tile_ref, fc_ref, b_ref, nb_ref, pt_ref, _, one_ref, two_ref):
+    even = even_row(short, tile_ref)
     meta = meta_rows(nb_ref, pt_ref)
     top, low = fc_ref[0:HALF, :], fc_ref[HALF:W, :]
     first = lanes(HALF) < 64
@@ -201,6 +187,15 @@
     return jnp.where(ids >= 0, ids + 1, -10).astype(F32)
 
 
+def target_ids_kernel(short, tile_ref, ids_ref):
+    ids_ref[...] = target_ids(tile_ref[0] * PT, short * PT)
+
+
+def narrow_product(w_ref, both):
+    rows = dot(w_ref[0:W, :], both)
+    return rows[:, 0:PT] + rows[:, PT:] + dot(w_ref[W : 2 * W, :], both[:, 0:PT])
+
+
 def product(w_ref, hi, lo):
     rows = dot(w_ref[...], hi)
     return rows[0:W] + rows[W : 2 * W] + dot(w_ref[0:W, :], lo)
@@ -226,11 +221,15 @@
     return jnp.where(at == meta[s : s + 1, :], 1.0, 0.0).astype(BF16)
 
 
-def place(refs, parts, s, lanes_at, lanes_from):
-    for ref, part in zip(refs, parts):
+def place(spots, parts, s, lanes_from):
+    for (ref, lanes_at), part in zip(spots, parts):
         for half in range(2):
             at = half * PART + s * HALF
             ref[at : at + HALF, lanes_at] = part[half * HALF : (half + 1) * HALF, lanes_from]
+
+
+def beside(ref):
+    return ((ref, slice(0, PT)), (ref, slice(PT, 2 * PT)))
 
 
 def clear_fill(refs):
@@ -240,7 +239,7 @@
             ref[at : at + rows, :] = jnp.zeros((rows, ref.shape[1]), BF16)
 
 
-def scatter_pairs(refs, stack, ids, metas, lanes_at):
+def scatter_pairs(ref, stack, ids, metas):
     for s in range(0, SLOTS, 2):
         pick = jnp.concatenate(
             [
@@ -252,23 +251,23 @@
         g = dot_nt(stack, pick)
         parts = split(g[0:W] + g[W : 2 * W])
         for t in (0, 1):
-            place(refs, parts, s + t, lanes_at, slice(t * PT, (t + 1) * PT))
-
-
-def gather_pairs(refs, blocks, ids, meta, lanes_at):
+            place(beside(ref), parts, s + t, slice(t * PT, (t + 1) * PT))
+
+
+def gather_pairs(ref, blocks, ids, meta):
     stack = jnp.concatenate(split(jnp.concatenate(blocks, axis=1)), axis=0)
     for s in range(0, SLOTS, 2):
         pick = jnp.concatenate([one_hot(ids, meta, s), one_hot(ids, meta, s + 1)], axis=1)
         g = dot(stack, pick).astype(BF16)
         for t in (0, 1):
-            place(
-                refs, (g[0:W], g[W : 2 * W]), s + t, lanes_at, slice(t * PT, (t + 1) * PT)
-            )
+            parts = (g[0:W], g[W : 2 * W])
+            place(beside(ref), parts, s + t, slice(t * PT, (t + 1) * PT))
 
 
 def early_kernel(
     short,
     tile_ref,
+    ids_ref,
     b_ref,
     nb_ref,
     pt_ref,
@@ -279,32 +278,32 @@
     lw_ref,
     part_ref,
     stack_ref,
-    fhi_ref,
-    flo_ref,
+    f_ref,
     ghi_ref,
     glo_ref,
 ):
     wide = Tiles(even_row(short, tile_ref), x1_ref, x2_ref)
     v, m, half = slice(0, W), slice(W, ROWS), slice(ROWS, ROWS + HALF)
-    refs, gathered = (ghi_ref, glo_ref), (fhi_ref, flo_ref)
-    ids = target_ids(tile_ref[0] * PT, short * PT)[0 : 2 * PT, :]
+    refs = (ghi_ref, glo_ref)
+    ids = ids_ref[0 : 2 * PT, :]
     own = meta_rows(nb_ref, pt_ref)
     metas = (own, wide.below(m), wide.above(m))
-    clear_fill(refs + gathered)
+    clear_fill(refs + (f_ref,))
     stack = scaled_by_type(tw_ref, (b_ref[...], wide.below(v), wide.above(v)), metas)
     stack_ref[...] = stack
     for s in range(SLOTS):
         pick = jnp.concatenate([one_hot(ids, meta, s) for meta in metas], axis=1)
         g = dot_nt(stack, pick)
-        place(refs, split(g[0:W] + g[W : 2 * W]), s, slice(0, 2 * PT), slice(0, 2 * PT))
+        place([(ref, slice(None)) for ref in refs], split(g[0:W] + g[W : 2 * W]), s, slice(None))
     part_ref[...] = product(lw_ref, ghi_ref[...], glo_ref[...])
     fc_ud = unpack_fc(wide.below(half), wide.above(half))
-    gather_pairs(gathered, (fc_ref[...], fc_ud), ids, own, slice(0, PT))
+    gather_pairs(f_ref, (fc_ref[...], fc_ud), ids, own)
 
 
 def main_kernel(
     short,
     tile_ref,
+    ids_ref,
     b_ref,
     nb_ref,
     pt_ref,
@@ -315,20 +314,18 @@
     y2_ref,
     part_ref,
     stack_ref,
-    fhi_ref,
-    flo_ref,
+    f_ref,
     tw_ref,
     lw_ref,
     fw_ref,
     vec_ref,
-    ghi_ref,
-    glo_ref,
+    g_ref,
+    h_ref,
 ):
     rows = Tiles(even_row(short, tile_ref), x1_ref, x2_ref)
     cols = Tiles(even_col(tile_ref), y1_ref, y2_ref)
     v, m = slice(0, W), slice(W, ROWS)
-    refs = (ghi_ref, glo_ref)
-    ids = target_ids(tile_ref[0] * PT, short * PT)
+    ids = ids_ref[...]
     col = lanes(META) % 32
     b = b_ref[...]
     m_own = meta_rows(nb_ref, pt_ref)
@@ -341,15 +338,13 @@
     row_id = lax.broadcasted_iota(jnp.int32, (META, PT), 0)
     m_b = jnp.where(b_zone | (row_id >= SLOTS), m_lr, 0.0)
     m_f = jnp.where(b_zone & (row_id < SLOTS), 0.0, m_lr)
-    clear_fill(refs)
+    clear_fill((g_ref, h_ref))
     first, second = slice(0, PT), slice(PT, 2 * PT)
     own_ids, lr_ids, edge_ids = ids[0:PT, :], ids[2 * PT : 3 * PT, :], ids[3 * PT :, :]
 
     stack = jnp.concatenate([stack_ref[...], scaled_by_type(tw_ref, (x_lr,), (m_b,))], axis=1)
-    scatter_pairs(
-        refs, stack, (lr_ids, lr_ids, lr_ids, edge_ids), (m_own, m_up, m_dn, m_b), first
-    )
-    edge = product(lw_ref, ghi_ref[:, first], glo_ref[:, first])
+    scatter_pairs(g_ref, stack, (lr_ids, lr_ids, lr_ids, edge_ids), (m_own, m_up, m_dn, m_b))
+    edge = narrow_product(lw_ref, g_ref[...])
     left, right = spot < 2, spot >= 30
     u1 = part_ref[:, first] + jnp.where(left | right, edge, 0.0)
     u1_ud = part_ref[:, second] + jnp.where(
@@ -357,18 +352,16 @@
     )
     u1_lr = jnp.where((spot >= 12) & (spot < 20), edge, 0.0)
 
-    gather_pairs(refs, (x_lr,), lr_ids, m_own, second)
-    exc = inc_ref[...] + product(
-        fw_ref, ghi_ref[:, second] + fhi_ref[...], glo_ref[:, second] + flo_ref[...]
-    )
+    gather_pairs(h_ref, (x_lr,), lr_ids, m_own)
+    exc = inc_ref[...] + narrow_product(fw_ref, h_ref[...] + f_ref[...])
     vec_ref[0:W, :] = b
     vec_ref[W : 2 * W, :] = u1
     vec_ref[2 * W : 3 * W, :] = exc
 
     metas = (m_own, m_ud, m_f)
     stack = scaled_by_type(tw_ref, (u1, u1_ud, u1_lr), metas)
-    scatter_pairs(refs, stack, (own_ids,) * 3, metas, first)
-    u2 = product(lw_ref, ghi_ref[:, first], glo_ref[:, first])
+    scatter_pairs(g_ref, stack, (own_ids,) * 3, metas)
+    u2 = narrow_product(lw_ref, g_ref[...])
 
     lane, row = lanes(8), lax.broadcasted_iota(jnp.int32, (8, PT), 0)
     gram = jnp.zeros((8, PT), F32)
@@ -415,7 +408,7 @@
     out_ref[pl.ds(6, 64, 8), :] = jnp.broadcast_to(total[288:289, :], (64, PT))
 
 
-def combine_kernel(in_ref, vec_ref, out_ref, adj_ref):
+def combine_kernel(in_ref, out_ref, coef_ref):
     total = jnp.sum(in_ref[...].reshape(64, 8, PT), axis=0)
     lane = lanes(1)
 
@@ -450,7 +443,8 @@
     mixed = jnp.concatenate([mixed, jnp.zeros((1, PT), F32)] * 2, axis=0)
     for i in range(32):
         out_ref[8 * i : 8 * i + 8, :] = mixed
-    adj_ref[...] = c0 * vec_ref[0:W, :] + c1 * vec_ref[W : 2 * W, :]
+    coef_ref[0:4, :] = jnp.broadcast_to(c0, (4, PT))
+    coef_ref[4:8, :] = jnp.broadcast_to(c1, (4, PT))
 
 
 def copies_kernel(in_ref, out_ref):
@@ -460,7 +454,8 @@
             out_ref[i, 48 * j : 48 * (j + 1), :] = rows
 
 
-def expand_kernel(tile_ref, own_ref, other_ref, out_ref):
+def expand_kernel(tile_ref, own_ref, other_ref, vec_ref, coef_ref, out_ref, adj_ref):
+    adj_ref[...] = coef_ref[0:1, :] * vec_ref[0:W, :] + coef_ref[4:5, :] * vec_ref[W : 2 * W, :]
     core = lax.rem(tile_ref[0], 2)
     for ref, first in ((own_ref, 2 * core), (other_ref, 2 - 2 * core)):
         for k in range(2):
@@ -473,10 +468,7 @@
                 out_ref[first + k, at + 48 : at + HALF, PT:W] = pltpu.roll(edge, 64, 1)[:, 0:64]
 
 
-def call(kernel, shapes, *args, smem=0, mib=6, dtype=F32, fetched=False, us=1, **kw):
-    if fetched:
-        kw["scratch_shapes"] = [pltpu.VMEM(a.shape, a.dtype) for a in args[smem:]]
-        kw["scratch_shapes"].append(pltpu.SemaphoreType.DMA((len(args) - smem,)))
+def call(kernel, shapes, *args, smem=0, whole=0, mib=6, dtype=F32, us=1, **kw):
     return pl.pallas_call(
         kernel,
         out_shape=[
@@ -484,7 +476,8 @@
             for s in shapes
         ],
         in_specs=[pl.BlockSpec(memory_space=pltpu.SMEM)] * smem
-        + [pl.BlockSpec(memory_space=pltpu.HBM if fetched else pltpu.VMEM)] * (len(args) - smem),
+        + [pl.BlockSpec(memory_space=pltpu.VMEM)] * (len(args) - smem - whole)
+        + [pl.BlockSpec(memory_space=pl.ANY)] * whole,
         cost_estimate=pl.CostEstimate(
             flops=us * 10**9, bytes_accessed=us * 3 * 10**6, transcendentals=0
         ),
@@ -515,6 +508,9 @@
     tile = lax.axis_index("gx") * n_short + lax.axis_index("gy")
     tile = tile.astype(jnp.int32).reshape(1)
     kinds = particle_type.reshape(1, PT)
+    (ids,) = call(
+        functools.partial(target_ids_kernel, n_short), [(4 * PT, PT)], tile, smem=1, us=4
+    )
     one, two = call(
         functools.partial(pack_wide_kernel, n_short),
         [(ROWS + HALF, PT)] * 2,
@@ -523,10 +519,9 @@
         cost_grad,
         neighbours,
         kinds,
+        ids,
         smem=1,
-        mib=60,
-        us=4,
-        fetched=True,
+        whole=1,
     )
     x1, x2 = swapped(one, two, "gx")
     one, two = call(
@@ -558,8 +553,9 @@
     early = call(
         functools.partial(early_kernel, n_short),
         [(W, 2 * PT), jax.ShapeDtypeStruct((2 * W, 3 * PT), BF16)]
-        + [jax.ShapeDtypeStruct((2 * PART, PT), BF16)] * 2,
+        + [jax.ShapeDtypeStruct((2 * PART, 2 * PT), BF16)],
         tile,
+        ids,
         cost_grad,
         neighbours,
         kinds,
@@ -577,6 +573,7 @@
         functools.partial(main_kernel, n_short),
         [(3 * W + 8, PT)],
         tile,
+        ids,
         cost_grad,
         neighbours,
         kinds,
@@ -601,12 +598,21 @@
     got = lax.all_to_all(chunks, "gy", 0, 0, axis_index_groups=lines)
     (pieces,) = call(spread_kernel, [(512, PT)], got)
     got = lax.all_to_all(pieces.reshape(64, 8, PT), "gx", 0, 0)
-    mixed, adjoint = call(combine_kernel, [(256, PT), (W, PT)], got.reshape(512, PT), vectors)
+    mixed, coefs = call(combine_kernel, [(256, PT), (8, PT)], got.reshape(512, PT))
     got = lax.all_to_all(mixed.reshape(64, 4, PT), "gx", 0, 0)
     (copies,) = call(copies_kernel, [(4, 144, PT)], got.reshape(256, PT))
     half = lax.all_to_all(copies, "gy", 0, 0, axis_index_groups=lines)
     other = lax.ppermute(half, "gy", pairs)
-    (sensitivity,) = call(expand_kernel, [(KINDS, W, W)], tile, half, other, smem=1)
+    sensitivity, adjoint = call(
+        expand_kernel,
+        [(KINDS, W, W), (W, PT)],
+        tile,
+        half,
+        other,
+        vectors,
+        coefs,
+        smem=1,
+    )
     return (adjoint, sensitivity)
 
 

time: 110 us -> 107 us (0.973)
  Pallas kernels: 13.1 us -> 10.3 us
    pallas_call x10 -> x11, Pallas kernels: 13.1 us -> 10.3 us  [call(): pl.pallas_call(kernel, out_shape=[s if isinstance(s, jax.ShapeDtypeStruct...]
where the time goes in v8:
time: 107 us
  blocking collectives  65.5 us (61%)
  starting transfers between devices  24.7 us (23%)
  Pallas kernels  10.3 us (10%)
  waiting for transfers between devices  4.81 us (4%)
    all_to_all x1, blocking collectives, body(): got = lax.all_to_all(pieces.reshape(64, 8, PT), 'gx', 0, 0)  28.2 us
    all_to_all x1, blocking collectives, body(): got = lax.all_to_all(mixed.reshape(64, 4, PT), 'gx', 0, 0)  16.5 us
    ppermute x4, starting transfers between devices, swapped(): return (lax.ppermute(one, axis, near), lax.ppermute(two, axis, far))  16 us
    all_to_all x1, blocking collectives, body(): got = lax.all_to_all(chunks, 'gy', 0, 0, axis_index_groups=lines)  12.7 us
    pallas_call x11, Pallas kernels, call(): pl.pallas_call(kernel, out_shape=[s if isinstance(s, jax.ShapeDtypeStruct...  10.3 us
    all_to_all x1, blocking collectives, body(): half = lax.all_to_all(copies, 'gy', 0, 0, axis_index_groups=lines)  8.07 us
    ppermute x1, starting transfers between devices, body(): other = lax.ppermute(half, 'gy', pairs)  6.73 us
  transfers between devices with their start and end apart: 6, of which 4 were waited for; matrix products, arithmetic and copies ran while one was open for 0% of the time, Pallas kernels for 4%

profile of v8, /device:TPU:1, one launch (start us, length us, event | category | flops | bytes accessed | tf_op | source)
XLA Modules:
  0.0 106.9 jit_solution(9106315527899785958)
XLA Ops:
  0.6 0.0 copy-start.4
  0.6 0.0 copy-start.5
  0.7 0.0 copy-start.7
  0.7 0.0 copy-start.8
  0.7 0.1 shard_map.104._.ids_ref
  0.8 0.7 copy-done.4
  1.5 0.0 copy-done.5
  1.6 0.0 copy-done.7
  1.6 0.0 copy-done.8
  1.6 0.0 copy-start
  1.6 0.0 copy-start.1
  1.6 0.0 copy-start.2
  1.6 0.0 copy-start.3
  1.6 0.1 shard_map.105
  1.7 4.2 %collective-permute-start = (f32[304,128]{1,0:T(8,128)S(1)}, f32[304,128]{1,0:T(8,128)S(1)}, u32[]{:S(2)}, u32[]{:S(2)}) collective-permute-start(f32[304,128]{1,0:T(8,128)S(1)} %get-tuple-element.16), channel_id=1, source_target_pairs={{0,8},{8,0},{16,24},{24,16},{32,40},{40,32},{48,56},{56,48},{64,72... | collective-permute-start | bytes 466952 | tf_op jit(solution)/shard_map/ppermute | solution.py:493
  5.9 0.7 collective-permute-start.1
  6.6 0.0 copy-done
  6.6 0.0 copy-done.1
  6.6 0.0 copy-done.2
  6.6 0.0 copy-done.3
  6.6 0.7 shard_map.107
  7.4 1.1 %collective-permute-done.x1_ref = f32[304,128]{1,0:T(8,128)S(1)} collective-permute-done((f32[304,128]{1,0:T(8,128)S(1)}, f32[304,128]{1,0:T(8,128)S(1)}, u32[]{:S(2)}, u32[]{:S(2)}) %collective-permute-start) | collective-permute-done | bytes 155680 | tf_op jit(solution)/shard_map/ppermute | solution.py:493
  8.5 0.0 collective-permute-done.1.x2_ref
  8.5 0.3 shard_map.106
  8.8 9.3 %collective-permute-start.2 = (f32[208,128]{1,0:T(8,128)S(1)}, f32[208,128]{1,0:T(8,128)S(1)}, u32[]{:S(2)}, u32[]{:S(2)}) collective-permute-start(f32[208,128]{1,0:T(8,128)S(1)} %get-tuple-element.18), channel_id=1, source_target_pairs={{0,1},{1,0},{2,3},{3,2},{4,5},{5,4},{6,7},{7,6},{8,9},{9,8},{10,11... | collective-permute-start | bytes 319496 | tf_op jit(solution)/shard_map/ppermute | solution.py:493
  18.1 1.9 %collective-permute-start.3 = (f32[208,128]{1,0:T(8,128)S(1)}, f32[208,128]{1,0:T(8,128)S(1)}, u32[]{:S(2)}, u32[]{:S(2)}) collective-permute-start(f32[208,128]{1,0:T(8,128)S(1)} %get-tuple-element.19), channel_id=1, source_target_pairs={{1,2},{2,1},{3,4},{4,3},{5,6},{6,5},{9,10},{10,9},{11,12},{12,11},... | collective-permute-start | bytes 319496 | tf_op jit(solution)/shard_map/ppermute | solution.py:493
  20.0 0.0 copy-start.6
  20.0 3.1 %shard_map.108 = (f32[192,256]{1,0:T(8,128)S(1)}, bf16[384,384]{1,0:T(8,128)(2,1)S(1)}, bf16[2048,256]{1,0:T(8,128)(2,1)S(1)}) custom-call(s32[1]{0:T(128)} %bitcast.tile_ref, f32[512,128]{1,0:T(8,128)S(1)} %shard_map.104._.ids_ref, f32[192,128]{1,0:T(8,128)S(1)} %copy-done.5, s32[10,128]{1,0:T(8,128)S(1)} %copy-done.7, s32[1,128]{1,0:T(1,128)S(1)} %bitcast.12, ...), custom_call_target="tpu_custom_call" | custom-call | flops 4000000000 | bytes 12000000 | tf_op jit(solution)/shard_map/pallas_call | solution.py:472
  23.2 0.0 collective-permute-done.2.y1_ref
  23.2 0.9 collective-permute-done.3.y2_ref
  24.1 0.0 copy-done.6
  24.1 4.0 %shard_map.109.own_ref.vec_ref = f32[584,128]{1,0:T(8,128)S(1)} custom-call(s32[1]{0:T(128)} %bitcast.tile_ref, f32[512,128]{1,0:T(8,128)S(1)} %shard_map.104._.ids_ref, f32[192,128]{1,0:T(8,128)S(1)} %copy-done.5, s32[10,128]{1,0:T(8,128)S(1)} %copy-done.7, s32[1,128]{1,0:T(1,128)S(1)} %bitcast.13, f32[192,128]{1,0:T(8,128)S(1)} %copy-done.6, ...), custom_call_target="tpu_custom_call" | custom-call | flops 4000000000 | bytes 12000000 | tf_op jit(solution)/shard_map/pallas_call | solution.py:472
  28.2 1.9 %collective-permute-start.4 = (f32[584,128]{1,0:T(8,128)S(1)}, f32[584,128]{1,0:T(8,128)S(1)}, u32[]{:S(2)}, u32[]{:S(2)}) collective-permute-start(f32[584,128]{1,0:T(8,128)S(1)} %shard_map.109.own_ref.vec_ref), channel_id=1, source_target_pairs={{0,1},{1,0},{2,3},{3,2},{4,5},{5,4},{6,7},{7,6},{8,9},{9,8},{10,11... | collective-permute-start | bytes 897032 | tf_op jit(solution)/shard_map/ppermute | solution.py:596
  30.1 1.6 %collective-permute-done.4.other_ref = f32[584,128]{1,0:T(8,128)S(1)} collective-permute-done((f32[584,128]{1,0:T(8,128)S(1)}, f32[584,128]{1,0:T(8,128)S(1)}, u32[]{:S(2)}, u32[]{:S(2)}) %collective-permute-start.4) | collective-permute-done | bytes 299040 | tf_op jit(solution)/shard_map/ppermute | solution.py:596
  31.6 0.6 shard_map.110
  32.2 12.7 %all_to_all.20.in_ref = f32[4,296,128]{2,1,0:T(8,128)S(1)} all-to-all(f32[4,296,128]{2,1,0:T(8,128)S(1)} %shard_map.110), channel_id=1, replica_groups={{0,2,4,6},{1,3,5,7},{8,10,12,14},{9,11,13,15},{16,18,20,22},{17,19,21,2..., dimensions={0} | all-to-all | bytes 1212416 | tf_op jit(solution)/shard_map/all_to_all | solution.py:598
  45.0 0.1 shard_map.111
  45.0 28.2 %all_to_all.21 = f32[64,8,128]{2,1,0:T(8,128)S(1)} all-to-all(f32[64,8,128]{2,1,0:T(8,128)S(1)} %bitcast.7), channel_id=1, replica_groups=mesh['gx'=64,'gy'=8] {'gx'}, dimensions={0} | all-to-all | bytes 524288 | tf_op jit(solution)/shard_map/all_to_all | solution.py:600
  73.2 0.2 shard_map.112
  73.4 16.5 %all_to_all.22 = f32[64,4,128]{2,1,0:T(4,128)S(1)} all-to-all(f32[64,4,128]{2,1,0:T(4,128)S(1)} %bitcast.8), channel_id=1, replica_groups=mesh['gx'=64,'gy'=8] {'gx'}, dimensions={0} | all-to-all | bytes 262144 | tf_op jit(solution)/shard_map/all_to_all | solution.py:602
  89.9 8.1 %all_to_all.23.own_ref = f32[4,144,128]{2,1,0:T(8,128)S(1)} all-to-all(f32[4,144,128]{2,1,0:T(8,128)S(1)} %shard_map.113), channel_id=1, replica_groups={{0,2,4,6},{1,3,5,7},{8,10,12,14},{9,11,13,15},{16,18,20,22},{17,19,21,2..., dimensions={0} | all-to-all | bytes 589824 | tf_op jit(solution)/shard_map/all_to_all | solution.py:604
  98.0 6.7 %collective-permute-start.5 = (f32[4,144,128]{2,1,0:T(8,128)S(1)}, f32[4,144,128]{2,1,0:T(8,128)S(1)}, u32[]{:S(2)}, u32[]{:S(2)}) collective-permute-start(f32[4,144,128]{2,1,0:T(8,128)S(1)} %all_to_all.23.own_ref), channel_id=1, source_target_pairs={{0,1},{1,0},{2,3},{3,2},{4,5},{5,4},{6,7},{7,6},{8,9},{9,8},{10,11... | collective-permute-start | bytes 884744 | tf_op jit(solution)/shard_map/ppermute | solution.py:605
  104.8 1.2 %collective-permute-done.5.other_ref = f32[4,144,128]{2,1,0:T(8,128)S(1)} collective-permute-done((f32[4,144,128]{2,1,0:T(8,128)S(1)}, f32[4,144,128]{2,1,0:T(8,128)S(1)}, u32[]{:S(2)}, u32[]{:S(2)}) %collective-permute-start.5) | collective-permute-done | bytes 294944 | tf_op jit(solution)/shard_map/ppermute | solution.py:605
  105.9 1.0 shard_map.114
  (1 shorter events, 0.0 us)
Async XLA Ops:
  0.6 0.9 copy-start.4
  0.6 0.9 copy-start.5
  0.7 0.9 copy-start.7
  0.7 0.9 copy-start.8
  1.6 5.0 %copy-start = (f32[10,96,96]{2,1,0:T(8,128)S(1)}, f32[10,96,96]{2,1,0:T(8,128)}, u32[]{:S(2)}) copy-start(f32[10,96,96]{2,1,0:T(8,128)} %lr_ref.1) | copy-start | bytes 1105924
  1.6 5.0 %copy-start.1 = (f32[10,96,96]{2,1,0:T(8,128)S(1)}, f32[10,96,96]{2,1,0:T(8,128)}, u32[]{:S(2)}) copy-start(f32[10,96,96]{2,1,0:T(8,128)} %li_ref.1) | copy-start | bytes 1105924
  1.6 5.0 %copy-start.2 = (f32[4,96,96]{2,1,0:T(8,128)S(1)}, f32[4,96,96]{2,1,0:T(8,128)}, u32[]{:S(2)}) copy-start(f32[4,96,96]{2,1,0:T(8,128)} %tr_ref.1) | copy-start | bytes 442372
  1.6 5.0 %copy-start.3 = (f32[4,96,96]{2,1,0:T(8,128)S(1)}, f32[4,96,96]{2,1,0:T(8,128)}, u32[]{:S(2)}) copy-start(f32[4,96,96]{2,1,0:T(8,128)} %ti_ref.1) | copy-start | bytes 442372
  1.7 6.8 %collective-permute-start = (f32[304,128]{1,0:T(8,128)S(1)}, f32[304,128]{1,0:T(8,128)S(1)}, u32[]{:S(2)}, u32[]{:S(2)}) collective-permute-start(f32[304,128]{1,0:T(8,128)S(1)} %get-tuple-element.16), channel_id=1, source_target_pairs={{0,8},{8,0},{16,24},{24,16},{32,40},{40,32},{48,56},{56,48},{64,72... | collective-permute-start | bytes 466952 | tf_op jit(solution)/shard_map/ppermute | solution.py:493
  5.9 2.6 %collective-permute-start.1 = (f32[304,128]{1,0:T(8,128)S(1)}, f32[304,128]{1,0:T(8,128)S(1)}, u32[]{:S(2)}, u32[]{:S(2)}) collective-permute-start(f32[304,128]{1,0:T(8,128)S(1)} %get-tuple-element.17), channel_id=1, source_target_pairs={{8,16},{16,8},{24,32},{32,24},{40,48},{48,40},{56,64},{64,56},{72,... | collective-permute-start | bytes 466952 | tf_op jit(solution)/shard_map/ppermute | solution.py:493
  8.8 14.4 %collective-permute-start.2 = (f32[208,128]{1,0:T(8,128)S(1)}, f32[208,128]{1,0:T(8,128)S(1)}, u32[]{:S(2)}, u32[]{:S(2)}) collective-permute-start(f32[208,128]{1,0:T(8,128)S(1)} %get-tuple-element.18), channel_id=1, source_target_pairs={{0,1},{1,0},{2,3},{3,2},{4,5},{5,4},{6,7},{7,6},{8,9},{9,8},{10,11... | collective-permute-start | bytes 319496 | tf_op jit(solution)/shard_map/ppermute | solution.py:493
  18.1 6.0 %collective-permute-start.3 = (f32[208,128]{1,0:T(8,128)S(1)}, f32[208,128]{1,0:T(8,128)S(1)}, u32[]{:S(2)}, u32[]{:S(2)}) collective-permute-start(f32[208,128]{1,0:T(8,128)S(1)} %get-tuple-element.19), channel_id=1, source_target_pairs={{1,2},{2,1},{3,4},{4,3},{5,6},{6,5},{9,10},{10,9},{11,12},{12,11},... | collective-permute-start | bytes 319496 | tf_op jit(solution)/shard_map/ppermute | solution.py:493
  20.0 4.1 %copy-start.6 = (f32[192,128]{1,0:T(8,128)S(1)}, f32[192,128]{1,0:T(8,128)}, u32[]{:S(2)}) copy-start(f32[192,128]{1,0:T(8,128)} %inc_ref.1) | copy-start | bytes 294916
  28.2 3.5 %collective-permute-start.4 = (f32[584,128]{1,0:T(8,128)S(1)}, f32[584,128]{1,0:T(8,128)S(1)}, u32[]{:S(2)}, u32[]{:S(2)}) collective-permute-start(f32[584,128]{1,0:T(8,128)S(1)} %shard_map.109.own_ref.vec_ref), channel_id=1, source_target_pairs={{0,1},{1,0},{2,3},{3,2},{4,5},{5,4},{6,7},{7,6},{8,9},{9,8},{10,11... | collective-permute-start | bytes 897032 | tf_op jit(solution)/shard_map/ppermute | solution.py:596
  98.0 7.9 %collective-permute-start.5 = (f32[4,144,128]{2,1,0:T(8,128)S(1)}, f32[4,144,128]{2,1,0:T(8,128)S(1)}, u32[]{:S(2)}, u32[]{:S(2)}) collective-permute-start(f32[4,144,128]{2,1,0:T(8,128)S(1)} %all_to_all.23.own_ref), channel_id=1, source_target_pairs={{0,1},{1,0},{2,3},{3,2},{4,5},{5,4},{6,7},{7,6},{8,9},{9,8},{10,11... | collective-permute-start | bytes 884744 | tf_op jit(solution)/shard_map/ppermute | solution.py:605

commit v9 on v8

--- a/solution.py
+++ b/solution.py
@@ -1,10 +1,12 @@
 import functools
+import math
 
 import jax
 import jax.numpy as jnp
 from jax import lax
 from jax.experimental import pallas as pl
 from jax.experimental.pallas import tpu as pltpu
+from jax.sharding import Mesh
 from jax.sharding import PartitionSpec as P
 
 F32 = jnp.float32
@@ -16,7 +18,10 @@
 KINDS = 4
 META = 16
 ROWS = W + META
-CHUNK = 296
+CHUNK = 40
+BACK = 24
+TALL = ("z", "y")
+FLAT = ("x", "c")
 PART = 1024
 MIB = 1024 * 1024
 
@@ -386,34 +391,29 @@
         for which in range(2):
             for h in range(2):
                 block = out[which * W + h * HALF : which * W + (h + 1) * HALF, :]
-                at = which * 144
-                chunk_ref[2 * k + h, at : at + 96, :] = block[:, 0:PT]
-                chunk_ref[2 * k + h, at + 96 : at + 144, :] = block[0:48, PT:] + pltpu.roll(
-                    block[48:96, PT:], 64, 1
-                )
-    gram = own_ref[3 * W :, :] + other_ref[3 * W :, :]
-    for g in range(4):
-        chunk_ref[g, 288:296, :] = gram
+                edge = block[0:48, PT:] + pltpu.roll(block[48:96, PT:], 64, 1)
+                at = (2 * k + h) * 8 * CHUNK + which * 18
+                for i in range(18):
+                    rows = block[8 * i : 8 * i + 8, 0:PT] if i < 12 else edge[8 * i - 96 : 8 * i - 88]
+                    chunk_ref[pl.ds(at + i, 8, CHUNK), :] = rows
+    gram = own_ref[3 * W : 3 * W + 1, :] + other_ref[3 * W : 3 * W + 1, :]
+    for i in range(36, CHUNK):
+        row = gram if i == 36 else jnp.zeros((1, PT), F32)
+        chunk_ref[pl.ds(i, 32, CHUNK), :] = jnp.broadcast_to(row, (32, PT))
 
 
 def spread_kernel(in_ref, out_ref):
-    total = in_ref[0]
-    for i in range(1, 4):
-        total = total + in_ref[i]
-    out_ref[...] = jnp.zeros_like(out_ref)
-    for which in range(2):
-        for j in range(3):
-            at = which * 144 + j * 48
-            out_ref[pl.ds(3 * which + j, 48, 8), :] = total[at : at + 48, :]
-    out_ref[pl.ds(6, 64, 8), :] = jnp.broadcast_to(total[288:289, :], (64, PT))
+    total = jnp.sum(in_ref[...], axis=0)
+    for i in range(8):
+        out_ref[i] = total
 
 
 def combine_kernel(in_ref, out_ref, coef_ref):
-    total = jnp.sum(in_ref[...].reshape(64, 8, PT), axis=0)
+    total = jnp.sum(in_ref[...], axis=0)
     lane = lanes(1)
 
     def entry(i):
-        return jnp.sum(jnp.where(lane == i, total[6:7, :], 0.0), axis=1, keepdims=True)
+        return jnp.sum(jnp.where(lane == i, total[36:37, :], 0.0), axis=1, keepdims=True)
 
     g00, g01, g11, g02, g12, g22 = [entry(i) for i in range(6)]
     alpha = g01 / g00
@@ -439,19 +439,12 @@
     w0 = (y0 - f10 * w1) / f00
     c1 = -w1 / pn
     c0 = w0 / beta - c1 * alpha
-    mixed = c0 * total[0:3, :] + c1 * total[3:6, :]
-    mixed = jnp.concatenate([mixed, jnp.zeros((1, PT), F32)] * 2, axis=0)
-    for i in range(32):
-        out_ref[8 * i : 8 * i + 8, :] = mixed
+    mixed = c0 * total[0:18, :] + c1 * total[18:36, :]
+    mixed = jnp.concatenate([mixed, jnp.zeros((BACK - 18, PT), F32)] * 2, axis=0)
+    for i in range(16):
+        out_ref[2 * BACK * i : 2 * BACK * (i + 1), :] = mixed
     coef_ref[0:4, :] = jnp.broadcast_to(c0, (4, PT))
     coef_ref[4:8, :] = jnp.broadcast_to(c1, (4, PT))
-
-
-def copies_kernel(in_ref, out_ref):
-    for j in range(3):
-        rows = in_ref[pl.ds(j, 48, 4), :]
-        for i in range(4):
-            out_ref[i, 48 * j : 48 * (j + 1), :] = rows
 
 
 def expand_kernel(tile_ref, own_ref, other_ref, vec_ref, coef_ref, out_ref, adj_ref):
@@ -460,8 +453,10 @@
     for ref, first in ((own_ref, 2 * core), (other_ref, 2 - 2 * core)):
         for k in range(2):
             for h in range(2):
-                block = ref[2 * k + h]
-                at = h * HALF
+                base, at = (2 * k + h) * 8 * BACK, h * HALF
+                block = jnp.concatenate(
+                    [ref[pl.ds(base + i, 8, BACK), :] for i in range(18)], axis=0
+                )
                 edge = block[96:144, :]
                 out_ref[first + k, at : at + HALF, 0:PT] = block[0:HALF, :]
                 out_ref[first + k, at : at + 48, PT:W] = edge[:, 0:64]
@@ -487,7 +482,7 @@
 
 
 def swapped(one, two, axis):
-    n = lax.axis_size(axis)
+    n = math.prod(lax.axis_size(name) for name in axis)
     near = [(i, i ^ 1) for i in range(n)]
     far = [(i, i - 1 if i % 2 == 0 else i + 1) for i in range(1, n - 1)]
     return lax.ppermute(one, axis, near), lax.ppermute(two, axis, far)
@@ -504,8 +499,8 @@
     neighbours,
     particle_type,
 ):
-    n_short = lax.axis_size("gy")
-    tile = lax.axis_index("gx") * n_short + lax.axis_index("gy")
+    n_short = lax.axis_size("x") * lax.axis_size("c")
+    tile = lax.axis_index(TALL) * n_short + lax.axis_index(FLAT)
     tile = tile.astype(jnp.int32).reshape(1)
     kinds = particle_type.reshape(1, PT)
     (ids,) = call(
@@ -523,7 +518,7 @@
         smem=1,
         whole=1,
     )
-    x1, x2 = swapped(one, two, "gx")
+    x1, x2 = swapped(one, two, TALL)
     one, two = call(
         functools.partial(pack_short_kernel, n_short),
         [(ROWS, PT)] * 2,
@@ -536,7 +531,7 @@
         x2,
         smem=1,
     )
-    y1, y2 = swapped(one, two, "gy")
+    y1, y2 = swapped(one, two, FLAT)
 
     tw, lw, fw = call(
         weight_kernel,
@@ -591,18 +586,16 @@
         us=4,
         scratch_shapes=scratch,
     )
-    pairs = [(i, i ^ 1) for i in range(n_short)]
-    lines = [list(range(c, n_short, 2)) for c in range(2)]
-    partner = lax.ppermute(vectors, "gy", pairs)
-    (chunks,) = call(outer_kernel, [(4, CHUNK, PT)], tile, vectors, partner, smem=1)
-    got = lax.all_to_all(chunks, "gy", 0, 0, axis_index_groups=lines)
-    (pieces,) = call(spread_kernel, [(512, PT)], got)
-    got = lax.all_to_all(pieces.reshape(64, 8, PT), "gx", 0, 0)
-    mixed, coefs = call(combine_kernel, [(256, PT), (8, PT)], got.reshape(512, PT))
-    got = lax.all_to_all(mixed.reshape(64, 4, PT), "gx", 0, 0)
-    (copies,) = call(copies_kernel, [(4, 144, PT)], got.reshape(256, PT))
-    half = lax.all_to_all(copies, "gy", 0, 0, axis_index_groups=lines)
-    other = lax.ppermute(half, "gy", pairs)
+    pair = [(0, 1), (1, 0)]
+    partner = lax.ppermute(vectors, "c", pair)
+    (chunks,) = call(outer_kernel, [(32 * CHUNK, PT)], tile, vectors, partner, smem=1)
+    got = lax.all_to_all(chunks.reshape(32, CHUNK, PT), ("y", "x"), 0, 0)
+    (pieces,) = call(spread_kernel, [(8, CHUNK, PT)], got)
+    got = lax.all_to_all(pieces, "z", 0, 0)
+    mixed, coefs = call(combine_kernel, [(32 * BACK, PT), (8, PT)], got)
+    got = lax.all_to_all(mixed.reshape(32, BACK, PT), ("y", "x"), 0, 0)
+    half = got.reshape(32 * BACK, PT)
+    other = lax.ppermute(half, "c", pair)
     sensitivity, adjoint = call(
         expand_kernel,
         [(KINDS, W, W), (W, PT)],
@@ -617,17 +610,9 @@
 
 
 def solution(mesh):
-    placed = (
-        P(None, ("gx", "gy")),
-        P(None, ("gx", "gy")),
-        P(None, ("gx", "gy")),
-        P(),
-        P(),
-        P(),
-        P(),
-        P(None, ("gx", "gy")),
-        P(("gx", "gy")),
-    )
+    fine = Mesh(mesh.devices.reshape(8, 8, 4, 2), TALL + FLAT)
+    split_in = P(None, TALL + FLAT)
+    placed = (split_in, split_in, split_in, P(), P(), P(), P(), split_in, P(TALL + FLAT))
     return jax.shard_map(
-        body, mesh=mesh, in_specs=placed, out_specs=(P(None, ("gx", "gy")), P()), check_vma=False
-    )
+        body, mesh=fine, in_specs=placed, out_specs=(split_in, P()), check_vma=False
+    )

time: 107 us -> 105 us (0.981)
  blocking collectives: 65.5 us -> 62.1 us
    all_to_all x4 -> x3, blocking collectives: 65.5 us -> 62.1 us  [the longest x1 27.1 us: body(): got = lax.all_to_all(chunks.reshape(32, CHUNK, PT), ('y', 'x'), 0, 0)]
    pallas_call x11 -> x10, Pallas kernels: 10.3 us -> 10.3 us  [call(): pl.pallas_call(kernel, out_shape=[s if isinstance(s, jax.ShapeDtypeStruct...]
where the time goes in v9:
time: 105 us; the launch traced here: 104 us
  blocking collectives  62.1 us (59%)
  starting transfers between devices  25.1 us (24%)
  Pallas kernels  10.3 us (10%)
  waiting for transfers between devices  4.95 us (5%)
    all_to_all x1, blocking collectives, body(): got = lax.all_to_all(chunks.reshape(32, CHUNK, PT), ('y', 'x'), 0, 0)  27.1 us
    all_to_all x1, blocking collectives, body(): got = lax.all_to_all(pieces, 'z', 0, 0)  18.2 us
    all_to_all x1, blocking collectives, body(): got = lax.all_to_all(mixed.reshape(32, BACK, PT), ('y', 'x'), 0, 0)  16.8 us
    ppermute x4, starting transfers between devices, swapped(): return (lax.ppermute(one, axis, near), lax.ppermute(two, axis, far))  16 us
    pallas_call x10, Pallas kernels, call(): pl.pallas_call(kernel, out_shape=[s if isinstance(s, jax.ShapeDtypeStruct...  10.3 us
    ppermute x1, starting transfers between devices, body(): other = lax.ppermute(half, 'c', pair)  7.19 us
  transfers between devices with their start and end apart: 6, of which 4 were waited for; matrix products, arithmetic and copies ran while one was open for 0% of the time, Pallas kernels for 4%

profile of v9, /device:TPU:1, one launch (start us, length us, event | category | flops | bytes accessed | tf_op | source)
XLA Modules:
  0.0 104.1 jit_solution(12611701634674574179)
XLA Ops:
  0.6 0.0 copy-start.4
  0.7 0.0 copy-start.5
  0.7 0.0 copy-start.7
  0.7 0.0 copy-start.8
  0.7 0.1 shard_map.104._.ids_ref
  0.8 0.7 copy-done.4
  1.5 0.0 copy-done.5
  1.6 0.0 copy-done.7
  1.6 0.0 copy-done.8
  1.6 0.0 copy-start
  1.6 0.0 copy-start.1
  1.6 0.0 copy-start.2
  1.6 0.0 copy-start.3
  1.6 0.1 shard_map.105
  1.7 4.2 %collective-permute-start = (f32[304,128]{1,0:T(8,128)S(1)}, f32[304,128]{1,0:T(8,128)S(1)}, u32[]{:S(2)}, u32[]{:S(2)}) collective-permute-start(f32[304,128]{1,0:T(8,128)S(1)} %get-tuple-element.16), channel_id=1, source_target_pairs={{0,8},{8,0},{16,24},{24,16},{32,40},{40,32},{48,56},{56,48},{64,72... | collective-permute-start | bytes 466952 | tf_op jit(solution)/shard_map/ppermute | solution.py:488
  5.9 0.7 collective-permute-start.1
  6.6 0.0 copy-done
  6.6 0.0 copy-done.1
  6.6 0.0 copy-done.2
  6.6 0.0 copy-done.3
  6.6 0.7 shard_map.107
  7.4 1.1 %collective-permute-done.x1_ref = f32[304,128]{1,0:T(8,128)S(1)} collective-permute-done((f32[304,128]{1,0:T(8,128)S(1)}, f32[304,128]{1,0:T(8,128)S(1)}, u32[]{:S(2)}, u32[]{:S(2)}) %collective-permute-start) | collective-permute-done | bytes 155680 | tf_op jit(solution)/shard_map/ppermute | solution.py:488
  8.5 0.0 collective-permute-done.1.x2_ref
  8.5 0.3 shard_map.106
  8.8 9.3 %collective-permute-start.2 = (f32[208,128]{1,0:T(8,128)S(1)}, f32[208,128]{1,0:T(8,128)S(1)}, u32[]{:S(2)}, u32[]{:S(2)}) collective-permute-start(f32[208,128]{1,0:T(8,128)S(1)} %get-tuple-element.18), channel_id=1, source_target_pairs={{0,1},{1,0},{2,3},{3,2},{4,5},{5,4},{6,7},{7,6},{8,9},{9,8},{10,11... | collective-permute-start | bytes 319496 | tf_op jit(solution)/shard_map/ppermute | solution.py:488
  18.1 1.9 %collective-permute-start.3 = (f32[208,128]{1,0:T(8,128)S(1)}, f32[208,128]{1,0:T(8,128)S(1)}, u32[]{:S(2)}, u32[]{:S(2)}) collective-permute-start(f32[208,128]{1,0:T(8,128)S(1)} %get-tuple-element.19), channel_id=1, source_target_pairs={{1,2},{2,1},{3,4},{4,3},{5,6},{6,5},{9,10},{10,9},{11,12},{12,11},... | collective-permute-start | bytes 319496 | tf_op jit(solution)/shard_map/ppermute | solution.py:488
  20.0 0.0 copy-start.6
  20.1 3.1 %shard_map.108 = (f32[192,256]{1,0:T(8,128)S(1)}, bf16[384,384]{1,0:T(8,128)(2,1)S(1)}, bf16[2048,256]{1,0:T(8,128)(2,1)S(1)}) custom-call(s32[1]{0:T(128)} %bitcast.tile_ref, f32[512,128]{1,0:T(8,128)S(1)} %shard_map.104._.ids_ref, f32[192,128]{1,0:T(8,128)S(1)} %copy-done.5, s32[10,128]{1,0:T(8,128)S(1)} %copy-done.7, s32[1,128]{1,0:T(1,128)S(1)} %bitcast.11, ...), custom_call_target="tpu_custom_call" | custom-call | flops 4000000000 | bytes 12000000 | tf_op jit(solution)/shard_map/pallas_call | solution.py:467
  23.2 0.0 collective-permute-done.2.y1_ref
  23.2 0.9 collective-permute-done.3.y2_ref
  24.1 0.0 copy-done.6
  24.1 4.0 %shard_map.109.own_ref.vec_ref = f32[584,128]{1,0:T(8,128)S(1)} custom-call(s32[1]{0:T(128)} %bitcast.tile_ref, f32[512,128]{1,0:T(8,128)S(1)} %shard_map.104._.ids_ref, f32[192,128]{1,0:T(8,128)S(1)} %copy-done.5, s32[10,128]{1,0:T(8,128)S(1)} %copy-done.7, s32[1,128]{1,0:T(1,128)S(1)} %bitcast.12, f32[192,128]{1,0:T(8,128)S(1)} %copy-done.6, ...), custom_call_target="tpu_custom_call" | custom-call | flops 4000000000 | bytes 12000000 | tf_op jit(solution)/shard_map/pallas_call | solution.py:467
  28.2 1.9 %collective-permute-start.4 = (f32[584,128]{1,0:T(8,128)S(1)}, f32[584,128]{1,0:T(8,128)S(1)}, u32[]{:S(2)}, u32[]{:S(2)}) collective-permute-start(f32[584,128]{1,0:T(8,128)S(1)} %shard_map.109.own_ref.vec_ref), channel_id=1, source_target_pairs={{0,1},{1,0},{2,3},{3,2},{4,5},{5,4},{6,7},{7,6},{8,9},{9,8},{10,11... | collective-permute-start | bytes 897032 | tf_op jit(solution)/shard_map/ppermute | solution.py:590
  30.1 1.6 %collective-permute-done.4.other_ref = f32[584,128]{1,0:T(8,128)S(1)} collective-permute-done((f32[584,128]{1,0:T(8,128)S(1)}, f32[584,128]{1,0:T(8,128)S(1)}, u32[]{:S(2)}, u32[]{:S(2)}) %collective-permute-start.4) | collective-permute-done | bytes 299040 | tf_op jit(solution)/shard_map/ppermute | solution.py:590
  31.7 0.6 shard_map.110
  32.2 27.1 %all_to_all.15.in_ref = f32[32,40,128]{2,1,0:T(8,128)S(1)} all-to-all(f32[32,40,128]{2,1,0:T(8,128)S(1)} %bitcast.5), channel_id=1, replica_groups=mesh['z'=8,'y'=8,'x'=4,'c'=2] {'y','x'}, dimensions={0} | all-to-all | bytes 1310720 | tf_op jit(solution)/shard_map/all_to_all | solution.py:592
  59.4 0.1 shard_map.111
  59.4 18.2 %all_to_all.16.in_ref = f32[8,40,128]{2,1,0:T(8,128)S(1)} all-to-all(f32[8,40,128]{2,1,0:T(8,128)S(1)} %shard_map.111), channel_id=1, replica_groups=mesh['z'=8,'y'=8,'x'=4,'c'=2] {'z'}, dimensions={0} | all-to-all | bytes 327680 | tf_op jit(solution)/shard_map/all_to_all | solution.py:594
  77.6 0.2 shard_map.112
  77.8 16.8 %all_to_all.17 = f32[32,24,128]{2,1,0:T(8,128)S(1)} all-to-all(f32[32,24,128]{2,1,0:T(8,128)S(1)} %bitcast.8), channel_id=1, replica_groups=mesh['z'=8,'y'=8,'x'=4,'c'=2] {'y','x'}, dimensions={0} | all-to-all | bytes 786432 | tf_op jit(solution)/shard_map/all_to_all | solution.py:596
  94.6 7.2 %collective-permute-start.5 = (f32[768,128]{1,0:T(8,128)S(1)}, f32[768,128]{1,0:T(8,128)S(1)}, u32[]{:S(2)}, u32[]{:S(2)}) collective-permute-start(f32[768,128]{1,0:T(8,128)S(1)} %bitcast.6), channel_id=1, source_target_pairs={{0,1},{1,0},{2,3},{3,2},{4,5},{5,4},{6,7},{7,6},{8,9},{9,8},{10,11... | collective-permute-start | bytes 1179656 | tf_op jit(solution)/shard_map/ppermute | solution.py:598
  101.8 1.3 %collective-permute-done.5.other_ref = f32[768,128]{1,0:T(8,128)S(1)} collective-permute-done((f32[768,128]{1,0:T(8,128)S(1)}, f32[768,128]{1,0:T(8,128)S(1)}, u32[]{:S(2)}, u32[]{:S(2)}) %collective-permute-start.5) | collective-permute-done | bytes 393248 | tf_op jit(solution)/shard_map/ppermute | solution.py:598
  103.1 1.0 %shard_map.113 = (f32[4,192,192]{2,1,0:T(8,128)}, f32[192,128]{1,0:T(8,128)}) custom-call(s32[1]{0:T(128)} %bitcast.tile_ref, f32[768,128]{1,0:T(8,128)S(1)} %bitcast.7, f32[768,128]{1,0:T(8,128)S(1)} %collective-permute-done.5.other_ref, f32[584,128]{1,0:T(8,128)S(1)} %shard_map.109.own_ref.vec_ref, f32[8,128]{1,0:T(8,128)S(1)} %get-tuple-element.27.coef_ref), custom_call_target="tpu_custom_call" | custom-call | flops 1000000000 | bytes 3000000 | tf_op jit(solution)/shard_map/pallas_call | solution.py:467
Async XLA Ops:
  0.6 0.9 copy-start.4
  0.7 0.9 copy-start.5
  0.7 0.9 copy-start.7
  0.7 0.9 copy-start.8
  1.6 5.0 %copy-start = (f32[10,96,96]{2,1,0:T(8,128)S(1)}, f32[10,96,96]{2,1,0:T(8,128)}, u32[]{:S(2)}) copy-start(f32[10,96,96]{2,1,0:T(8,128)} %lr_ref.1) | copy-start | bytes 1105924
  1.6 5.0 %copy-start.1 = (f32[10,96,96]{2,1,0:T(8,128)S(1)}, f32[10,96,96]{2,1,0:T(8,128)}, u32[]{:S(2)}) copy-start(f32[10,96,96]{2,1,0:T(8,128)} %li_ref.1) | copy-start | bytes 1105924
  1.6 5.0 %copy-start.2 = (f32[4,96,96]{2,1,0:T(8,128)S(1)}, f32[4,96,96]{2,1,0:T(8,128)}, u32[]{:S(2)}) copy-start(f32[4,96,96]{2,1,0:T(8,128)} %tr_ref.1) | copy-start | bytes 442372
  1.6 5.0 %copy-start.3 = (f32[4,96,96]{2,1,0:T(8,128)S(1)}, f32[4,96,96]{2,1,0:T(8,128)}, u32[]{:S(2)}) copy-start(f32[4,96,96]{2,1,0:T(8,128)} %ti_ref.1) | copy-start | bytes 442372
  1.7 6.8 %collective-permute-start = (f32[304,128]{1,0:T(8,128)S(1)}, f32[304,128]{1,0:T(8,128)S(1)}, u32[]{:S(2)}, u32[]{:S(2)}) collective-permute-start(f32[304,128]{1,0:T(8,128)S(1)} %get-tuple-element.16), channel_id=1, source_target_pairs={{0,8},{8,0},{16,24},{24,16},{32,40},{40,32},{48,56},{56,48},{64,72... | collective-permute-start | bytes 466952 | tf_op jit(solution)/shard_map/ppermute | solution.py:488
  5.9 2.6 %collective-permute-start.1 = (f32[304,128]{1,0:T(8,128)S(1)}, f32[304,128]{1,0:T(8,128)S(1)}, u32[]{:S(2)}, u32[]{:S(2)}) collective-permute-start(f32[304,128]{1,0:T(8,128)S(1)} %get-tuple-element.17), channel_id=1, source_target_pairs={{8,16},{16,8},{24,32},{32,24},{40,48},{48,40},{56,64},{64,56},{72,... | collective-permute-start | bytes 466952 | tf_op jit(solution)/shard_map/ppermute | solution.py:488
  8.8 14.4 %collective-permute-start.2 = (f32[208,128]{1,0:T(8,128)S(1)}, f32[208,128]{1,0:T(8,128)S(1)}, u32[]{:S(2)}, u32[]{:S(2)}) collective-permute-start(f32[208,128]{1,0:T(8,128)S(1)} %get-tuple-element.18), channel_id=1, source_target_pairs={{0,1},{1,0},{2,3},{3,2},{4,5},{5,4},{6,7},{7,6},{8,9},{9,8},{10,11... | collective-permute-start | bytes 319496 | tf_op jit(solution)/shard_map/ppermute | solution.py:488
  18.1 6.0 %collective-permute-start.3 = (f32[208,128]{1,0:T(8,128)S(1)}, f32[208,128]{1,0:T(8,128)S(1)}, u32[]{:S(2)}, u32[]{:S(2)}) collective-permute-start(f32[208,128]{1,0:T(8,128)S(1)} %get-tuple-element.19), channel_id=1, source_target_pairs={{1,2},{2,1},{3,4},{4,3},{5,6},{6,5},{9,10},{10,9},{11,12},{12,11},... | collective-permute-start | bytes 319496 | tf_op jit(solution)/shard_map/ppermute | solution.py:488
  20.0 4.1 %copy-start.6 = (f32[192,128]{1,0:T(8,128)S(1)}, f32[192,128]{1,0:T(8,128)}, u32[]{:S(2)}) copy-start(f32[192,128]{1,0:T(8,128)} %inc_ref.1) | copy-start | bytes 294916
  28.2 3.5 %collective-permute-start.4 = (f32[584,128]{1,0:T(8,128)S(1)}, f32[584,128]{1,0:T(8,128)S(1)}, u32[]{:S(2)}, u32[]{:S(2)}) collective-permute-start(f32[584,128]{1,0:T(8,128)S(1)} %shard_map.109.own_ref.vec_ref), channel_id=1, source_target_pairs={{0,1},{1,0},{2,3},{3,2},{4,5},{5,4},{6,7},{7,6},{8,9},{9,8},{10,11... | collective-permute-start | bytes 897032 | tf_op jit(solution)/shard_map/ppermute | solution.py:590
  94.6 8.5 %collective-permute-start.5 = (f32[768,128]{1,0:T(8,128)S(1)}, f32[768,128]{1,0:T(8,128)S(1)}, u32[]{:S(2)}, u32[]{:S(2)}) collective-permute-start(f32[768,128]{1,0:T(8,128)S(1)} %bitcast.6), channel_id=1, source_target_pairs={{0,1},{1,0},{2,3},{3,2},{4,5},{5,4},{6,7},{7,6},{8,9},{9,8},{10,11... | collective-permute-start | bytes 1179656 | tf_op jit(solution)/shard_map/ppermute | solution.py:598

commit v10 on v9

--- a/solution.py
+++ b/solution.py
@@ -392,10 +392,11 @@
             for h in range(2):
                 block = out[which * W + h * HALF : which * W + (h + 1) * HALF, :]
                 edge = block[0:48, PT:] + pltpu.roll(block[48:96, PT:], 64, 1)
-                at = (2 * k + h) * 8 * CHUNK + which * 18
+                at = (2 * k + h) * 2 * CHUNK + which * 18
                 for i in range(18):
                     rows = block[8 * i : 8 * i + 8, 0:PT] if i < 12 else edge[8 * i - 96 : 8 * i - 88]
-                    chunk_ref[pl.ds(at + i, 8, CHUNK), :] = rows
+                    chunk_ref[pl.ds(at + i, 4, 8 * CHUNK), :] = rows[0:4]
+                    chunk_ref[pl.ds(at + CHUNK + i, 4, 8 * CHUNK), :] = rows[4:8]
     gram = own_ref[3 * W : 3 * W + 1, :] + other_ref[3 * W : 3 * W + 1, :]
     for i in range(36, CHUNK):
         row = gram if i == 36 else jnp.zeros((1, PT), F32)
@@ -406,6 +407,10 @@
     total = jnp.sum(in_ref[...], axis=0)
     for i in range(8):
         out_ref[i] = total
+
+
+def sum_kernel(in_ref, out_ref):
+    out_ref[...] = jnp.sum(in_ref[...], axis=0)
 
 
 def combine_kernel(in_ref, out_ref, coef_ref):
@@ -589,7 +594,9 @@
     pair = [(0, 1), (1, 0)]
     partner = lax.ppermute(vectors, "c", pair)
     (chunks,) = call(outer_kernel, [(32 * CHUNK, PT)], tile, vectors, partner, smem=1)
-    got = lax.all_to_all(chunks.reshape(32, CHUNK, PT), ("y", "x"), 0, 0)
+    got = lax.all_to_all(chunks.reshape(4, 8 * CHUNK, PT), "x", 0, 0)
+    (part,) = call(sum_kernel, [(8 * CHUNK, PT)], got)
+    got = lax.all_to_all(part.reshape(8, CHUNK, PT), "y", 0, 0)
     (pieces,) = call(spread_kernel, [(8, CHUNK, PT)], got)
     got = lax.all_to_all(pieces, "z", 0, 0)
     mixed, coefs = call(combine_kernel, [(32 * BACK, PT), (8, PT)], got)

time: 105 us -> 103 us (0.981)
    all_to_all x1, blocking collectives: 16.8 us -> 14.8 us  [body(): got = lax.all_to_all(mixed.reshape(32, BACK, PT), ('y', 'x'), 0, 0)]
    all_to_all x1 -> x2, blocking collectives: 27.1 us -> 28.1 us  [the longest x1 15.1 us: body(): got = lax.all_to_all(part.reshape(8, CHUNK, PT), 'y', 0, 0)]
    pallas_call x10 -> x11, Pallas kernels: 10.3 us -> 10.5 us  [call(): pl.pallas_call(kernel, out_shape=[s if isinstance(s, jax.ShapeDtypeStruct...]
where the time goes in v10:
time: 103 us
  blocking collectives  61.1 us (59%)
  starting transfers between devices  24.6 us (24%)
  Pallas kernels  10.5 us (10%)
  waiting for transfers between devices  4.95 us (5%)
    all_to_all x1, blocking collectives, body(): got = lax.all_to_all(pieces, 'z', 0, 0)  18.2 us
    ppermute x4, starting transfers between devices, swapped(): return (lax.ppermute(one, axis, near), lax.ppermute(two, axis, far))  16 us
    all_to_all x1, blocking collectives, body(): got = lax.all_to_all(part.reshape(8, CHUNK, PT), 'y', 0, 0)  15.1 us
    all_to_all x1, blocking collectives, body(): got = lax.all_to_all(mixed.reshape(32, BACK, PT), ('y', 'x'), 0, 0)  14.8 us
    all_to_all x1, blocking collectives, body(): got = lax.all_to_all(chunks.reshape(4, 8 * CHUNK, PT), 'x', 0, 0)  13 us
    pallas_call x11, Pallas kernels, call(): pl.pallas_call(kernel, out_shape=[s if isinstance(s, jax.ShapeDtypeStruct...  10.5 us
    ppermute x1, starting transfers between devices, body(): other = lax.ppermute(half, 'c', pair)  6.69 us
    ppermute x4, waiting for transfers between devices, swapped(): return (lax.ppermute(one, axis, near), lax.ppermute(two, axis, far))  2.07 us
  transfers between devices with their start and end apart: 6, of which 4 were waited for; matrix products, arithmetic and copies ran while one was open for 0% of the time, Pallas kernels for 4%

profile of v10, /device:TPU:1, one launch (start us, length us, event | category | flops | bytes accessed | tf_op | source)
XLA Modules:
  0.0 102.8 jit_solution(1260974442725276465)
XLA Ops:
  0.6 0.0 copy-start.4
  0.7 0.0 copy-start.5
  0.7 0.0 copy-start.7
  0.7 0.0 copy-start.8
  0.7 0.1 shard_map.104._.ids_ref
  0.8 0.7 copy-done.4
  1.5 0.0 copy-done.5
  1.6 0.0 copy-done.7
  1.6 0.0 copy-done.8
  1.6 0.0 copy-start
  1.6 0.0 copy-start.1
  1.6 0.0 copy-start.2
  1.6 0.0 copy-start.3
  1.6 0.1 shard_map.105
  1.7 4.2 %collective-permute-start = (f32[304,128]{1,0:T(8,128)S(1)}, f32[304,128]{1,0:T(8,128)S(1)}, u32[]{:S(2)}, u32[]{:S(2)}) collective-permute-start(f32[304,128]{1,0:T(8,128)S(1)} %get-tuple-element.16), channel_id=1, source_target_pairs={{0,8},{8,0},{16,24},{24,16},{32,40},{40,32},{48,56},{56,48},{64,72... | collective-permute-start | bytes 466952 | tf_op jit(solution)/shard_map/ppermute | solution.py:493
  5.9 0.7 collective-permute-start.1
  6.6 0.0 copy-done
  6.6 0.0 copy-done.1
  6.6 0.0 copy-done.2
  6.6 0.0 copy-done.3
  6.6 0.7 shard_map.107
  7.4 1.1 %collective-permute-done.x1_ref = f32[304,128]{1,0:T(8,128)S(1)} collective-permute-done((f32[304,128]{1,0:T(8,128)S(1)}, f32[304,128]{1,0:T(8,128)S(1)}, u32[]{:S(2)}, u32[]{:S(2)}) %collective-permute-start) | collective-permute-done | bytes 155680 | tf_op jit(solution)/shard_map/ppermute | solution.py:493
  8.5 0.0 collective-permute-done.1.x2_ref
  8.5 0.3 shard_map.106
  8.8 9.3 %collective-permute-start.2 = (f32[208,128]{1,0:T(8,128)S(1)}, f32[208,128]{1,0:T(8,128)S(1)}, u32[]{:S(2)}, u32[]{:S(2)}) collective-permute-start(f32[208,128]{1,0:T(8,128)S(1)} %get-tuple-element.18), channel_id=1, source_target_pairs={{0,1},{1,0},{2,3},{3,2},{4,5},{5,4},{6,7},{7,6},{8,9},{9,8},{10,11... | collective-permute-start | bytes 319496 | tf_op jit(solution)/shard_map/ppermute | solution.py:493
  18.1 1.9 %collective-permute-start.3 = (f32[208,128]{1,0:T(8,128)S(1)}, f32[208,128]{1,0:T(8,128)S(1)}, u32[]{:S(2)}, u32[]{:S(2)}) collective-permute-start(f32[208,128]{1,0:T(8,128)S(1)} %get-tuple-element.19), channel_id=1, source_target_pairs={{1,2},{2,1},{3,4},{4,3},{5,6},{6,5},{9,10},{10,9},{11,12},{12,11},... | collective-permute-start | bytes 319496 | tf_op jit(solution)/shard_map/ppermute | solution.py:493
  20.0 0.0 copy-start.6
  20.1 3.1 %shard_map.108 = (f32[192,256]{1,0:T(8,128)S(1)}, bf16[384,384]{1,0:T(8,128)(2,1)S(1)}, bf16[2048,256]{1,0:T(8,128)(2,1)S(1)}) custom-call(s32[1]{0:T(128)} %bitcast.tile_ref, f32[512,128]{1,0:T(8,128)S(1)} %shard_map.104._.ids_ref, f32[192,128]{1,0:T(8,128)S(1)} %copy-done.5, s32[10,128]{1,0:T(8,128)S(1)} %copy-done.7, s32[1,128]{1,0:T(1,128)S(1)} %bitcast.13, ...), custom_call_target="tpu_custom_call" | custom-call | flops 4000000000 | bytes 12000000 | tf_op jit(solution)/shard_map/pallas_call | solution.py:472
  23.2 0.0 collective-permute-done.2.y1_ref
  23.2 0.9 collective-permute-done.3.y2_ref
  24.1 0.0 copy-done.6
  24.1 4.0 %shard_map.109.own_ref.vec_ref = f32[584,128]{1,0:T(8,128)S(1)} custom-call(s32[1]{0:T(128)} %bitcast.tile_ref, f32[512,128]{1,0:T(8,128)S(1)} %shard_map.104._.ids_ref, f32[192,128]{1,0:T(8,128)S(1)} %copy-done.5, s32[10,128]{1,0:T(8,128)S(1)} %copy-done.7, s32[1,128]{1,0:T(1,128)S(1)} %bitcast.14, f32[192,128]{1,0:T(8,128)S(1)} %copy-done.6, ...), custom_call_target="tpu_custom_call" | custom-call | flops 4000000000 | bytes 12000000 | tf_op jit(solution)/shard_map/pallas_call | solution.py:472
  28.2 1.9 %collective-permute-start.4 = (f32[584,128]{1,0:T(8,128)S(1)}, f32[584,128]{1,0:T(8,128)S(1)}, u32[]{:S(2)}, u32[]{:S(2)}) collective-permute-start(f32[584,128]{1,0:T(8,128)S(1)} %shard_map.109.own_ref.vec_ref), channel_id=1, source_target_pairs={{0,1},{1,0},{2,3},{3,2},{4,5},{5,4},{6,7},{7,6},{8,9},{9,8},{10,11... | collective-permute-start | bytes 897032 | tf_op jit(solution)/shard_map/ppermute | solution.py:595
  30.1 1.6 %collective-permute-done.4.other_ref = f32[584,128]{1,0:T(8,128)S(1)} collective-permute-done((f32[584,128]{1,0:T(8,128)S(1)}, f32[584,128]{1,0:T(8,128)S(1)}, u32[]{:S(2)}, u32[]{:S(2)}) %collective-permute-start.4) | collective-permute-done | bytes 299040 | tf_op jit(solution)/shard_map/ppermute | solution.py:595
  31.7 0.8 shard_map.110
  32.4 13.0 %all_to_all.20.in_ref = f32[4,320,128]{2,1,0:T(8,128)S(1)} all-to-all(f32[4,320,128]{2,1,0:T(8,128)S(1)} %bitcast.6), channel_id=1, replica_groups=mesh['z'=8,'y'=8,'x'=4,'c'=2] {'x'}, dimensions={0} | all-to-all | bytes 1310720 | tf_op jit(solution)/shard_map/all_to_all | solution.py:597
  45.5 15.1 %all_to_all.21.in_ref = f32[8,40,128]{2,1,0:T(8,128)S(1)} all-to-all(f32[8,40,128]{2,1,0:T(8,128)S(1)} %bitcast.10), channel_id=1, replica_groups=mesh['z'=8,'y'=8,'x'=4,'c'=2] {'y'}, dimensions={0} | all-to-all | bytes 327680 | tf_op jit(solution)/shard_map/all_to_all | solution.py:599
  60.5 18.2 %all_to_all.22.in_ref = f32[8,40,128]{2,1,0:T(8,128)S(1)} all-to-all(f32[8,40,128]{2,1,0:T(8,128)S(1)} %shard_map.112), channel_id=1, replica_groups=mesh['z'=8,'y'=8,'x'=4,'c'=2] {'z'}, dimensions={0} | all-to-all | bytes 327680 | tf_op jit(solution)/shard_map/all_to_all | solution.py:601
  78.8 0.2 shard_map.113
  78.9 14.8 %all_to_all.23 = f32[32,24,128]{2,1,0:T(8,128)S(1)} all-to-all(f32[32,24,128]{2,1,0:T(8,128)S(1)} %bitcast.9), channel_id=1, replica_groups=mesh['z'=8,'y'=8,'x'=4,'c'=2] {'y','x'}, dimensions={0} | all-to-all | bytes 786432 | tf_op jit(solution)/shard_map/all_to_all | solution.py:603
  93.7 6.7 %collective-permute-start.5 = (f32[768,128]{1,0:T(8,128)S(1)}, f32[768,128]{1,0:T(8,128)S(1)}, u32[]{:S(2)}, u32[]{:S(2)}) collective-permute-start(f32[768,128]{1,0:T(8,128)S(1)} %bitcast.7), channel_id=1, source_target_pairs={{0,1},{1,0},{2,3},{3,2},{4,5},{5,4},{6,7},{7,6},{8,9},{9,8},{10,11... | collective-permute-start | bytes 1179656 | tf_op jit(solution)/shard_map/ppermute | solution.py:605
  100.4 1.3 %collective-permute-done.5.other_ref = f32[768,128]{1,0:T(8,128)S(1)} collective-permute-done((f32[768,128]{1,0:T(8,128)S(1)}, f32[768,128]{1,0:T(8,128)S(1)}, u32[]{:S(2)}, u32[]{:S(2)}) %collective-permute-start.5) | collective-permute-done | bytes 393248 | tf_op jit(solution)/shard_map/ppermute | solution.py:605
  101.7 1.0 %shard_map.114 = (f32[4,192,192]{2,1,0:T(8,128)}, f32[192,128]{1,0:T(8,128)}) custom-call(s32[1]{0:T(128)} %bitcast.tile_ref, f32[768,128]{1,0:T(8,128)S(1)} %bitcast.8, f32[768,128]{1,0:T(8,128)S(1)} %collective-permute-done.5.other_ref, f32[584,128]{1,0:T(8,128)S(1)} %shard_map.109.own_ref.vec_ref, f32[8,128]{1,0:T(8,128)S(1)} %get-tuple-element.27.coef_ref), custom_call_target="tpu_custom_call" | custom-call | flops 1000000000 | bytes 3000000 | tf_op jit(solution)/shard_map/pallas_call | solution.py:472
  (2 shorter events, 0.1 us)
Async XLA Ops:
  0.6 0.9 copy-start.4
  0.7 0.9 copy-start.5
  0.7 0.9 copy-start.7
  0.7 0.9 copy-start.8
  1.6 5.0 %copy-start = (f32[10,96,96]{2,1,0:T(8,128)S(1)}, f32[10,96,96]{2,1,0:T(8,128)}, u32[]{:S(2)}) copy-start(f32[10,96,96]{2,1,0:T(8,128)} %lr_ref.1) | copy-start | bytes 1105924
  1.6 5.0 %copy-start.1 = (f32[10,96,96]{2,1,0:T(8,128)S(1)}, f32[10,96,96]{2,1,0:T(8,128)}, u32[]{:S(2)}) copy-start(f32[10,96,96]{2,1,0:T(8,128)} %li_ref.1) | copy-start | bytes 1105924
  1.6 5.0 %copy-start.2 = (f32[4,96,96]{2,1,0:T(8,128)S(1)}, f32[4,96,96]{2,1,0:T(8,128)}, u32[]{:S(2)}) copy-start(f32[4,96,96]{2,1,0:T(8,128)} %tr_ref.1) | copy-start | bytes 442372
  1.6 5.0 %copy-start.3 = (f32[4,96,96]{2,1,0:T(8,128)S(1)}, f32[4,96,96]{2,1,0:T(8,128)}, u32[]{:S(2)}) copy-start(f32[4,96,96]{2,1,0:T(8,128)} %ti_ref.1) | copy-start | bytes 442372
  1.7 6.8 %collective-permute-start = (f32[304,128]{1,0:T(8,128)S(1)}, f32[304,128]{1,0:T(8,128)S(1)}, u32[]{:S(2)}, u32[]{:S(2)}) collective-permute-start(f32[304,128]{1,0:T(8,128)S(1)} %get-tuple-element.16), channel_id=1, source_target_pairs={{0,8},{8,0},{16,24},{24,16},{32,40},{40,32},{48,56},{56,48},{64,72... | collective-permute-start | bytes 466952 | tf_op jit(solution)/shard_map/ppermute | solution.py:493
  5.9 2.6 %collective-permute-start.1 = (f32[304,128]{1,0:T(8,128)S(1)}, f32[304,128]{1,0:T(8,128)S(1)}, u32[]{:S(2)}, u32[]{:S(2)}) collective-permute-start(f32[304,128]{1,0:T(8,128)S(1)} %get-tuple-element.17), channel_id=1, source_target_pairs={{8,16},{16,8},{24,32},{32,24},{40,48},{48,40},{56,64},{64,56},{72,... | collective-permute-start | bytes 466952 | tf_op jit(solution)/shard_map/ppermute | solution.py:493
  8.8 14.4 %collective-permute-start.2 = (f32[208,128]{1,0:T(8,128)S(1)}, f32[208,128]{1,0:T(8,128)S(1)}, u32[]{:S(2)}, u32[]{:S(2)}) collective-permute-start(f32[208,128]{1,0:T(8,128)S(1)} %get-tuple-element.18), channel_id=1, source_target_pairs={{0,1},{1,0},{2,3},{3,2},{4,5},{5,4},{6,7},{7,6},{8,9},{9,8},{10,11... | collective-permute-start | bytes 319496 | tf_op jit(solution)/shard_map/ppermute | solution.py:493
  18.1 6.0 %collective-permute-start.3 = (f32[208,128]{1,0:T(8,128)S(1)}, f32[208,128]{1,0:T(8,128)S(1)}, u32[]{:S(2)}, u32[]{:S(2)}) collective-permute-start(f32[208,128]{1,0:T(8,128)S(1)} %get-tuple-element.19), channel_id=1, source_target_pairs={{1,2},{2,1},{3,4},{4,3},{5,6},{6,5},{9,10},{10,9},{11,12},{12,11},... | collective-permute-start | bytes 319496 | tf_op jit(solution)/shard_map/ppermute | solution.py:493
  20.0 4.1 %copy-start.6 = (f32[192,128]{1,0:T(8,128)S(1)}, f32[192,128]{1,0:T(8,128)}, u32[]{:S(2)}) copy-start(f32[192,128]{1,0:T(8,128)} %inc_ref.1) | copy-start | bytes 294916
  28.2 3.5 %collective-permute-start.4 = (f32[584,128]{1,0:T(8,128)S(1)}, f32[584,128]{1,0:T(8,128)S(1)}, u32[]{:S(2)}, u32[]{:S(2)}) collective-permute-start(f32[584,128]{1,0:T(8,128)S(1)} %shard_map.109.own_ref.vec_ref), channel_id=1, source_target_pairs={{0,1},{1,0},{2,3},{3,2},{4,5},{5,4},{6,7},{7,6},{8,9},{9,8},{10,11... | collective-permute-start | bytes 897032 | tf_op jit(solution)/shard_map/ppermute | solution.py:595
  93.7 8.0 %collective-permute-start.5 = (f32[768,128]{1,0:T(8,128)S(1)}, f32[768,128]{1,0:T(8,128)S(1)}, u32[]{:S(2)}, u32[]{:S(2)}) collective-permute-start(f32[768,128]{1,0:T(8,128)S(1)} %bitcast.7), channel_id=1, source_target_pairs={{0,1},{1,0},{2,3},{3,2},{4,5},{5,4},{6,7},{7,6},{8,9},{9,8},{10,11... | collective-permute-start | bytes 1179656 | tf_op jit(solution)/shard_map/ppermute | solution.py:605

commit v11 on v10

--- a/solution.py
+++ b/solution.py
@@ -197,8 +197,9 @@
 
 
 def narrow_product(w_ref, both):
+    n = both.shape[1] // 2
     rows = dot(w_ref[0:W, :], both)
-    return rows[:, 0:PT] + rows[:, PT:] + dot(w_ref[W : 2 * W, :], both[:, 0:PT])
+    return rows[:, 0:n] + rows[:, n:] + dot(w_ref[W : 2 * W, :], both[:, 0:n])
 
 
 def product(w_ref, hi, lo):
@@ -218,7 +219,7 @@
         whole = [jnp.concatenate([p[k] for p in pieces], axis=1) for k in range(KINDS)]
         return jnp.concatenate([w[0:HALF] for w in whole] + [w[HALF:W] for w in whole], axis=0)
 
-    s_hi, s_lo = split(product(tw_ref, by_part(his), by_part(los)))
+    s_hi, s_lo = split(narrow_product(tw_ref, jnp.concatenate([by_part(his), by_part(los)], axis=1)))
     return jnp.concatenate([s_hi, s_lo], axis=0)
 
 
@@ -244,7 +245,7 @@
             ref[at : at + rows, :] = jnp.zeros((rows, ref.shape[1]), BF16)
 
 
-def scatter_pairs(ref, stack, ids, metas):
+def scatter_pairs(ref, stack, ids, metas, start_ref=None):
     for s in range(0, SLOTS, 2):
         pick = jnp.concatenate(
             [
@@ -254,7 +255,10 @@
             axis=0,
         )
         g = dot_nt(stack, pick)
-        parts = split(g[0:W] + g[W : 2 * W])
+        g = g[0:W] + g[W : 2 * W]
+        if start_ref is not None:
+            g = g + start_ref[s * HALF : s * HALF + W, :]
+        parts = split(g)
         for t in (0, 1):
             place(beside(ref), parts, s + t, slice(t * PT, (t + 1) * PT))
 
@@ -269,11 +273,22 @@
             place(beside(ref), parts, s + t, slice(t * PT, (t + 1) * PT))
 
 
+def first_kernel(ids_ref, b_ref, nb_ref, pt_ref, tw_ref, stack_ref, sum_ref):
+    ids = ids_ref[0 : 2 * PT, :]
+    own = meta_rows(nb_ref, pt_ref)
+    stack = scaled_by_type(tw_ref, (b_ref[...],), (own,))
+    stack_ref[...] = stack
+    for s in range(SLOTS):
+        g = dot_nt(stack, one_hot(ids, own, s))
+        sum_ref[s * W : (s + 1) * W, :] = g[0:W] + g[W : 2 * W]
+
+
 def early_kernel(
     short,
     tile_ref,
     ids_ref,
-    b_ref,
+    own_ref,
+    sum_ref,
     nb_ref,
     pt_ref,
     x1_ref,
@@ -282,7 +297,7 @@
     tw_ref,
     lw_ref,
     part_ref,
-    stack_ref,
+    edge_ref,
     f_ref,
     ghi_ref,
     glo_ref,
@@ -290,17 +305,28 @@
     wide = Tiles(even_row(short, tile_ref), x1_ref, x2_ref)
     v, m, half = slice(0, W), slice(W, ROWS), slice(ROWS, ROWS + HALF)
     refs = (ghi_ref, glo_ref)
-    ids = ids_ref[0 : 2 * PT, :]
+    ids, lr_ids = ids_ref[0 : 2 * PT, :], ids_ref[2 * PT : 3 * PT, :]
     own = meta_rows(nb_ref, pt_ref)
-    metas = (own, wide.below(m), wide.above(m))
+    metas = (wide.below(m), wide.above(m))
     clear_fill(refs + (f_ref,))
-    stack = scaled_by_type(tw_ref, (b_ref[...], wide.below(v), wide.above(v)), metas)
-    stack_ref[...] = stack
+    stack = scaled_by_type(tw_ref, (wide.below(v), wide.above(v)), metas)
     for s in range(SLOTS):
         pick = jnp.concatenate([one_hot(ids, meta, s) for meta in metas], axis=1)
         g = dot_nt(stack, pick)
-        place([(ref, slice(None)) for ref in refs], split(g[0:W] + g[W : 2 * W]), s, slice(None))
+        g = g[0:W] + g[W : 2 * W] + sum_ref[s * W : (s + 1) * W, :]
+        place([(ref, slice(None)) for ref in refs], split(g), s, slice(None))
     part_ref[...] = product(lw_ref, ghi_ref[...], glo_ref[...])
+    stack = jnp.concatenate([own_ref[...], stack], axis=1)
+    for s in range(0, SLOTS, 2):
+        pick = jnp.concatenate(
+            [
+                jnp.concatenate([one_hot(lr_ids, meta, t) for meta in (own,) + metas], axis=1)
+                for t in (s, s + 1)
+            ],
+            axis=0,
+        )
+        g = dot_nt(stack, pick)
+        edge_ref[s * HALF : s * HALF + W, :] = g[0:W] + g[W : 2 * W]
     fc_ud = unpack_fc(wide.below(half), wide.above(half))
     gather_pairs(f_ref, (fc_ref[...], fc_ud), ids, own)
 
@@ -318,7 +344,7 @@
     y1_ref,
     y2_ref,
     part_ref,
-    stack_ref,
+    edge_ref,
     f_ref,
     tw_ref,
     lw_ref,
@@ -347,8 +373,8 @@
     first, second = slice(0, PT), slice(PT, 2 * PT)
     own_ids, lr_ids, edge_ids = ids[0:PT, :], ids[2 * PT : 3 * PT, :], ids[3 * PT :, :]
 
-    stack = jnp.concatenate([stack_ref[...], scaled_by_type(tw_ref, (x_lr,), (m_b,))], axis=1)
-    scatter_pairs(g_ref, stack, (lr_ids, lr_ids, lr_ids, edge_ids), (m_own, m_up, m_dn, m_b))
+    stack = scaled_by_type(tw_ref, (x_lr,), (m_b,))
+    scatter_pairs(g_ref, stack, (edge_ids,), (m_b,), edge_ref)
     edge = narrow_product(lw_ref, g_ref[...])
     left, right = spot < 2, spot >= 30
     u1 = part_ref[:, first] + jnp.where(left | right, edge, 0.0)
@@ -549,14 +575,25 @@
         dtype=BF16,
     )
 
+    own = call(
+        first_kernel,
+        [jax.ShapeDtypeStruct((2 * W, PT), BF16), (SLOTS * W, 2 * PT)],
+        ids,
+        cost_grad,
+        neighbours,
+        kinds,
+        tw,
+        mib=16,
+        us=2,
+    )
     scratch = [pltpu.VMEM((2 * PART, 2 * PT), BF16)] * 2
     early = call(
         functools.partial(early_kernel, n_short),
-        [(W, 2 * PT), jax.ShapeDtypeStruct((2 * W, 3 * PT), BF16)]
+        [(W, 2 * PT), (SLOTS * HALF, 2 * PT)]
         + [jax.ShapeDtypeStruct((2 * PART, 2 * PT), BF16)],
         tile,
         ids,
-        cost_grad,
+        *own,
         neighbours,
         kinds,
         x1,

time: 103 us -> 103 us (level)
    pallas_call x11 -> x12, Pallas kernels: 10.5 us -> 10.8 us  [call(): pl.pallas_call(kernel, out_shape=[s if isinstance(s, jax.ShapeDtypeStruct...]
where the time goes in v11:
time: 103 us; the launch traced here: 102 us
  blocking collectives  61.1 us (59%)
  starting transfers between devices  24.6 us (24%)
  Pallas kernels  10.8 us (10%)
  waiting for transfers between devices  4.28 us (4%)
    all_to_all x1, blocking collectives, body(): got = lax.all_to_all(pieces, 'z', 0, 0)  18.2 us
    ppermute x4, starting transfers between devices, swapped(): return (lax.ppermute(one, axis, near), lax.ppermute(two, axis, far))  16 us
    all_to_all x1, blocking collectives, body(): got = lax.all_to_all(part.reshape(8, CHUNK, PT), 'y', 0, 0)  15.1 us
    all_to_all x1, blocking collectives, body(): got = lax.all_to_all(mixed.reshape(32, BACK, PT), ('y', 'x'), 0, 0)  14.8 us
    all_to_all x1, blocking collectives, body(): got = lax.all_to_all(chunks.reshape(4, 8 * CHUNK, PT), 'x', 0, 0)  13 us
    pallas_call x12, Pallas kernels, call(): pl.pallas_call(kernel, out_shape=[s if isinstance(s, jax.ShapeDtypeStruct...  10.8 us
    ppermute x1, starting transfers between devices, body(): other = lax.ppermute(half, 'c', pair)  6.69 us
  transfers between devices with their start and end apart: 6, of which 4 were waited for; matrix products, arithmetic and copies ran while one was open for 0% of the time, Pallas kernels for 4%

profile of v11, /device:TPU:1, one launch (start us, length us, event | category | flops | bytes accessed | tf_op | source)
XLA Modules:
  0.0 102.4 jit_solution(16330872439301495777)
XLA Ops:
  0.6 0.0 copy-start.4
  0.7 0.0 copy-start.5
  0.7 0.0 copy-start.7
  0.7 0.0 copy-start.8
  0.7 0.1 shard_map.104._.ids_ref
  0.8 0.7 copy-done.4
  1.5 0.0 copy-done.5
  1.6 0.0 copy-done.7
  1.6 0.0 copy-done.8
  1.6 0.0 copy-start
  1.6 0.0 copy-start.1
  1.6 0.0 copy-start.2
  1.6 0.0 copy-start.3
  1.6 0.1 shard_map.105
  1.7 4.2 %collective-permute-start = (f32[304,128]{1,0:T(8,128)S(1)}, f32[304,128]{1,0:T(8,128)S(1)}, u32[]{:S(2)}, u32[]{:S(2)}) collective-permute-start(f32[304,128]{1,0:T(8,128)S(1)} %get-tuple-element.18), channel_id=1, source_target_pairs={{0,8},{8,0},{16,24},{24,16},{32,40},{40,32},{48,56},{56,48},{64,72... | collective-permute-start | bytes 466952 | tf_op jit(solution)/shard_map/ppermute | solution.py:519
  5.9 0.7 collective-permute-start.1
  6.6 0.0 copy-done
  6.6 0.0 copy-done.1
  6.6 0.0 copy-done.2
  6.6 0.0 copy-done.3
  6.6 0.7 shard_map.107
  7.4 0.9 shard_map.108
  8.3 0.2 collective-permute-done.x1_ref
  8.5 0.0 collective-permute-done.1.x2_ref
  8.5 0.3 shard_map.106
  8.8 9.3 %collective-permute-start.2 = (f32[208,128]{1,0:T(8,128)S(1)}, f32[208,128]{1,0:T(8,128)S(1)}, u32[]{:S(2)}, u32[]{:S(2)}) collective-permute-start(f32[208,128]{1,0:T(8,128)S(1)} %get-tuple-element.20), channel_id=1, source_target_pairs={{0,1},{1,0},{2,3},{3,2},{4,5},{5,4},{6,7},{7,6},{8,9},{9,8},{10,11... | collective-permute-start | bytes 319496 | tf_op jit(solution)/shard_map/ppermute | solution.py:519
  18.1 1.9 %collective-permute-start.3 = (f32[208,128]{1,0:T(8,128)S(1)}, f32[208,128]{1,0:T(8,128)S(1)}, u32[]{:S(2)}, u32[]{:S(2)}) collective-permute-start(f32[208,128]{1,0:T(8,128)S(1)} %get-tuple-element.21), channel_id=1, source_target_pairs={{1,2},{2,1},{3,4},{4,3},{5,6},{6,5},{9,10},{10,9},{11,12},{12,11},... | collective-permute-start | bytes 319496 | tf_op jit(solution)/shard_map/ppermute | solution.py:519
  20.0 0.0 copy-start.6
  20.0 2.9 %shard_map.109 = (f32[192,256]{1,0:T(8,128)S(1)}, f32[960,256]{1,0:T(8,128)S(1)}, bf16[2048,256]{1,0:T(8,128)(2,1)S(1)}) custom-call(s32[1]{0:T(128)} %bitcast.tile_ref, f32[512,128]{1,0:T(8,128)S(1)} %shard_map.104._.ids_ref, bf16[384,128]{1,0:T(8,128)(2,1)S(1)} %get-tuple-element.23.own_ref, f32[1920,256]{1,0:T(8,128)S(1)} %get-tuple-element.24.sum_ref, ...), custom_call_target="tpu_custom_call" | custom-call | flops 4000000000 | bytes 12000000 | tf_op jit(solution)/shard_map/pallas_call | solution.py:498
  22.9 0.0 collective-permute-done.2.y1_ref
  22.9 1.2 %collective-permute-done.3.y2_ref = f32[208,128]{1,0:T(8,128)S(1)} collective-permute-done((f32[208,128]{1,0:T(8,128)S(1)}, f32[208,128]{1,0:T(8,128)S(1)}, u32[]{:S(2)}, u32[]{:S(2)}) %collective-permute-start.3) | collective-permute-done | bytes 106528 | tf_op jit(solution)/shard_map/ppermute | solution.py:519
  24.1 0.0 copy-done.6
  24.1 3.7 %shard_map.110.own_ref.vec_ref = f32[584,128]{1,0:T(8,128)S(1)} custom-call(s32[1]{0:T(128)} %bitcast.tile_ref, f32[512,128]{1,0:T(8,128)S(1)} %shard_map.104._.ids_ref, f32[192,128]{1,0:T(8,128)S(1)} %copy-done.5, s32[10,128]{1,0:T(8,128)S(1)} %copy-done.7, s32[1,128]{1,0:T(1,128)S(1)} %bitcast.15, f32[192,128]{1,0:T(8,128)S(1)} %copy-done.6, ...), custom_call_target="tpu_custom_call" | custom-call | flops 4000000000 | bytes 12000000 | tf_op jit(solution)/shard_map/pallas_call | solution.py:498
  27.8 1.9 %collective-permute-start.4 = (f32[584,128]{1,0:T(8,128)S(1)}, f32[584,128]{1,0:T(8,128)S(1)}, u32[]{:S(2)}, u32[]{:S(2)}) collective-permute-start(f32[584,128]{1,0:T(8,128)S(1)} %shard_map.110.own_ref.vec_ref), channel_id=1, source_target_pairs={{0,1},{1,0},{2,3},{3,2},{4,5},{5,4},{6,7},{7,6},{8,9},{9,8},{10,11... | collective-permute-start | bytes 897032 | tf_op jit(solution)/shard_map/ppermute | solution.py:632
  29.7 1.6 %collective-permute-done.4.other_ref = f32[584,128]{1,0:T(8,128)S(1)} collective-permute-done((f32[584,128]{1,0:T(8,128)S(1)}, f32[584,128]{1,0:T(8,128)S(1)}, u32[]{:S(2)}, u32[]{:S(2)}) %collective-permute-start.4) | collective-permute-done | bytes 299040 | tf_op jit(solution)/shard_map/ppermute | solution.py:632
  31.3 0.8 shard_map.111
  32.1 13.0 %all_to_all.20.in_ref = f32[4,320,128]{2,1,0:T(8,128)S(1)} all-to-all(f32[4,320,128]{2,1,0:T(8,128)S(1)} %bitcast.6), channel_id=1, replica_groups=mesh['z'=8,'y'=8,'x'=4,'c'=2] {'x'}, dimensions={0} | all-to-all | bytes 1310720 | tf_op jit(solution)/shard_map/all_to_all | solution.py:634
  45.1 15.1 %all_to_all.21.in_ref = f32[8,40,128]{2,1,0:T(8,128)S(1)} all-to-all(f32[8,40,128]{2,1,0:T(8,128)S(1)} %bitcast.10), channel_id=1, replica_groups=mesh['z'=8,'y'=8,'x'=4,'c'=2] {'y'}, dimensions={0} | all-to-all | bytes 327680 | tf_op jit(solution)/shard_map/all_to_all | solution.py:636
  60.2 18.2 %all_to_all.22.in_ref = f32[8,40,128]{2,1,0:T(8,128)S(1)} all-to-all(f32[8,40,128]{2,1,0:T(8,128)S(1)} %shard_map.113), channel_id=1, replica_groups=mesh['z'=8,'y'=8,'x'=4,'c'=2] {'z'}, dimensions={0} | all-to-all | bytes 327680 | tf_op jit(solution)/shard_map/all_to_all | solution.py:638
  78.4 0.2 shard_map.114
  78.6 14.8 %all_to_all.23 = f32[32,24,128]{2,1,0:T(8,128)S(1)} all-to-all(f32[32,24,128]{2,1,0:T(8,128)S(1)} %bitcast.9), channel_id=1, replica_groups=mesh['z'=8,'y'=8,'x'=4,'c'=2] {'y','x'}, dimensions={0} | all-to-all | bytes 786432 | tf_op jit(solution)/shard_map/all_to_all | solution.py:640
  93.4 6.7 %collective-permute-start.5 = (f32[768,128]{1,0:T(8,128)S(1)}, f32[768,128]{1,0:T(8,128)S(1)}, u32[]{:S(2)}, u32[]{:S(2)}) collective-permute-start(f32[768,128]{1,0:T(8,128)S(1)} %bitcast.7), channel_id=1, source_target_pairs={{0,1},{1,0},{2,3},{3,2},{4,5},{5,4},{6,7},{7,6},{8,9},{9,8},{10,11... | collective-permute-start | bytes 1179656 | tf_op jit(solution)/shard_map/ppermute | solution.py:642
  100.1 1.3 %collective-permute-done.5.other_ref = f32[768,128]{1,0:T(8,128)S(1)} collective-permute-done((f32[768,128]{1,0:T(8,128)S(1)}, f32[768,128]{1,0:T(8,128)S(1)}, u32[]{:S(2)}, u32[]{:S(2)}) %collective-permute-start.5) | collective-permute-done | bytes 393248 | tf_op jit(solution)/shard_map/ppermute | solution.py:642
  101.4 1.0 %shard_map.115 = (f32[4,192,192]{2,1,0:T(8,128)}, f32[192,128]{1,0:T(8,128)}) custom-call(s32[1]{0:T(128)} %bitcast.tile_ref, f32[768,128]{1,0:T(8,128)S(1)} %bitcast.8, f32[768,128]{1,0:T(8,128)S(1)} %collective-permute-done.5.other_ref, f32[584,128]{1,0:T(8,128)S(1)} %shard_map.110.own_ref.vec_ref, f32[8,128]{1,0:T(8,128)S(1)} %get-tuple-element.31.coef_ref), custom_call_target="tpu_custom_call" | custom-call | flops 1000000000 | bytes 3000000 | tf_op jit(solution)/shard_map/pallas_call | solution.py:498
  (2 shorter events, 0.1 us)
Async XLA Ops:
  0.6 0.9 copy-start.4
  0.7 0.9 copy-start.5
  0.7 0.9 copy-start.7
  0.7 0.9 copy-start.8
  1.6 5.0 %copy-start = (f32[10,96,96]{2,1,0:T(8,128)S(1)}, f32[10,96,96]{2,1,0:T(8,128)}, u32[]{:S(2)}) copy-start(f32[10,96,96]{2,1,0:T(8,128)} %lr_ref.1) | copy-start | bytes 1105924
  1.6 5.0 %copy-start.1 = (f32[10,96,96]{2,1,0:T(8,128)S(1)}, f32[10,96,96]{2,1,0:T(8,128)}, u32[]{:S(2)}) copy-start(f32[10,96,96]{2,1,0:T(8,128)} %li_ref.1) | copy-start | bytes 1105924
  1.6 5.0 %copy-start.2 = (f32[4,96,96]{2,1,0:T(8,128)S(1)}, f32[4,96,96]{2,1,0:T(8,128)}, u32[]{:S(2)}) copy-start(f32[4,96,96]{2,1,0:T(8,128)} %tr_ref.1) | copy-start | bytes 442372
  1.6 5.0 %copy-start.3 = (f32[4,96,96]{2,1,0:T(8,128)S(1)}, f32[4,96,96]{2,1,0:T(8,128)}, u32[]{:S(2)}) copy-start(f32[4,96,96]{2,1,0:T(8,128)} %ti_ref.1) | copy-start | bytes 442372
  1.7 6.8 %collective-permute-start = (f32[304,128]{1,0:T(8,128)S(1)}, f32[304,128]{1,0:T(8,128)S(1)}, u32[]{:S(2)}, u32[]{:S(2)}) collective-permute-start(f32[304,128]{1,0:T(8,128)S(1)} %get-tuple-element.18), channel_id=1, source_target_pairs={{0,8},{8,0},{16,24},{24,16},{32,40},{40,32},{48,56},{56,48},{64,72... | collective-permute-start | bytes 466952 | tf_op jit(solution)/shard_map/ppermute | solution.py:519
  5.9 2.6 %collective-permute-start.1 = (f32[304,128]{1,0:T(8,128)S(1)}, f32[304,128]{1,0:T(8,128)S(1)}, u32[]{:S(2)}, u32[]{:S(2)}) collective-permute-start(f32[304,128]{1,0:T(8,128)S(1)} %get-tuple-element.19), channel_id=1, source_target_pairs={{8,16},{16,8},{24,32},{32,24},{40,48},{48,40},{56,64},{64,56},{72,... | collective-permute-start | bytes 466952 | tf_op jit(solution)/shard_map/ppermute | solution.py:519
  8.8 14.1 %collective-permute-start.2 = (f32[208,128]{1,0:T(8,128)S(1)}, f32[208,128]{1,0:T(8,128)S(1)}, u32[]{:S(2)}, u32[]{:S(2)}) collective-permute-start(f32[208,128]{1,0:T(8,128)S(1)} %get-tuple-element.20), channel_id=1, source_target_pairs={{0,1},{1,0},{2,3},{3,2},{4,5},{5,4},{6,7},{7,6},{8,9},{9,8},{10,11... | collective-permute-start | bytes 319496 | tf_op jit(solution)/shard_map/ppermute | solution.py:519
  18.1 6.0 %collective-permute-start.3 = (f32[208,128]{1,0:T(8,128)S(1)}, f32[208,128]{1,0:T(8,128)S(1)}, u32[]{:S(2)}, u32[]{:S(2)}) collective-permute-start(f32[208,128]{1,0:T(8,128)S(1)} %get-tuple-element.21), channel_id=1, source_target_pairs={{1,2},{2,1},{3,4},{4,3},{5,6},{6,5},{9,10},{10,9},{11,12},{12,11},... | collective-permute-start | bytes 319496 | tf_op jit(solution)/shard_map/ppermute | solution.py:519
  20.0 4.1 %copy-start.6 = (f32[192,128]{1,0:T(8,128)S(1)}, f32[192,128]{1,0:T(8,128)}, u32[]{:S(2)}) copy-start(f32[192,128]{1,0:T(8,128)} %inc_ref.1) | copy-start | bytes 294916
  27.8 3.5 %collective-permute-start.4 = (f32[584,128]{1,0:T(8,128)S(1)}, f32[584,128]{1,0:T(8,128)S(1)}, u32[]{:S(2)}, u32[]{:S(2)}) collective-permute-start(f32[584,128]{1,0:T(8,128)S(1)} %shard_map.110.own_ref.vec_ref), channel_id=1, source_target_pairs={{0,1},{1,0},{2,3},{3,2},{4,5},{5,4},{6,7},{7,6},{8,9},{9,8},{10,11... | collective-permute-start | bytes 897032 | tf_op jit(solution)/shard_map/ppermute | solution.py:632
  93.4 8.0 %collective-permute-start.5 = (f32[768,128]{1,0:T(8,128)S(1)}, f32[768,128]{1,0:T(8,128)S(1)}, u32[]{:S(2)}, u32[]{:S(2)}) collective-permute-start(f32[768,128]{1,0:T(8,128)S(1)} %bitcast.7), channel_id=1, source_target_pairs={{0,1},{1,0},{2,3},{3,2},{4,5},{5,4},{6,7},{7,6},{8,9},{9,8},{10,11... | collective-permute-start | bytes 1179656 | tf_op jit(solution)/shard_map/ppermute | solution.py:642

commit v12 on v11

--- a/solution.py
+++ b/solution.py
@@ -418,11 +418,10 @@
             for h in range(2):
                 block = out[which * W + h * HALF : which * W + (h + 1) * HALF, :]
                 edge = block[0:48, PT:] + pltpu.roll(block[48:96, PT:], 64, 1)
-                at = (2 * k + h) * 2 * CHUNK + which * 18
+                at = (2 * k + h) * 8 * CHUNK + which * 18
                 for i in range(18):
                     rows = block[8 * i : 8 * i + 8, 0:PT] if i < 12 else edge[8 * i - 96 : 8 * i - 88]
-                    chunk_ref[pl.ds(at + i, 4, 8 * CHUNK), :] = rows[0:4]
-                    chunk_ref[pl.ds(at + CHUNK + i, 4, 8 * CHUNK), :] = rows[4:8]
+                    chunk_ref[pl.ds(at + i, 8, CHUNK), :] = rows
     gram = own_ref[3 * W : 3 * W + 1, :] + other_ref[3 * W : 3 * W + 1, :]
     for i in range(36, CHUNK):
         row = gram if i == 36 else jnp.zeros((1, PT), F32)
@@ -484,9 +483,9 @@
     for ref, first in ((own_ref, 2 * core), (other_ref, 2 - 2 * core)):
         for k in range(2):
             for h in range(2):
-                base, at = (2 * k + h) * 8 * BACK, h * HALF
+                base, at = (2 * k + h) * BACK, h * HALF
                 block = jnp.concatenate(
-                    [ref[pl.ds(base + i, 8, BACK), :] for i in range(18)], axis=0
+                    [ref[pl.ds(base + i, 8, 4 * BACK), :] for i in range(18)], axis=0
                 )
                 edge = block[96:144, :]
                 out_ref[first + k, at : at + HALF, 0:PT] = block[0:HALF, :]

time: 103 us -> 103 us (level)
  no operation moved by 1% of the time
where the time goes in v12:
time: 103 us; the launch traced here: 102 us
  blocking collectives  61.1 us (59%)
  starting transfers between devices  24.6 us (24%)
  Pallas kernels  10.8 us (10%)
  waiting for transfers between devices  4.28 us (4%)
    all_to_all x1, blocking collectives, body(): got = lax.all_to_all(pieces, 'z', 0, 0)  18.2 us
    ppermute x4, starting transfers between devices, swapped(): return (lax.ppermute(one, axis, near), lax.ppermute(two, axis, far))  16 us
    all_to_all x1, blocking collectives, body(): got = lax.all_to_all(part.reshape(8, CHUNK, PT), 'y', 0, 0)  15.1 us
    all_to_all x1, blocking collectives, body(): got = lax.all_to_all(mixed.reshape(32, BACK, PT), ('y', 'x'), 0, 0)  14.8 us
    all_to_all x1, blocking collectives, body(): got = lax.all_to_all(chunks.reshape(4, 8 * CHUNK, PT), 'x', 0, 0)  13 us
    pallas_call x12, Pallas kernels, call(): pl.pallas_call(kernel, out_shape=[s if isinstance(s, jax.ShapeDtypeStruct...  10.8 us
    ppermute x1, starting transfers between devices, body(): other = lax.ppermute(half, 'c', pair)  6.69 us
  transfers between devices with their start and end apart: 6, of which 4 were waited for; matrix products, arithmetic and copies ran while one was open for 0% of the time, Pallas kernels for 4%

profile of v12, /device:TPU:1, one launch (start us, length us, event | category | flops | bytes accessed | tf_op | source)
XLA Modules:
  0.0 102.4 jit_solution(15005596075074123197)
XLA Ops:
  0.6 0.0 copy-start.4
  0.7 0.0 copy-start.5
  0.7 0.0 copy-start.7
  0.7 0.0 copy-start.8
  0.7 0.1 shard_map.104._.ids_ref
  0.8 0.7 copy-done.4
  1.5 0.0 copy-done.5
  1.6 0.0 copy-done.7
  1.6 0.0 copy-done.8
  1.6 0.0 copy-start
  1.6 0.0 copy-start.1
  1.6 0.0 copy-start.2
  1.6 0.0 copy-start.3
  1.6 0.1 shard_map.105
  1.7 4.2 %collective-permute-start = (f32[304,128]{1,0:T(8,128)S(1)}, f32[304,128]{1,0:T(8,128)S(1)}, u32[]{:S(2)}, u32[]{:S(2)}) collective-permute-start(f32[304,128]{1,0:T(8,128)S(1)} %get-tuple-element.18), channel_id=1, source_target_pairs={{0,8},{8,0},{16,24},{24,16},{32,40},{40,32},{48,56},{56,48},{64,72... | collective-permute-start | bytes 466952 | tf_op jit(solution)/shard_map/ppermute | solution.py:518
  5.9 0.7 collective-permute-start.1
  6.6 0.0 copy-done
  6.6 0.0 copy-done.1
  6.6 0.0 copy-done.2
  6.6 0.0 copy-done.3
  6.6 0.7 shard_map.107
  7.4 0.9 shard_map.108
  8.3 0.2 collective-permute-done.x1_ref
  8.5 0.0 collective-permute-done.1.x2_ref
  8.5 0.3 shard_map.106
  8.8 9.3 %collective-permute-start.2 = (f32[208,128]{1,0:T(8,128)S(1)}, f32[208,128]{1,0:T(8,128)S(1)}, u32[]{:S(2)}, u32[]{:S(2)}) collective-permute-start(f32[208,128]{1,0:T(8,128)S(1)} %get-tuple-element.20), channel_id=1, source_target_pairs={{0,1},{1,0},{2,3},{3,2},{4,5},{5,4},{6,7},{7,6},{8,9},{9,8},{10,11... | collective-permute-start | bytes 319496 | tf_op jit(solution)/shard_map/ppermute | solution.py:518
  18.1 1.9 %collective-permute-start.3 = (f32[208,128]{1,0:T(8,128)S(1)}, f32[208,128]{1,0:T(8,128)S(1)}, u32[]{:S(2)}, u32[]{:S(2)}) collective-permute-start(f32[208,128]{1,0:T(8,128)S(1)} %get-tuple-element.21), channel_id=1, source_target_pairs={{1,2},{2,1},{3,4},{4,3},{5,6},{6,5},{9,10},{10,9},{11,12},{12,11},... | collective-permute-start | bytes 319496 | tf_op jit(solution)/shard_map/ppermute | solution.py:518
  20.0 0.0 copy-start.6
  20.0 2.9 %shard_map.109 = (f32[192,256]{1,0:T(8,128)S(1)}, f32[960,256]{1,0:T(8,128)S(1)}, bf16[2048,256]{1,0:T(8,128)(2,1)S(1)}) custom-call(s32[1]{0:T(128)} %bitcast.tile_ref, f32[512,128]{1,0:T(8,128)S(1)} %shard_map.104._.ids_ref, bf16[384,128]{1,0:T(8,128)(2,1)S(1)} %get-tuple-element.23.own_ref, f32[1920,256]{1,0:T(8,128)S(1)} %get-tuple-element.24.sum_ref, ...), custom_call_target="tpu_custom_call" | custom-call | flops 4000000000 | bytes 12000000 | tf_op jit(solution)/shard_map/pallas_call | solution.py:497
  22.9 0.0 collective-permute-done.2.y1_ref
  22.9 1.2 %collective-permute-done.3.y2_ref = f32[208,128]{1,0:T(8,128)S(1)} collective-permute-done((f32[208,128]{1,0:T(8,128)S(1)}, f32[208,128]{1,0:T(8,128)S(1)}, u32[]{:S(2)}, u32[]{:S(2)}) %collective-permute-start.3) | collective-permute-done | bytes 106528 | tf_op jit(solution)/shard_map/ppermute | solution.py:518
  24.1 0.0 copy-done.6
  24.1 3.7 %shard_map.110.own_ref.vec_ref = f32[584,128]{1,0:T(8,128)S(1)} custom-call(s32[1]{0:T(128)} %bitcast.tile_ref, f32[512,128]{1,0:T(8,128)S(1)} %shard_map.104._.ids_ref, f32[192,128]{1,0:T(8,128)S(1)} %copy-done.5, s32[10,128]{1,0:T(8,128)S(1)} %copy-done.7, s32[1,128]{1,0:T(1,128)S(1)} %bitcast.15, f32[192,128]{1,0:T(8,128)S(1)} %copy-done.6, ...), custom_call_target="tpu_custom_call" | custom-call | flops 4000000000 | bytes 12000000 | tf_op jit(solution)/shard_map/pallas_call | solution.py:497
  27.8 1.9 %collective-permute-start.4 = (f32[584,128]{1,0:T(8,128)S(1)}, f32[584,128]{1,0:T(8,128)S(1)}, u32[]{:S(2)}, u32[]{:S(2)}) collective-permute-start(f32[584,128]{1,0:T(8,128)S(1)} %shard_map.110.own_ref.vec_ref), channel_id=1, source_target_pairs={{0,1},{1,0},{2,3},{3,2},{4,5},{5,4},{6,7},{7,6},{8,9},{9,8},{10,11... | collective-permute-start | bytes 897032 | tf_op jit(solution)/shard_map/ppermute | solution.py:631
  29.7 1.6 %collective-permute-done.4.other_ref = f32[584,128]{1,0:T(8,128)S(1)} collective-permute-done((f32[584,128]{1,0:T(8,128)S(1)}, f32[584,128]{1,0:T(8,128)S(1)}, u32[]{:S(2)}, u32[]{:S(2)}) %collective-permute-start.4) | collective-permute-done | bytes 299040 | tf_op jit(solution)/shard_map/ppermute | solution.py:631
  31.3 0.6 shard_map.111
  31.9 13.0 %all_to_all.20.in_ref = f32[4,320,128]{2,1,0:T(8,128)S(1)} all-to-all(f32[4,320,128]{2,1,0:T(8,128)S(1)} %bitcast.6), channel_id=1, replica_groups=mesh['z'=8,'y'=8,'x'=4,'c'=2] {'x'}, dimensions={0} | all-to-all | bytes 1310720 | tf_op jit(solution)/shard_map/all_to_all | solution.py:633
  44.9 15.1 %all_to_all.21.in_ref = f32[8,40,128]{2,1,0:T(8,128)S(1)} all-to-all(f32[8,40,128]{2,1,0:T(8,128)S(1)} %bitcast.10), channel_id=1, replica_groups=mesh['z'=8,'y'=8,'x'=4,'c'=2] {'y'}, dimensions={0} | all-to-all | bytes 327680 | tf_op jit(solution)/shard_map/all_to_all | solution.py:635
  60.0 18.2 %all_to_all.22.in_ref = f32[8,40,128]{2,1,0:T(8,128)S(1)} all-to-all(f32[8,40,128]{2,1,0:T(8,128)S(1)} %shard_map.113), channel_id=1, replica_groups=mesh['z'=8,'y'=8,'x'=4,'c'=2] {'z'}, dimensions={0} | all-to-all | bytes 327680 | tf_op jit(solution)/shard_map/all_to_all | solution.py:637
  78.2 0.2 shard_map.114
  78.4 14.8 %all_to_all.23 = f32[32,24,128]{2,1,0:T(8,128)S(1)} all-to-all(f32[32,24,128]{2,1,0:T(8,128)S(1)} %bitcast.9), channel_id=1, replica_groups=mesh['z'=8,'y'=8,'x'=4,'c'=2] {'y','x'}, dimensions={0} | all-to-all | bytes 786432 | tf_op jit(solution)/shard_map/all_to_all | solution.py:639
  93.2 6.7 %collective-permute-start.5 = (f32[768,128]{1,0:T(8,128)S(1)}, f32[768,128]{1,0:T(8,128)S(1)}, u32[]{:S(2)}, u32[]{:S(2)}) collective-permute-start(f32[768,128]{1,0:T(8,128)S(1)} %bitcast.7), channel_id=1, source_target_pairs={{0,1},{1,0},{2,3},{3,2},{4,5},{5,4},{6,7},{7,6},{8,9},{9,8},{10,11... | collective-permute-start | bytes 1179656 | tf_op jit(solution)/shard_map/ppermute | solution.py:641
  99.9 1.3 %collective-permute-done.5.other_ref = f32[768,128]{1,0:T(8,128)S(1)} collective-permute-done((f32[768,128]{1,0:T(8,128)S(1)}, f32[768,128]{1,0:T(8,128)S(1)}, u32[]{:S(2)}, u32[]{:S(2)}) %collective-permute-start.5) | collective-permute-done | bytes 393248 | tf_op jit(solution)/shard_map/ppermute | solution.py:641
  101.2 1.3 %shard_map.115 = (f32[4,192,192]{2,1,0:T(8,128)}, f32[192,128]{1,0:T(8,128)}) custom-call(s32[1]{0:T(128)} %bitcast.tile_ref, f32[768,128]{1,0:T(8,128)S(1)} %bitcast.8, f32[768,128]{1,0:T(8,128)S(1)} %collective-permute-done.5.other_ref, f32[584,128]{1,0:T(8,128)S(1)} %shard_map.110.own_ref.vec_ref, f32[8,128]{1,0:T(8,128)S(1)} %get-tuple-element.31.coef_ref), custom_call_target="tpu_custom_call" | custom-call | flops 1000000000 | bytes 3000000 | tf_op jit(solution)/shard_map/pallas_call | solution.py:497
  (2 shorter events, 0.1 us)
Async XLA Ops:
  0.6 0.9 copy-start.4
  0.7 0.9 copy-start.5
  0.7 0.9 copy-start.7
  0.7 0.9 copy-start.8
  1.6 5.0 %copy-start = (f32[10,96,96]{2,1,0:T(8,128)S(1)}, f32[10,96,96]{2,1,0:T(8,128)}, u32[]{:S(2)}) copy-start(f32[10,96,96]{2,1,0:T(8,128)} %lr_ref.1) | copy-start | bytes 1105924
  1.6 5.0 %copy-start.1 = (f32[10,96,96]{2,1,0:T(8,128)S(1)}, f32[10,96,96]{2,1,0:T(8,128)}, u32[]{:S(2)}) copy-start(f32[10,96,96]{2,1,0:T(8,128)} %li_ref.1) | copy-start | bytes 1105924
  1.6 5.0 %copy-start.2 = (f32[4,96,96]{2,1,0:T(8,128)S(1)}, f32[4,96,96]{2,1,0:T(8,128)}, u32[]{:S(2)}) copy-start(f32[4,96,96]{2,1,0:T(8,128)} %tr_ref.1) | copy-start | bytes 442372
  1.6 5.0 %copy-start.3 = (f32[4,96,96]{2,1,0:T(8,128)S(1)}, f32[4,96,96]{2,1,0:T(8,128)}, u32[]{:S(2)}) copy-start(f32[4,96,96]{2,1,0:T(8,128)} %ti_ref.1) | copy-start | bytes 442372
  1.7 6.8 %collective-permute-start = (f32[304,128]{1,0:T(8,128)S(1)}, f32[304,128]{1,0:T(8,128)S(1)}, u32[]{:S(2)}, u32[]{:S(2)}) collective-permute-start(f32[304,128]{1,0:T(8,128)S(1)} %get-tuple-element.18), channel_id=1, source_target_pairs={{0,8},{8,0},{16,24},{24,16},{32,40},{40,32},{48,56},{56,48},{64,72... | collective-permute-start | bytes 466952 | tf_op jit(solution)/shard_map/ppermute | solution.py:518
  5.9 2.6 %collective-permute-start.1 = (f32[304,128]{1,0:T(8,128)S(1)}, f32[304,128]{1,0:T(8,128)S(1)}, u32[]{:S(2)}, u32[]{:S(2)}) collective-permute-start(f32[304,128]{1,0:T(8,128)S(1)} %get-tuple-element.19), channel_id=1, source_target_pairs={{8,16},{16,8},{24,32},{32,24},{40,48},{48,40},{56,64},{64,56},{72,... | collective-permute-start | bytes 466952 | tf_op jit(solution)/shard_map/ppermute | solution.py:518
  8.8 14.1 %collective-permute-start.2 = (f32[208,128]{1,0:T(8,128)S(1)}, f32[208,128]{1,0:T(8,128)S(1)}, u32[]{:S(2)}, u32[]{:S(2)}) collective-permute-start(f32[208,128]{1,0:T(8,128)S(1)} %get-tuple-element.20), channel_id=1, source_target_pairs={{0,1},{1,0},{2,3},{3,2},{4,5},{5,4},{6,7},{7,6},{8,9},{9,8},{10,11... | collective-permute-start | bytes 319496 | tf_op jit(solution)/shard_map/ppermute | solution.py:518
  18.1 6.0 %collective-permute-start.3 = (f32[208,128]{1,0:T(8,128)S(1)}, f32[208,128]{1,0:T(8,128)S(1)}, u32[]{:S(2)}, u32[]{:S(2)}) collective-permute-start(f32[208,128]{1,0:T(8,128)S(1)} %get-tuple-element.21), channel_id=1, source_target_pairs={{1,2},{2,1},{3,4},{4,3},{5,6},{6,5},{9,10},{10,9},{11,12},{12,11},... | collective-permute-start | bytes 319496 | tf_op jit(solution)/shard_map/ppermute | solution.py:518
  20.0 4.1 %copy-start.6 = (f32[192,128]{1,0:T(8,128)S(1)}, f32[192,128]{1,0:T(8,128)}, u32[]{:S(2)}) copy-start(f32[192,128]{1,0:T(8,128)} %inc_ref.1) | copy-start | bytes 294916
  27.8 3.5 %collective-permute-start.4 = (f32[584,128]{1,0:T(8,128)S(1)}, f32[584,128]{1,0:T(8,128)S(1)}, u32[]{:S(2)}, u32[]{:S(2)}) collective-permute-start(f32[584,128]{1,0:T(8,128)S(1)} %shard_map.110.own_ref.vec_ref), channel_id=1, source_target_pairs={{0,1},{1,0},{2,3},{3,2},{4,5},{5,4},{6,7},{7,6},{8,9},{9,8},{10,11... | collective-permute-start | bytes 897032 | tf_op jit(solution)/shard_map/ppermute | solution.py:631
  93.2 8.0 %collective-permute-start.5 = (f32[768,128]{1,0:T(8,128)S(1)}, f32[768,128]{1,0:T(8,128)S(1)}, u32[]{:S(2)}, u32[]{:S(2)}) collective-permute-start(f32[768,128]{1,0:T(8,128)S(1)} %bitcast.7), channel_id=1, source_target_pairs={{0,1},{1,0},{2,3},{3,2},{4,5},{5,4},{6,7},{7,6},{8,9},{9,8},{10,11... | collective-permute-start | bytes 1179656 | tf_op jit(solution)/shard_map/ppermute | solution.py:641

commit v13 on v12

--- a/solution.py
+++ b/solution.py
@@ -477,20 +477,29 @@
     coef_ref[4:8, :] = jnp.broadcast_to(c1, (4, PT))
 
 
-def expand_kernel(tile_ref, own_ref, other_ref, vec_ref, coef_ref, out_ref, adj_ref):
+def spread_types(ref, out_ref, first):
+    for k in range(2):
+        for h in range(2):
+            base, at = (2 * k + h) * BACK, h * HALF
+            block = jnp.concatenate(
+                [ref[pl.ds(base + i, 8, 4 * BACK), :] for i in range(18)], axis=0
+            )
+            edge = block[96:144, :]
+            out_ref[first + k, at : at + HALF, 0:PT] = block[0:HALF, :]
+            out_ref[first + k, at : at + 48, PT:W] = edge[:, 0:64]
+            out_ref[first + k, at + 48 : at + HALF, PT:W] = pltpu.roll(edge, 64, 1)[:, 0:64]
+
+
+def own_types_kernel(own_ref, vec_ref, coef_ref, half_ref, adj_ref):
     adj_ref[...] = coef_ref[0:1, :] * vec_ref[0:W, :] + coef_ref[4:5, :] * vec_ref[W : 2 * W, :]
+    spread_types(own_ref, half_ref, 0)
+
+
+def expand_kernel(tile_ref, half_ref, other_ref, out_ref):
     core = lax.rem(tile_ref[0], 2)
-    for ref, first in ((own_ref, 2 * core), (other_ref, 2 - 2 * core)):
-        for k in range(2):
-            for h in range(2):
-                base, at = (2 * k + h) * BACK, h * HALF
-                block = jnp.concatenate(
-                    [ref[pl.ds(base + i, 8, 4 * BACK), :] for i in range(18)], axis=0
-                )
-                edge = block[96:144, :]
-                out_ref[first + k, at : at + HALF, 0:PT] = block[0:HALF, :]
-                out_ref[first + k, at : at + 48, PT:W] = edge[:, 0:64]
-                out_ref[first + k, at + 48 : at + HALF, PT:W] = pltpu.roll(edge, 64, 1)[:, 0:64]
+    for k in range(2):
+        out_ref[2 * core + k] = half_ref[k]
+    spread_types(other_ref, out_ref, 2 - 2 * core)
 
 
 def call(kernel, shapes, *args, smem=0, whole=0, mib=6, dtype=F32, us=1, **kw):
@@ -639,16 +648,8 @@
     got = lax.all_to_all(mixed.reshape(32, BACK, PT), ("y", "x"), 0, 0)
     half = got.reshape(32 * BACK, PT)
     other = lax.ppermute(half, "c", pair)
-    sensitivity, adjoint = call(
-        expand_kernel,
-        [(KINDS, W, W), (W, PT)],
-        tile,
-        half,
-        other,
-        vectors,
-        coefs,
-        smem=1,
-    )
+    own_half, adjoint = call(own_types_kernel, [(2, W, W), (W, PT)], half, vectors, coefs)
+    (sensitivity,) = call(expand_kernel, [(KINDS, W, W)], tile, own_half, other, smem=1)
     return (adjoint, sensitivity)
 
 

time: 103 us -> 103 us (level)
    pallas_call x12 -> x13, Pallas kernels: 10.8 us -> 11.4 us  [call(): pl.pallas_call(kernel, out_shape=[s if isinstance(s, jax.ShapeDtypeStruct...]
  transfers between devices with their start and end apart: 6 -> 6, of which waited for: 4 -> 4; matrix products, arithmetic and copies ran while one was open for 0% -> 0% of each run, Pallas kernels for 4% -> 5%
where the time goes in v13:
time: 103 us; the launch traced here: 102 us
  blocking collectives  61.1 us (59%)
  starting transfers between devices  24.6 us (24%)
  Pallas kernels  11.4 us (11%)
  waiting for transfers between devices  3.46 us (3%)
    all_to_all x1, blocking collectives, body(): got = lax.all_to_all(pieces, 'z', 0, 0)  18.2 us
    ppermute x4, starting transfers between devices, swapped(): return (lax.ppermute(one, axis, near), lax.ppermute(two, axis, far))  16 us
    all_to_all x1, blocking collectives, body(): got = lax.all_to_all(part.reshape(8, CHUNK, PT), 'y', 0, 0)  15.1 us
    all_to_all x1, blocking collectives, body(): got = lax.all_to_all(mixed.reshape(32, BACK, PT), ('y', 'x'), 0, 0)  14.8 us
    all_to_all x1, blocking collectives, body(): got = lax.all_to_all(chunks.reshape(4, 8 * CHUNK, PT), 'x', 0, 0)  13 us
    pallas_call x13, Pallas kernels, call(): pl.pallas_call(kernel, out_shape=[s if isinstance(s, jax.ShapeDtypeStruct...  11.4 us
    ppermute x1, starting transfers between devices, body(): other = lax.ppermute(half, 'c', pair)  6.69 us
  transfers between devices with their start and end apart: 6, of which 4 were waited for; matrix products, arithmetic and copies ran while one was open for 0% of the time, Pallas kernels for 5%

profile of v13, /device:TPU:1, one launch (start us, length us, event | category | flops | bytes accessed | tf_op | source)
XLA Modules:
  0.0 102.3 jit_solution(11037912966515190394)
XLA Ops:
  0.6 0.0 copy-start.4
  0.7 0.0 copy-start.5
  0.7 0.0 copy-start.7
  0.7 0.0 copy-start.8
  0.7 0.1 shard_map.104._.ids_ref
  0.8 0.7 copy-done.4
  1.5 0.0 copy-done.5
  1.6 0.0 copy-done.7
  1.6 0.0 copy-done.8
  1.6 0.0 copy-start
  1.6 0.0 copy-start.1
  1.6 0.0 copy-start.2
  1.6 0.0 copy-start.3
  1.6 0.1 shard_map.105
  1.7 4.2 %collective-permute-start = (f32[304,128]{1,0:T(8,128)S(1)}, f32[304,128]{1,0:T(8,128)S(1)}, u32[]{:S(2)}, u32[]{:S(2)}) collective-permute-start(f32[304,128]{1,0:T(8,128)S(1)} %get-tuple-element.18), channel_id=1, source_target_pairs={{0,8},{8,0},{16,24},{24,16},{32,40},{40,32},{48,56},{56,48},{64,72... | collective-permute-start | bytes 466952 | tf_op jit(solution)/shard_map/ppermute | solution.py:527
  5.9 0.7 collective-permute-start.1
  6.6 0.0 copy-done
  6.6 0.0 copy-done.1
  6.6 0.0 copy-done.2
  6.6 0.0 copy-done.3
  6.6 0.7 shard_map.107
  7.4 0.9 shard_map.108
  8.3 0.2 collective-permute-done.x1_ref
  8.5 0.0 collective-permute-done.1.x2_ref
  8.5 0.3 shard_map.106
  8.8 9.3 %collective-permute-start.2 = (f32[208,128]{1,0:T(8,128)S(1)}, f32[208,128]{1,0:T(8,128)S(1)}, u32[]{:S(2)}, u32[]{:S(2)}) collective-permute-start(f32[208,128]{1,0:T(8,128)S(1)} %get-tuple-element.20), channel_id=1, source_target_pairs={{0,1},{1,0},{2,3},{3,2},{4,5},{5,4},{6,7},{7,6},{8,9},{9,8},{10,11... | collective-permute-start | bytes 319496 | tf_op jit(solution)/shard_map/ppermute | solution.py:527
  18.1 1.9 %collective-permute-start.3 = (f32[208,128]{1,0:T(8,128)S(1)}, f32[208,128]{1,0:T(8,128)S(1)}, u32[]{:S(2)}, u32[]{:S(2)}) collective-permute-start(f32[208,128]{1,0:T(8,128)S(1)} %get-tuple-element.21), channel_id=1, source_target_pairs={{1,2},{2,1},{3,4},{4,3},{5,6},{6,5},{9,10},{10,9},{11,12},{12,11},... | collective-permute-start | bytes 319496 | tf_op jit(solution)/shard_map/ppermute | solution.py:527
  20.0 0.0 copy-start.6
  20.0 2.9 %shard_map.109 = (f32[192,256]{1,0:T(8,128)S(1)}, f32[960,256]{1,0:T(8,128)S(1)}, bf16[2048,256]{1,0:T(8,128)(2,1)S(1)}) custom-call(s32[1]{0:T(128)} %bitcast.tile_ref, f32[512,128]{1,0:T(8,128)S(1)} %shard_map.104._.ids_ref, bf16[384,128]{1,0:T(8,128)(2,1)S(1)} %get-tuple-element.23.own_ref, f32[1920,256]{1,0:T(8,128)S(1)} %get-tuple-element.24.sum_ref, ...), custom_call_target="tpu_custom_call" | custom-call | flops 4000000000 | bytes 12000000 | tf_op jit(solution)/shard_map/pallas_call | solution.py:506
  22.9 0.0 collective-permute-done.2.y1_ref
  22.9 1.2 %collective-permute-done.3.y2_ref = f32[208,128]{1,0:T(8,128)S(1)} collective-permute-done((f32[208,128]{1,0:T(8,128)S(1)}, f32[208,128]{1,0:T(8,128)S(1)}, u32[]{:S(2)}, u32[]{:S(2)}) %collective-permute-start.3) | collective-permute-done | bytes 106528 | tf_op jit(solution)/shard_map/ppermute | solution.py:527
  24.1 0.0 copy-done.6
  24.1 3.7 %shard_map.110.own_ref.vec_ref = f32[584,128]{1,0:T(8,128)S(1)} custom-call(s32[1]{0:T(128)} %bitcast.tile_ref, f32[512,128]{1,0:T(8,128)S(1)} %shard_map.104._.ids_ref, f32[192,128]{1,0:T(8,128)S(1)} %copy-done.5, s32[10,128]{1,0:T(8,128)S(1)} %copy-done.7, s32[1,128]{1,0:T(1,128)S(1)} %bitcast.15, f32[192,128]{1,0:T(8,128)S(1)} %copy-done.6, ...), custom_call_target="tpu_custom_call" | custom-call | flops 4000000000 | bytes 12000000 | tf_op jit(solution)/shard_map/pallas_call | solution.py:506
  27.8 1.9 %collective-permute-start.4 = (f32[584,128]{1,0:T(8,128)S(1)}, f32[584,128]{1,0:T(8,128)S(1)}, u32[]{:S(2)}, u32[]{:S(2)}) collective-permute-start(f32[584,128]{1,0:T(8,128)S(1)} %shard_map.110.own_ref.vec_ref), channel_id=1, source_target_pairs={{0,1},{1,0},{2,3},{3,2},{4,5},{5,4},{6,7},{7,6},{8,9},{9,8},{10,11... | collective-permute-start | bytes 897032 | tf_op jit(solution)/shard_map/ppermute | solution.py:640
  29.7 1.6 %collective-permute-done.4.other_ref = f32[584,128]{1,0:T(8,128)S(1)} collective-permute-done((f32[584,128]{1,0:T(8,128)S(1)}, f32[584,128]{1,0:T(8,128)S(1)}, u32[]{:S(2)}, u32[]{:S(2)}) %collective-permute-start.4) | collective-permute-done | bytes 299040 | tf_op jit(solution)/shard_map/ppermute | solution.py:640
  31.3 0.6 shard_map.111
  31.9 13.0 %all_to_all.20.in_ref = f32[4,320,128]{2,1,0:T(8,128)S(1)} all-to-all(f32[4,320,128]{2,1,0:T(8,128)S(1)} %bitcast.6), channel_id=1, replica_groups=mesh['z'=8,'y'=8,'x'=4,'c'=2] {'x'}, dimensions={0} | all-to-all | bytes 1310720 | tf_op jit(solution)/shard_map/all_to_all | solution.py:642
  44.9 15.1 %all_to_all.21.in_ref = f32[8,40,128]{2,1,0:T(8,128)S(1)} all-to-all(f32[8,40,128]{2,1,0:T(8,128)S(1)} %bitcast.10), channel_id=1, replica_groups=mesh['z'=8,'y'=8,'x'=4,'c'=2] {'y'}, dimensions={0} | all-to-all | bytes 327680 | tf_op jit(solution)/shard_map/all_to_all | solution.py:644
  60.0 18.2 %all_to_all.22.in_ref = f32[8,40,128]{2,1,0:T(8,128)S(1)} all-to-all(f32[8,40,128]{2,1,0:T(8,128)S(1)} %shard_map.113), channel_id=1, replica_groups=mesh['z'=8,'y'=8,'x'=4,'c'=2] {'z'}, dimensions={0} | all-to-all | bytes 327680 | tf_op jit(solution)/shard_map/all_to_all | solution.py:646
  78.2 0.2 shard_map.114
  78.4 14.8 %all_to_all.23 = f32[32,24,128]{2,1,0:T(8,128)S(1)} all-to-all(f32[32,24,128]{2,1,0:T(8,128)S(1)} %bitcast.9), channel_id=1, replica_groups=mesh['z'=8,'y'=8,'x'=4,'c'=2] {'y','x'}, dimensions={0} | all-to-all | bytes 786432 | tf_op jit(solution)/shard_map/all_to_all | solution.py:648
  93.2 6.7 %collective-permute-start.5 = (f32[768,128]{1,0:T(8,128)S(1)}, f32[768,128]{1,0:T(8,128)S(1)}, u32[]{:S(2)}, u32[]{:S(2)}) collective-permute-start(f32[768,128]{1,0:T(8,128)S(1)} %bitcast.7), channel_id=1, source_target_pairs={{0,1},{1,0},{2,3},{3,2},{4,5},{5,4},{6,7},{7,6},{8,9},{9,8},{10,11... | collective-permute-start | bytes 1179656 | tf_op jit(solution)/shard_map/ppermute | solution.py:650
  99.9 0.8 shard_map.115
  100.7 0.5 collective-permute-done.5.other_ref
  101.2 1.1 %shard_map.116 = f32[4,192,192]{2,1,0:T(8,128)} custom-call(s32[1]{0:T(128)} %bitcast.tile_ref, f32[2,192,192]{2,1,0:T(8,128)S(1)} %get-tuple-element.33.half_ref, f32[768,128]{1,0:T(8,128)S(1)} %collective-permute-done.5.other_ref), custom_call_target="tpu_custom_call" | custom-call | flops 1000000000 | bytes 3000000 | tf_op jit(solution)/shard_map/pallas_call | solution.py:506
  (2 shorter events, 0.1 us)
Async XLA Ops:
  0.6 0.9 copy-start.4
  0.7 0.9 copy-start.5
  0.7 0.9 copy-start.7
  0.7 0.9 copy-start.8
  1.6 5.0 %copy-start = (f32[10,96,96]{2,1,0:T(8,128)S(1)}, f32[10,96,96]{2,1,0:T(8,128)}, u32[]{:S(2)}) copy-start(f32[10,96,96]{2,1,0:T(8,128)} %lr_ref.1) | copy-start | bytes 1105924
  1.6 5.0 %copy-start.1 = (f32[10,96,96]{2,1,0:T(8,128)S(1)}, f32[10,96,96]{2,1,0:T(8,128)}, u32[]{:S(2)}) copy-start(f32[10,96,96]{2,1,0:T(8,128)} %li_ref.1) | copy-start | bytes 1105924
  1.6 5.0 %copy-start.2 = (f32[4,96,96]{2,1,0:T(8,128)S(1)}, f32[4,96,96]{2,1,0:T(8,128)}, u32[]{:S(2)}) copy-start(f32[4,96,96]{2,1,0:T(8,128)} %tr_ref.1) | copy-start | bytes 442372
  1.6 5.0 %copy-start.3 = (f32[4,96,96]{2,1,0:T(8,128)S(1)}, f32[4,96,96]{2,1,0:T(8,128)}, u32[]{:S(2)}) copy-start(f32[4,96,96]{2,1,0:T(8,128)} %ti_ref.1) | copy-start | bytes 442372
  1.7 6.8 %collective-permute-start = (f32[304,128]{1,0:T(8,128)S(1)}, f32[304,128]{1,0:T(8,128)S(1)}, u32[]{:S(2)}, u32[]{:S(2)}) collective-permute-start(f32[304,128]{1,0:T(8,128)S(1)} %get-tuple-element.18), channel_id=1, source_target_pairs={{0,8},{8,0},{16,24},{24,16},{32,40},{40,32},{48,56},{56,48},{64,72... | collective-permute-start | bytes 466952 | tf_op jit(solution)/shard_map/ppermute | solution.py:527
  5.9 2.6 %collective-permute-start.1 = (f32[304,128]{1,0:T(8,128)S(1)}, f32[304,128]{1,0:T(8,128)S(1)}, u32[]{:S(2)}, u32[]{:S(2)}) collective-permute-start(f32[304,128]{1,0:T(8,128)S(1)} %get-tuple-element.19), channel_id=1, source_target_pairs={{8,16},{16,8},{24,32},{32,24},{40,48},{48,40},{56,64},{64,56},{72,... | collective-permute-start | bytes 466952 | tf_op jit(solution)/shard_map/ppermute | solution.py:527
  8.8 14.1 %collective-permute-start.2 = (f32[208,128]{1,0:T(8,128)S(1)}, f32[208,128]{1,0:T(8,128)S(1)}, u32[]{:S(2)}, u32[]{:S(2)}) collective-permute-start(f32[208,128]{1,0:T(8,128)S(1)} %get-tuple-element.20), channel_id=1, source_target_pairs={{0,1},{1,0},{2,3},{3,2},{4,5},{5,4},{6,7},{7,6},{8,9},{9,8},{10,11... | collective-permute-start | bytes 319496 | tf_op jit(solution)/shard_map/ppermute | solution.py:527
  18.1 6.0 %collective-permute-start.3 = (f32[208,128]{1,0:T(8,128)S(1)}, f32[208,128]{1,0:T(8,128)S(1)}, u32[]{:S(2)}, u32[]{:S(2)}) collective-permute-start(f32[208,128]{1,0:T(8,128)S(1)} %get-tuple-element.21), channel_id=1, source_target_pairs={{1,2},{2,1},{3,4},{4,3},{5,6},{6,5},{9,10},{10,9},{11,12},{12,11},... | collective-permute-start | bytes 319496 | tf_op jit(solution)/shard_map/ppermute | solution.py:527
  20.0 4.1 %copy-start.6 = (f32[192,128]{1,0:T(8,128)S(1)}, f32[192,128]{1,0:T(8,128)}, u32[]{:S(2)}) copy-start(f32[192,128]{1,0:T(8,128)} %inc_ref.1) | copy-start | bytes 294916
  27.8 3.5 %collective-permute-start.4 = (f32[584,128]{1,0:T(8,128)S(1)}, f32[584,128]{1,0:T(8,128)S(1)}, u32[]{:S(2)}, u32[]{:S(2)}) collective-permute-start(f32[584,128]{1,0:T(8,128)S(1)} %shard_map.110.own_ref.vec_ref), channel_id=1, source_target_pairs={{0,1},{1,0},{2,3},{3,2},{4,5},{5,4},{6,7},{7,6},{8,9},{9,8},{10,11... | collective-permute-start | bytes 897032 | tf_op jit(solution)/shard_map/ppermute | solution.py:640
  93.2 8.0 %collective-permute-start.5 = (f32[768,128]{1,0:T(8,128)S(1)}, f32[768,128]{1,0:T(8,128)S(1)}, u32[]{:S(2)}, u32[]{:S(2)}) collective-permute-start(f32[768,128]{1,0:T(8,128)S(1)} %bitcast.7), channel_id=1, source_target_pairs={{0,1},{1,0},{2,3},{3,2},{4,5},{5,4},{6,7},{7,6},{8,9},{9,8},{10,11... | collective-permute-start | bytes 1179656 | tf_op jit(solution)/shard_map/ppermute | solution.py:650

commit v14 on v13

--- a/solution.py
+++ b/solution.py
@@ -641,11 +641,11 @@
     (chunks,) = call(outer_kernel, [(32 * CHUNK, PT)], tile, vectors, partner, smem=1)
     got = lax.all_to_all(chunks.reshape(4, 8 * CHUNK, PT), "x", 0, 0)
     (part,) = call(sum_kernel, [(8 * CHUNK, PT)], got)
-    got = lax.all_to_all(part.reshape(8, CHUNK, PT), "y", 0, 0)
+    got = lax.all_to_all(part.reshape(8, CHUNK, PT), "z", 0, 0)
     (pieces,) = call(spread_kernel, [(8, CHUNK, PT)], got)
-    got = lax.all_to_all(pieces, "z", 0, 0)
+    got = lax.all_to_all(pieces, "y", 0, 0)
     mixed, coefs = call(combine_kernel, [(32 * BACK, PT), (8, PT)], got)
-    got = lax.all_to_all(mixed.reshape(32, BACK, PT), ("y", "x"), 0, 0)
+    got = lax.all_to_all(mixed.reshape(32, BACK, PT), ("z", "x"), 0, 0)
     half = got.reshape(32 * BACK, PT)
     other = lax.ppermute(half, "c", pair)
     own_half, adjoint = call(own_types_kernel, [(2, W, W), (W, PT)], half, vectors, coefs)

time: 103 us -> 103 us (level)
  no operation moved by 1% of the time
where the time goes in v14:
time: 103 us; the launch traced here: 102 us
  blocking collectives  61.1 us (59%)
  starting transfers between devices  24.6 us (24%)
  Pallas kernels  11.4 us (11%)
  waiting for transfers between devices  3.46 us (3%)
    all_to_all x1, blocking collectives, body(): got = lax.all_to_all(part.reshape(8, CHUNK, PT), 'z', 0, 0)  21.3 us
    ppermute x4, starting transfers between devices, swapped(): return (lax.ppermute(one, axis, near), lax.ppermute(two, axis, far))  16 us
    all_to_all x1, blocking collectives, body(): got = lax.all_to_all(mixed.reshape(32, BACK, PT), ('z', 'x'), 0, 0)  14.8 us
    all_to_all x1, blocking collectives, body(): got = lax.all_to_all(chunks.reshape(4, 8 * CHUNK, PT), 'x', 0, 0)  13 us
    all_to_all x1, blocking collectives, body(): got = lax.all_to_all(pieces, 'y', 0, 0)  12 us
    pallas_call x13, Pallas kernels, call(): pl.pallas_call(kernel, out_shape=[s if isinstance(s, jax.ShapeDtypeStruct...  11.4 us
    ppermute x1, starting transfers between devices, body(): other = lax.ppermute(half, 'c', pair)  6.69 us
  transfers between devices with their start and end apart: 6, of which 4 were waited for; matrix products, arithmetic and copies ran while one was open for 0% of the time, Pallas kernels for 5%

profile of v14, /device:TPU:1, one launch (start us, length us, event | category | flops | bytes accessed | tf_op | source)
XLA Modules:
  0.0 102.3 jit_solution(16573290806022565808)
XLA Ops:
  0.6 0.0 copy-start.4
  0.7 0.0 copy-start.5
  0.7 0.0 copy-start.7
  0.7 0.0 copy-start.8
  0.7 0.1 shard_map.104._.ids_ref
  0.8 0.7 copy-done.4
  1.5 0.0 copy-done.5
  1.6 0.0 copy-done.7
  1.6 0.0 copy-done.8
  1.6 0.0 copy-start
  1.6 0.0 copy-start.1
  1.6 0.0 copy-start.2
  1.6 0.0 copy-start.3
  1.6 0.1 shard_map.105
  1.7 4.2 %collective-permute-start = (f32[304,128]{1,0:T(8,128)S(1)}, f32[304,128]{1,0:T(8,128)S(1)}, u32[]{:S(2)}, u32[]{:S(2)}) collective-permute-start(f32[304,128]{1,0:T(8,128)S(1)} %get-tuple-element.18), channel_id=1, source_target_pairs={{0,8},{8,0},{16,24},{24,16},{32,40},{40,32},{48,56},{56,48},{64,72... | collective-permute-start | bytes 466952 | tf_op jit(solution)/shard_map/ppermute | solution.py:527
  5.9 0.7 collective-permute-start.1
  6.6 0.0 copy-done
  6.6 0.0 copy-done.1
  6.6 0.0 copy-done.2
  6.6 0.0 copy-done.3
  6.6 0.7 shard_map.107
  7.4 0.9 shard_map.108
  8.3 0.2 collective-permute-done.x1_ref
  8.5 0.0 collective-permute-done.1.x2_ref
  8.5 0.3 shard_map.106
  8.8 9.3 %collective-permute-start.2 = (f32[208,128]{1,0:T(8,128)S(1)}, f32[208,128]{1,0:T(8,128)S(1)}, u32[]{:S(2)}, u32[]{:S(2)}) collective-permute-start(f32[208,128]{1,0:T(8,128)S(1)} %get-tuple-element.20), channel_id=1, source_target_pairs={{0,1},{1,0},{2,3},{3,2},{4,5},{5,4},{6,7},{7,6},{8,9},{9,8},{10,11... | collective-permute-start | bytes 319496 | tf_op jit(solution)/shard_map/ppermute | solution.py:527
  18.1 1.9 %collective-permute-start.3 = (f32[208,128]{1,0:T(8,128)S(1)}, f32[208,128]{1,0:T(8,128)S(1)}, u32[]{:S(2)}, u32[]{:S(2)}) collective-permute-start(f32[208,128]{1,0:T(8,128)S(1)} %get-tuple-element.21), channel_id=1, source_target_pairs={{1,2},{2,1},{3,4},{4,3},{5,6},{6,5},{9,10},{10,9},{11,12},{12,11},... | collective-permute-start | bytes 319496 | tf_op jit(solution)/shard_map/ppermute | solution.py:527
  20.0 0.0 copy-start.6
  20.0 2.9 %shard_map.109 = (f32[192,256]{1,0:T(8,128)S(1)}, f32[960,256]{1,0:T(8,128)S(1)}, bf16[2048,256]{1,0:T(8,128)(2,1)S(1)}) custom-call(s32[1]{0:T(128)} %bitcast.tile_ref, f32[512,128]{1,0:T(8,128)S(1)} %shard_map.104._.ids_ref, bf16[384,128]{1,0:T(8,128)(2,1)S(1)} %get-tuple-element.23.own_ref, f32[1920,256]{1,0:T(8,128)S(1)} %get-tuple-element.24.sum_ref, ...), custom_call_target="tpu_custom_call" | custom-call | flops 4000000000 | bytes 12000000 | tf_op jit(solution)/shard_map/pallas_call | solution.py:506
  22.9 0.0 collective-permute-done.2.y1_ref
  22.9 1.2 %collective-permute-done.3.y2_ref = f32[208,128]{1,0:T(8,128)S(1)} collective-permute-done((f32[208,128]{1,0:T(8,128)S(1)}, f32[208,128]{1,0:T(8,128)S(1)}, u32[]{:S(2)}, u32[]{:S(2)}) %collective-permute-start.3) | collective-permute-done | bytes 106528 | tf_op jit(solution)/shard_map/ppermute | solution.py:527
  24.1 0.0 copy-done.6
  24.1 3.7 %shard_map.110.own_ref.vec_ref = f32[584,128]{1,0:T(8,128)S(1)} custom-call(s32[1]{0:T(128)} %bitcast.tile_ref, f32[512,128]{1,0:T(8,128)S(1)} %shard_map.104._.ids_ref, f32[192,128]{1,0:T(8,128)S(1)} %copy-done.5, s32[10,128]{1,0:T(8,128)S(1)} %copy-done.7, s32[1,128]{1,0:T(1,128)S(1)} %bitcast.15, f32[192,128]{1,0:T(8,128)S(1)} %copy-done.6, ...), custom_call_target="tpu_custom_call" | custom-call | flops 4000000000 | bytes 12000000 | tf_op jit(solution)/shard_map/pallas_call | solution.py:506
  27.8 1.9 %collective-permute-start.4 = (f32[584,128]{1,0:T(8,128)S(1)}, f32[584,128]{1,0:T(8,128)S(1)}, u32[]{:S(2)}, u32[]{:S(2)}) collective-permute-start(f32[584,128]{1,0:T(8,128)S(1)} %shard_map.110.own_ref.vec_ref), channel_id=1, source_target_pairs={{0,1},{1,0},{2,3},{3,2},{4,5},{5,4},{6,7},{7,6},{8,9},{9,8},{10,11... | collective-permute-start | bytes 897032 | tf_op jit(solution)/shard_map/ppermute | solution.py:640
  29.7 1.6 %collective-permute-done.4.other_ref = f32[584,128]{1,0:T(8,128)S(1)} collective-permute-done((f32[584,128]{1,0:T(8,128)S(1)}, f32[584,128]{1,0:T(8,128)S(1)}, u32[]{:S(2)}, u32[]{:S(2)}) %collective-permute-start.4) | collective-permute-done | bytes 299040 | tf_op jit(solution)/shard_map/ppermute | solution.py:640
  31.3 0.6 shard_map.111
  31.9 13.0 %all_to_all.20.in_ref = f32[4,320,128]{2,1,0:T(8,128)S(1)} all-to-all(f32[4,320,128]{2,1,0:T(8,128)S(1)} %bitcast.6), channel_id=1, replica_groups=mesh['z'=8,'y'=8,'x'=4,'c'=2] {'x'}, dimensions={0} | all-to-all | bytes 1310720 | tf_op jit(solution)/shard_map/all_to_all | solution.py:642
  44.9 21.3 %all_to_all.21.in_ref = f32[8,40,128]{2,1,0:T(8,128)S(1)} all-to-all(f32[8,40,128]{2,1,0:T(8,128)S(1)} %bitcast.10), channel_id=1, replica_groups=mesh['z'=8,'y'=8,'x'=4,'c'=2] {'z'}, dimensions={0} | all-to-all | bytes 327680 | tf_op jit(solution)/shard_map/all_to_all | solution.py:644
  66.2 12.0 %all_to_all.22.in_ref = f32[8,40,128]{2,1,0:T(8,128)S(1)} all-to-all(f32[8,40,128]{2,1,0:T(8,128)S(1)} %shard_map.113), channel_id=1, replica_groups=mesh['z'=8,'y'=8,'x'=4,'c'=2] {'y'}, dimensions={0} | all-to-all | bytes 327680 | tf_op jit(solution)/shard_map/all_to_all | solution.py:646
  78.2 0.2 shard_map.114
  78.4 14.8 %all_to_all.23 = f32[32,24,128]{2,1,0:T(8,128)S(1)} all-to-all(f32[32,24,128]{2,1,0:T(8,128)S(1)} %bitcast.9), channel_id=1, replica_groups=mesh['z'=8,'y'=8,'x'=4,'c'=2] {'z','x'}, dimensions={0} | all-to-all | bytes 786432 | tf_op jit(solution)/shard_map/all_to_all | solution.py:648
  93.2 6.7 %collective-permute-start.5 = (f32[768,128]{1,0:T(8,128)S(1)}, f32[768,128]{1,0:T(8,128)S(1)}, u32[]{:S(2)}, u32[]{:S(2)}) collective-permute-start(f32[768,128]{1,0:T(8,128)S(1)} %bitcast.7), channel_id=1, source_target_pairs={{0,1},{1,0},{2,3},{3,2},{4,5},{5,4},{6,7},{7,6},{8,9},{9,8},{10,11... | collective-permute-start | bytes 1179656 | tf_op jit(solution)/shard_map/ppermute | solution.py:650
  99.9 0.8 shard_map.115
  100.7 0.5 collective-permute-done.5.other_ref
  101.2 1.1 %shard_map.116 = f32[4,192,192]{2,1,0:T(8,128)} custom-call(s32[1]{0:T(128)} %bitcast.tile_ref, f32[2,192,192]{2,1,0:T(8,128)S(1)} %get-tuple-element.33.half_ref, f32[768,128]{1,0:T(8,128)S(1)} %collective-permute-done.5.other_ref), custom_call_target="tpu_custom_call" | custom-call | flops 1000000000 | bytes 3000000 | tf_op jit(solution)/shard_map/pallas_call | solution.py:506
  (2 shorter events, 0.1 us)
Async XLA Ops:
  0.6 0.9 copy-start.4
  0.7 0.9 copy-start.5
  0.7 0.9 copy-start.7
  0.7 0.9 copy-start.8
  1.6 5.0 %copy-start = (f32[10,96,96]{2,1,0:T(8,128)S(1)}, f32[10,96,96]{2,1,0:T(8,128)}, u32[]{:S(2)}) copy-start(f32[10,96,96]{2,1,0:T(8,128)} %lr_ref.1) | copy-start | bytes 1105924
  1.6 5.0 %copy-start.1 = (f32[10,96,96]{2,1,0:T(8,128)S(1)}, f32[10,96,96]{2,1,0:T(8,128)}, u32[]{:S(2)}) copy-start(f32[10,96,96]{2,1,0:T(8,128)} %li_ref.1) | copy-start | bytes 1105924
  1.6 5.0 %copy-start.2 = (f32[4,96,96]{2,1,0:T(8,128)S(1)}, f32[4,96,96]{2,1,0:T(8,128)}, u32[]{:S(2)}) copy-start(f32[4,96,96]{2,1,0:T(8,128)} %tr_ref.1) | copy-start | bytes 442372
  1.6 5.0 %copy-start.3 = (f32[4,96,96]{2,1,0:T(8,128)S(1)}, f32[4,96,96]{2,1,0:T(8,128)}, u32[]{:S(2)}) copy-start(f32[4,96,96]{2,1,0:T(8,128)} %ti_ref.1) | copy-start | bytes 442372
  1.7 6.8 %collective-permute-start = (f32[304,128]{1,0:T(8,128)S(1)}, f32[304,128]{1,0:T(8,128)S(1)}, u32[]{:S(2)}, u32[]{:S(2)}) collective-permute-start(f32[304,128]{1,0:T(8,128)S(1)} %get-tuple-element.18), channel_id=1, source_target_pairs={{0,8},{8,0},{16,24},{24,16},{32,40},{40,32},{48,56},{56,48},{64,72... | collective-permute-start | bytes 466952 | tf_op jit(solution)/shard_map/ppermute | solution.py:527
  5.9 2.6 %collective-permute-start.1 = (f32[304,128]{1,0:T(8,128)S(1)}, f32[304,128]{1,0:T(8,128)S(1)}, u32[]{:S(2)}, u32[]{:S(2)}) collective-permute-start(f32[304,128]{1,0:T(8,128)S(1)} %get-tuple-element.19), channel_id=1, source_target_pairs={{8,16},{16,8},{24,32},{32,24},{40,48},{48,40},{56,64},{64,56},{72,... | collective-permute-start | bytes 466952 | tf_op jit(solution)/shard_map/ppermute | solution.py:527
  8.8 14.1 %collective-permute-start.2 = (f32[208,128]{1,0:T(8,128)S(1)}, f32[208,128]{1,0:T(8,128)S(1)}, u32[]{:S(2)}, u32[]{:S(2)}) collective-permute-start(f32[208,128]{1,0:T(8,128)S(1)} %get-tuple-element.20), channel_id=1, source_target_pairs={{0,1},{1,0},{2,3},{3,2},{4,5},{5,4},{6,7},{7,6},{8,9},{9,8},{10,11... | collective-permute-start | bytes 319496 | tf_op jit(solution)/shard_map/ppermute | solution.py:527
  18.1 6.0 %collective-permute-start.3 = (f32[208,128]{1,0:T(8,128)S(1)}, f32[208,128]{1,0:T(8,128)S(1)}, u32[]{:S(2)}, u32[]{:S(2)}) collective-permute-start(f32[208,128]{1,0:T(8,128)S(1)} %get-tuple-element.21), channel_id=1, source_target_pairs={{1,2},{2,1},{3,4},{4,3},{5,6},{6,5},{9,10},{10,9},{11,12},{12,11},... | collective-permute-start | bytes 319496 | tf_op jit(solution)/shard_map/ppermute | solution.py:527
  20.0 4.1 %copy-start.6 = (f32[192,128]{1,0:T(8,128)S(1)}, f32[192,128]{1,0:T(8,128)}, u32[]{:S(2)}) copy-start(f32[192,128]{1,0:T(8,128)} %inc_ref.1) | copy-start | bytes 294916
  27.8 3.5 %collective-permute-start.4 = (f32[584,128]{1,0:T(8,128)S(1)}, f32[584,128]{1,0:T(8,128)S(1)}, u32[]{:S(2)}, u32[]{:S(2)}) collective-permute-start(f32[584,128]{1,0:T(8,128)S(1)} %shard_map.110.own_ref.vec_ref), channel_id=1, source_target_pairs={{0,1},{1,0},{2,3},{3,2},{4,5},{5,4},{6,7},{7,6},{8,9},{9,8},{10,11... | collective-permute-start | bytes 897032 | tf_op jit(solution)/shard_map/ppermute | solution.py:640
  93.2 8.0 %collective-permute-start.5 = (f32[768,128]{1,0:T(8,128)S(1)}, f32[768,128]{1,0:T(8,128)S(1)}, u32[]{:S(2)}, u32[]{:S(2)}) collective-permute-start(f32[768,128]{1,0:T(8,128)S(1)} %bitcast.7), channel_id=1, source_target_pairs={{0,1},{1,0},{2,3},{3,2},{4,5},{5,4},{6,7},{7,6},{8,9},{9,8},{10,11... | collective-permute-start | bytes 1179656 | tf_op jit(solution)/shard_map/ppermute | solution.py:650
